TPU v7x, 32 devices: a whole 2x2x4 slice. The times are simulated.
32 devices in a mesh: gx: 4 (over y, x), gy: 4 (over z), gz: 2 (over core).
Axes of the slice: x: 2, y: 2, z: 4, core: 2. Of those that a mesh axis runs over, the one named last changes fastest.
Arguments:
- positions: float32 [8, 8, 2, 192], P('gx', 'gy', 'gz'), may hold values from 0 to 1
- species: int32 [8, 8, 2, 64], P('gx', 'gy', 'gz'), may hold values from 0 to 88
- counts: int32 [8, 8, 2], P('gx', 'gy', 'gz'), may hold values from 1 to 64, as said below
- embed: bfloat16 [89, 128], replicated, may hold values from -6 to 6
- filters: bfloat16 [128, 512], replicated, may hold values from -0.5 to 0.5
- w_up: bfloat16 [128, 128], replicated, may hold values from -0.5 to 0.5
- w_energy: float32 [128], replicated, may hold values from -0.5 to 0.5
Outputs:
- energies: float32 [8, 8, 2, 64], P('gx', 'gy', 'gz')
- forces: float32 [8, 8, 2, 192], P('gx', 'gy', 'gz')
Inputs may be any that keep to these rules, and one draw needn't show every extreme that they name: `counts`: at most 64 atoms a cell; some cell holds exactly 64 and some exactly 1.
All inputs are finite; a program needn't handle non-finite values.
Results may differ from a plain program's by a relative error of at most 0.0038.
Values may be sent and summed in bfloat16 or wider, within the bound.
No kernel may reach another device: no remote copies, remote signals or barrier semaphores. Data moves between devices by JAX's collectives and lax.ppermute only.
A program may use at most 64 MiB of HBM per device.

v0:
```python
import jax
import jax.numpy as jnp
from jax import lax
from jax.sharding import PartitionSpec as P

MSG_SCALE = 0.1


def with_halo(block, sides, width):
    for axis, dim in sides:
        count = lax.axis_size(axis)
        forward = [(i, i + 1) for i in range(count - 1)]
        forward.append((count - 1, 0))
        backward = [(target, source) for source, target in forward]
        low = lax.ppermute(
            lax.slice_in_dim(block, block.shape[dim] - width, None, axis=dim), axis, forward
        )
        high = lax.ppermute(lax.slice_in_dim(block, 0, width, axis=dim), axis, backward)
        block = jnp.concatenate([low, block, high], axis=dim)
    return block


def radial(dist_sq, radial_count):
    decay_rates = 0.5 * 3.0 ** jnp.arange(radial_count).astype(jnp.float32)
    falloff = jnp.maximum(1.0 - dist_sq, 0.0)[..., None]
    decaying = jnp.exp(-decay_rates * dist_sq[..., None])
    return (
        decaying * falloff * falloff,
        -decaying * (decay_rates * falloff * falloff + 2.0 * falloff),
    )


def offset_of(index):
    first = index // 9 - 1
    second = index // 3 % 3 - 1
    third = index % 3 - 1
    return (first.astype(jnp.int32), second.astype(jnp.int32), third.astype(jnp.int32))


def geometry(anchor_pos, target_pos, offset):
    slot_count = anchor_pos.shape[-1] // 3
    leading = anchor_pos.shape[:-1]
    anchor = anchor_pos.reshape(leading + (3, slot_count))
    target = target_pos.reshape(leading + (3, slot_count))
    shift_vec = jnp.stack(offset).astype(jnp.float32).reshape((3, 1, 1))
    displace = target[..., :, None, :] - anchor[..., :, :, None] + shift_vec
    return (displace, jnp.sum(displace * displace, axis=-3))


def window(padded, offset, cell_shape):
    zero = jnp.zeros((), jnp.int32)
    starts = (offset[0] + 1, offset[1] + 1, offset[2] + 1) + (zero,) * (padded.ndim - 3)
    return lax.dynamic_slice(padded, starts, tuple(cell_shape) + padded.shape[3:])


def project(embedded, filters):
    return jnp.einsum(
        "abcsd,de->abcse", embedded, filters, preferred_element_type=jnp.float32
    ).astype(jnp.bfloat16)


def lookup(marked, embed):
    onehot = (marked[..., None] == jnp.arange(embed.shape[0], dtype=jnp.int32)).astype(jnp.bfloat16)
    return jnp.einsum("abcsk,kd->abcsd", onehot, embed, preferred_element_type=jnp.float32).astype(
        jnp.bfloat16
    )


def on_device(positions, species, counts, embed, filters, w_up, w_energy):
    cell_shape = positions.shape[:3]
    slot_count = species.shape[-1]
    feature_width = embed.shape[1]
    radial_count = filters.shape[1] // feature_width
    grouped_shape = cell_shape + (slot_count * radial_count, feature_width)
    centre = (jnp.zeros((), jnp.int32),) * 3
    occupied = (jnp.arange(slot_count, dtype=jnp.int32) < counts[..., None]).astype(jnp.float32)
    marked = jnp.where(occupied > 0.0, species, -1)
    pos_pad = with_halo(positions, (("gx", 0), ("gy", 1), ("gz", 2)), 1)
    marked_pad = with_halo(marked, (("gx", 0), ("gy", 1), ("gz", 2)), 1)
    emb_pad = lookup(marked_pad, embed)
    embedded = window(emb_pad, centre, cell_shape)
    feat_pad = project(emb_pad, filters)
    anchor_feat = window(feat_pad, centre, cell_shape).reshape(grouped_shape)
    diagonal = jnp.eye(slot_count, dtype=jnp.float32)[..., None]

    def message_step(index, message):
        offset = offset_of(index)
        target_pos = window(pos_pad, offset, cell_shape)
        target_feat = window(feat_pad, offset, cell_shape).reshape(grouped_shape)
        displace, dist_sq = geometry(positions, target_pos, offset)
        radial_vals = radial(dist_sq, radial_count)[0]
        centred = (index == 13).astype(jnp.float32)
        radial_vals = radial_vals * (1.0 - centred * diagonal)
        weights = radial_vals.reshape(cell_shape + (slot_count, slot_count * radial_count)).astype(
            jnp.bfloat16
        )
        return message + jnp.einsum(
            "abcip,abcpd->abcid", weights, target_feat, preferred_element_type=jnp.float32
        )

    message = lax.fori_loop(
        0, 27, message_step, jnp.zeros(cell_shape + (slot_count, feature_width), jnp.float32)
    )
    message = MSG_SCALE * message
    sigmoid_msg = jax.nn.sigmoid(message)
    activated = (message * sigmoid_msg).astype(jnp.bfloat16)
    hidden = embedded.astype(jnp.float32) + jnp.einsum(
        "abcsd,de->abcse", activated, w_up, preferred_element_type=jnp.float32
    )
    energies = occupied * jnp.sum(hidden * w_energy, axis=-1)
    readout = jnp.sum(w_up.astype(jnp.float32) * w_energy[None, :], axis=1)
    adjoint = (
        occupied[..., None] * sigmoid_msg * (1.0 + message * (1.0 - sigmoid_msg)) * readout
    ).astype(jnp.bfloat16)
    adj_pad = with_halo(adjoint, (("gx", 0), ("gy", 1), ("gz", 2)), 1)

    def force_step(index, forces):
        offset = offset_of(index)
        target_pos = window(pos_pad, offset, cell_shape)
        target_feat = window(feat_pad, offset, cell_shape).reshape(grouped_shape)
        target_adj = window(adj_pad, offset, cell_shape)
        displace, dist_sq = geometry(positions, target_pos, offset)
        radial_slope = radial(dist_sq, radial_count)[1]
        outward = jnp.einsum(
            "abcid,abcpd->abcip", adjoint, target_feat, preferred_element_type=jnp.float32
        ).reshape(cell_shape + (slot_count, slot_count, radial_count))
        inward = jnp.einsum(
            "abcjd,abcpd->abcjp", target_adj, anchor_feat, preferred_element_type=jnp.float32
        ).reshape(cell_shape + (slot_count, slot_count, radial_count))
        inward = jnp.swapaxes(inward, -3, -2)
        pair_weight = MSG_SCALE * jnp.sum(radial_slope * (outward + inward), axis=-1)
        return forces + 2.0 * jnp.sum(displace * pair_weight[..., None, :, :], axis=-1)

    forces = lax.fori_loop(0, 27, force_step, jnp.zeros(cell_shape + (3, slot_count), jnp.float32))
    forces = (forces * occupied[..., None, :]).reshape(positions.shape)
    return (energies, forces)


def solution(mesh):
    in_specs = (
        P("gx", "gy", "gz", None),
        P("gx", "gy", "gz", None),
        P("gx", "gy", "gz"),
        P(),
        P(),
        P(),
        P(),
    )
    out_specs = (P("gx", "gy", "gz", None), P("gx", "gy", "gz", None))
    return jax.shard_map(
        on_device, mesh=mesh, in_specs=in_specs, out_specs=out_specs, check_vma=False
    )
```

profile of v0, /device:TPU:0, one launch (start us, length us, event | category | flops | bytes accessed | tf_op | source)
XLA Modules:
  0.0 225.0 jit_solution(8410672240345877217)
XLA Ops:
  1.5 3.0 %collective-permute-start = (s32[1,2,1,64]{3,2,1,0:T(1,128)S(1)}, s32[1,2,1,64]{3,2,1,0:T(1,128)S(1)}, u32[]{:S(2)}, u32[]{:S(2)}) collective-permute-start(s32[1,2,1,64]{3,2,1,0:T(1,128)S(1)} %get-tuple-element.717), channel_id=1, source_target_pairs={{0,8},{8,16},{16,24},{24,0},{1,9},{9,17},{17,25},{25,1},{2,10},{10... | collective-permute-start | bytes 1544 | tf_op jit(solution)/shard_map/ppermute | solution.py:15
  4.4 1.0 collective-permute-start.1
  6.1 2.0 collective-permute-start.7
  9.8 2.0 collective-permute-start.2
  11.9 2.1 collective-permute-start.3
  14.9 3.6 %collective-permute-start.9 = (f32[4,1,1,192]{3,1,0,2:T(1,128)S(1)}, f32[4,1,1,192]{3,1,0,2:T(1,128)S(1)}, u32[]{:S(2)}, u32[]{:S(2)}) collective-permute-start(f32[4,1,1,192]{3,1,0,2:T(1,128)S(1)} %get-tuple-element.712), channel_id=1, source_target_pairs={{2,0},{4,2},{6,4},{0,6},{3,1},{5,3},{7,5},{1,7},{10,8},{12,10},{14... | collective-permute-start | bytes 9224 | tf_op jit(solution)/shard_map/ppermute | solution.py:18
  19.2 1.0 collective-permute-done.8
  20.8 1.6 fusion.19
  23.3 2.2 copy.51
  26.0 72.1 %while.38 = (s32[]{:T(128)}, f32[2,2,1,64,128]{4,3,1,0,2:T(8,128)S(1)}, f32[4,4,3,192]{3,1,0,2:T(4,128)S(1)}, f32[2,2,1,192]{3,1,0,2:T(2,128)S(1)}, bf16[4,4,3,6...) while((s32[]{:T(128)}, ...), condition=%wide.region_2.3_spmd.clone, body=%wide.region_0.2_spmd.clone.sunk | while | flops 17395772 | bytes 3404393 | solution.py:101
  27.0 1.0 constant_dynamic-slice_fusion.8
  29.6 1.0 constant_dynamic-slice_fusion.8
  35.0 1.0 constant_dynamic-slice_fusion.8
  40.3 1.0 constant_dynamic-slice_fusion.8
  43.0 1.0 constant_dynamic-slice_fusion.8
  45.7 1.0 constant_dynamic-slice_fusion.8
  48.3 1.0 constant_dynamic-slice_fusion.8
  51.0 1.0 constant_dynamic-slice_fusion.8
  56.3 1.0 constant_dynamic-slice_fusion.8
  59.0 1.0 constant_dynamic-slice_fusion.8
  64.3 1.0 constant_dynamic-slice_fusion.8
  67.0 1.0 constant_dynamic-slice_fusion.8
  72.3 1.0 constant_dynamic-slice_fusion.8
  75.0 1.0 constant_dynamic-slice_fusion.8
  88.3 1.0 constant_dynamic-slice_fusion.8
  91.0 1.0 constant_dynamic-slice_fusion.8
  98.2 1.7 collective-permute-start.12
  99.9 1.3 collective-permute-start.13
  101.2 1.9 collective-permute-done.12
  104.0 3.9 %collective-permute-start.15 = (bf16[4,1,1,64,128]{4,3,1,0,2:T(8,128)(2,1)S(1)}, bf16[4,1,1,64,128]{4,3,1,0,2:T(8,128)(2,1)S(1)}, u32[]{:S(2)}, u32[]{:S(2)}) collective-permute-start(bf16[4,1,1,64,128]{4,3,1,0,2:T(8,128)(2,1)S(1)} %get-tuple-element.708), channel_id=1, source_target_pairs={{2,0},{4,2},{6,4},{0,6},{3,1},{5,3},{7,5},{1,7},{10,8},{12,10},{14... | collective-permute-start | bytes 196616 | tf_op jit(solution)/shard_map/ppermute | solution.py:18
  109.0 1.7 collective-permute-done.14
  112.8 111.6 %while.39 = (s32[]{:T(128)}, f32[2,2,1,3,64]{4,3,1,0,2:T(4,128)S(1)}, f32[4,4,3,192]{3,1,0,2:T(4,128)S(1)}, f32[2,2,1,192]{3,1,0,2:T(2,128)S(1)}, bf16[4,4,3,64,...) while((s32[]{:T(128)}, ...), condition=%wide.region_9.10_spmd.clone, body=%wide.region_5.9_spmd.clone.sunk | while | flops 34571828 | bytes 5089951 | solution.py:134
  (1102 shorter events, 168.9 us)
Async XLA Ops:
  0.6 21.7 %copy-start = (bf16[128,512]{1,0:T(8,128)(2,1)S(1)}, bf16[128,512]{1,0:T(8,128)(2,1)}, u32[]{:S(2)}) copy-start(bf16[128,512]{1,0:T(8,128)(2,1)} %param.15) | copy-start | bytes 393220
  1.5 8.3 %collective-permute-start = (s32[1,2,1,64]{3,2,1,0:T(1,128)S(1)}, s32[1,2,1,64]{3,2,1,0:T(1,128)S(1)}, u32[]{:S(2)}, u32[]{:S(2)}) collective-permute-start(s32[1,2,1,64]{3,2,1,0:T(1,128)S(1)} %get-tuple-element.717), channel_id=1, source_target_pairs={{0,8},{8,16},{16,24},{24,0},{1,9},{9,17},{17,25},{25,1},{2,10},{10... | collective-permute-start | bytes 1544 | tf_op jit(solution)/shard_map/ppermute | solution.py:15
  4.4 5.4 %collective-permute-start.1 = (s32[1,2,1,64]{3,2,1,0:T(1,128)S(1)}, s32[1,2,1,64]{3,2,1,0:T(1,128)S(1)}, u32[]{:S(2)}, u32[]{:S(2)}) collective-permute-start(s32[1,2,1,64]{3,2,1,0:T(1,128)S(1)} %get-tuple-element.718), channel_id=1, source_target_pairs={{8,0},{16,8},{24,16},{0,24},{9,1},{17,9},{25,17},{1,25},{10,2},{18... | collective-permute-start | bytes 1544 | tf_op jit(solution)/shard_map/ppermute | solution.py:18
  6.1 8.5 %collective-permute-start.7 = (f32[1,2,1,192]{3,1,0,2:T(2,128)S(1)}, f32[1,2,1,192]{3,1,0,2:T(2,128)S(1)}, u32[]{:S(2)}, u32[]{:S(2)}) collective-permute-start(f32[1,2,1,192]{3,1,0,2:T(2,128)S(1)} %get-tuple-element.713), channel_id=1, source_target_pairs={{8,0},{16,8},{24,16},{0,24},{9,1},{17,9},{25,17},{1,25},{10,2},{18... | collective-permute-start | bytes 4616 | tf_op jit(solution)/shard_map/ppermute | solution.py:18
  8.1 5.9 %collective-permute-start.6 = (f32[1,2,1,192]{3,1,0,2:T(2,128)S(1)}, f32[1,2,1,192]{3,1,0,2:T(2,128)S(1)}, u32[]{:S(2)}, u32[]{:S(2)}) collective-permute-start(f32[1,2,1,192]{3,1,0,2:T(2,128)S(1)} %get-tuple-element.714), channel_id=1, source_target_pairs={{0,8},{8,16},{16,24},{24,0},{1,9},{9,17},{17,25},{25,1},{2,10},{10... | collective-permute-start | bytes 4616 | tf_op jit(solution)/shard_map/ppermute | solution.py:15
  9.8 8.7 %collective-permute-start.2 = (s32[4,1,1,64]{3,2,1,0:T(1,128)S(1)}, s32[4,1,1,64]{3,2,1,0:T(1,128)S(1)}, u32[]{:S(2)}, u32[]{:S(2)}) collective-permute-start(s32[4,1,1,64]{3,2,1,0:T(1,128)S(1)} %get-tuple-element.715), channel_id=1, source_target_pairs={{0,2},{2,4},{4,6},{6,0},{1,3},{3,5},{5,7},{7,1},{8,10},{10,12},{12... | collective-permute-start | bytes 3080 | tf_op jit(solution)/shard_map/ppermute | solution.py:15
  11.9 6.7 %collective-permute-start.3 = (s32[4,1,1,64]{3,2,1,0:T(1,128)S(1)}, s32[4,1,1,64]{3,2,1,0:T(1,128)S(1)}, u32[]{:S(2)}, u32[]{:S(2)}) collective-permute-start(s32[4,1,1,64]{3,2,1,0:T(1,128)S(1)} %get-tuple-element.716), channel_id=1, source_target_pairs={{2,0},{4,2},{6,4},{0,6},{3,1},{5,3},{7,5},{1,7},{10,8},{12,10},{14... | collective-permute-start | bytes 3080 | tf_op jit(solution)/shard_map/ppermute | solution.py:18
  14.7 5.5 %collective-permute-start.8 = (f32[4,1,1,192]{3,1,0,2:T(1,128)S(1)}, f32[4,1,1,192]{3,1,0,2:T(1,128)S(1)}, u32[]{:S(2)}, u32[]{:S(2)}) collective-permute-start(f32[4,1,1,192]{3,1,0,2:T(1,128)S(1)} %get-tuple-element.711), channel_id=1, source_target_pairs={{0,2},{2,4},{4,6},{6,0},{1,3},{3,5},{5,7},{7,1},{8,10},{10,12},{12... | collective-permute-start | bytes 9224 | tf_op jit(solution)/shard_map/ppermute | solution.py:15
  14.9 5.2 %collective-permute-start.9 = (f32[4,1,1,192]{3,1,0,2:T(1,128)S(1)}, f32[4,1,1,192]{3,1,0,2:T(1,128)S(1)}, u32[]{:S(2)}, u32[]{:S(2)}) collective-permute-start(f32[4,1,1,192]{3,1,0,2:T(1,128)S(1)} %get-tuple-element.712), channel_id=1, source_target_pairs={{2,0},{4,2},{6,4},{0,6},{3,1},{5,3},{7,5},{1,7},{10,8},{12,10},{14... | collective-permute-start | bytes 9224 | tf_op jit(solution)/shard_map/ppermute | solution.py:18
  18.6 2.2 collective-permute-start.5
  18.7 2.1 collective-permute-start.4
  20.2 5.8 %collective-permute-start.11 = (f32[4,4,1,192]{3,1,0,2:T(4,128)S(1)}, f32[4,4,1,192]{3,1,0,2:T(4,128)S(1)}, u32[]{:S(2)}, u32[]{:S(2)}) collective-permute-start(f32[4,4,1,192]{3,1,0,2:T(4,128)S(1)} %pad_maximum_fusion.4), channel_id=1, source_target_pairs={{1,0},{0,1},{3,2},{2,3},{5,4},{4,5},{7,6},{6,7},{9,8},{8,9},{11,10... | collective-permute-start | bytes 36872 | tf_op jit(solution)/shard_map/ppermute | solution.py:18
  20.2 5.7 %collective-permute-start.10 = (f32[4,4,1,192]{3,1,0,2:T(4,128)S(1)}, f32[4,4,1,192]{3,1,0,2:T(4,128)S(1)}, u32[]{:S(2)}, u32[]{:S(2)}) collective-permute-start(f32[4,4,1,192]{3,1,0,2:T(4,128)S(1)} %pad_maximum_fusion.4), channel_id=1, source_target_pairs={{0,1},{1,0},{2,3},{3,2},{4,5},{5,4},{6,7},{7,6},{8,9},{9,8},{10,11... | collective-permute-start | bytes 36872 | tf_op jit(solution)/shard_map/ppermute | solution.py:15
  23.3 2.6 %copy-start.1 = (bf16[4,4,3,64,512]{4,3,2,1,0:T(8,128)(2,1)}, bf16[4,4,3,64,512]{4,3,2,1,0:T(8,128)(2,1)S(1)}, u32[]{:S(2)}) copy-start(bf16[4,4,3,64,512]{4,3,2,1,0:T(8,128)(2,1)S(1)} %convolution_convert_fusion) | copy-start | bytes 9437188
  26.0 85.2 %copy-start.2 = (bf16[128,128]{1,0:T(8,128)(2,1)S(1)}, bf16[128,128]{1,0:T(8,128)(2,1)}, u32[]{:S(2)}) copy-start(bf16[128,128]{1,0:T(8,128)(2,1)} %param.16) | copy-start | bytes 98308
  26.0 85.2 %copy-start.4 = (f32[128]{0:T(128)S(1)}, f32[128]{0:T(128)}, u32[]{:S(2)}) copy-start(f32[128]{0:T(128)} %param.17) | copy-start | bytes 1540
  98.1 13.4 %copy-start.3 = (s32[2,2,1]{1,2,0:T(1,128)S(1)}, s32[2,2,1]{1,2,0:T(1,128)}, u32[]{:S(2)}) copy-start(s32[2,2,1]{1,2,0:T(1,128)} %param.13) | copy-start | bytes 52
  98.2 4.9 %collective-permute-start.12 = (bf16[1,2,1,64,128]{4,3,1,0,2:T(8,128)(2,1)S(1)}, bf16[1,2,1,64,128]{4,3,1,0,2:T(8,128)(2,1)S(1)}, u32[]{:S(2)}, u32[]{:S(2)}) collective-permute-start(bf16[1,2,1,64,128]{4,3,1,0,2:T(8,128)(2,1)S(1)} %get-tuple-element.709), channel_id=1, source_target_pairs={{0,8},{8,16},{16,24},{24,0},{1,9},{9,17},{17,25},{25,1},{2,10},{10... | collective-permute-start | bytes 98312 | tf_op jit(solution)/shard_map/ppermute | solution.py:15
  99.9 3.9 %collective-permute-start.13 = (bf16[1,2,1,64,128]{4,3,1,0,2:T(8,128)(2,1)S(1)}, bf16[1,2,1,64,128]{4,3,1,0,2:T(8,128)(2,1)S(1)}, u32[]{:S(2)}, u32[]{:S(2)}) collective-permute-start(bf16[1,2,1,64,128]{4,3,1,0,2:T(8,128)(2,1)S(1)} %get-tuple-element.710), channel_id=1, source_target_pairs={{8,0},{16,8},{24,16},{0,24},{9,1},{17,9},{25,17},{1,25},{10,2},{18... | collective-permute-start | bytes 98312 | tf_op jit(solution)/shard_map/ppermute | solution.py:18
  103.9 6.7 %collective-permute-start.14 = (bf16[4,1,1,64,128]{4,3,1,0,2:T(8,128)(2,1)S(1)}, bf16[4,1,1,64,128]{4,3,1,0,2:T(8,128)(2,1)S(1)}, u32[]{:S(2)}, u32[]{:S(2)}) collective-permute-start(bf16[4,1,1,64,128]{4,3,1,0,2:T(8,128)(2,1)S(1)} %get-tuple-element.707), channel_id=1, source_target_pairs={{0,2},{2,4},{4,6},{6,0},{1,3},{3,5},{5,7},{7,1},{8,10},{10,12},{12... | collective-permute-start | bytes 196616 | tf_op jit(solution)/shard_map/ppermute | solution.py:15
  104.0 6.7 %collective-permute-start.15 = (bf16[4,1,1,64,128]{4,3,1,0,2:T(8,128)(2,1)S(1)}, bf16[4,1,1,64,128]{4,3,1,0,2:T(8,128)(2,1)S(1)}, u32[]{:S(2)}, u32[]{:S(2)}) collective-permute-start(bf16[4,1,1,64,128]{4,3,1,0,2:T(8,128)(2,1)S(1)} %get-tuple-element.708), channel_id=1, source_target_pairs={{2,0},{4,2},{6,4},{0,6},{3,1},{5,3},{7,5},{1,7},{10,8},{12,10},{14... | collective-permute-start | bytes 196616 | tf_op jit(solution)/shard_map/ppermute | solution.py:18
  110.7 1.6 collective-permute-start.17
  110.8 1.9 collective-permute-start.16
where the time goes:
time: 227 us; the launch traced here: 225 us
  local copies, waits for them, and re-layouts  113 us (50%)
  other arithmetic  48.3 us (21%)
  matrix products  24.1 us (11%)
  starting transfers between devices  22.6 us (10%)
  loops' own time  10.7 us (5%)
  waiting for transfers between devices  5.78 us (3%)
    dynamic_slice x109, local copies, waits for them, and re-layouts, window(): lax.dynamic_slice(padded, starts, tuple(cell_shape) + padded.shape[3:])  54.3 us
    reduce_sum x27, other arithmetic, force_step(): jnp.sum(radial_slope * (outward + inward), axis=-1)  19.6 us
    ppermute x9, starting transfers between devices, with_halo(): lax.ppermute(lax.slice_in_dim(block, 0, width, axis=dim), axis, backward)  14.1 us
    dot_general x27, matrix products, message_step(): jnp.einsum('abcip,abcpd->abcid', weights, target_feat, preferred_element_...  9.91 us
    reduce_sum x54, other arithmetic, geometry(): return (displace, jnp.sum(displace * displace, axis=-3))  9.58 us
    reduce_sum x27, other arithmetic, force_step(): jnp.sum(displace * pair_weight[..., None, :, :], axis=-1)  9.19 us
    sub x108, local copies, waits for them, and re-layouts, geometry(): displace = target[..., :, None, :] - anchor[..., :, :, None] + shift_vec  8.95 us
    another operation x54, local copies, waits for them, and re-layouts  8.9 us
  transfers between devices with their start and end apart: 18, of which 6 were waited for; matrix products, arithmetic and copies ran while one was open for 4% of the time, Pallas kernels for 0%

commit v1 on v0

v1 whole, which is shorter than its diff:
```python
import functools

import jax
import jax.numpy as jnp
from jax import lax
from jax.experimental import pallas as pl
from jax.experimental.pallas import tpu as pltpu
from jax.sharding import PartitionSpec as P

MSG_SCALE = 0.1
HALO = 2
LANES = 128
NT = (((1,), (1,)), ((), ()))
NN = (((1,), (0,)), ((), ()))


def exchange(block, axis, dim, width):
    count = lax.axis_size(axis)
    first = lax.slice_in_dim(block, 0, width, axis=dim)
    last = lax.slice_in_dim(block, block.shape[dim] - width, None, axis=dim)
    if count % 2 == 0:
        odd = lax.axis_index(axis) % 2 == 1
        whole = block.shape[dim] == width
        up = block if whole else jnp.where(odd, last, first)
        down = block if whole else jnp.where(odd, first, last)
        far = [(i, (i + 1) % count if i % 2 else (i - 1) % count) for i in range(count)]
        near = [(i, i - 1 if i % 2 else i + 1) for i in range(count)]
        from_far = lax.ppermute(up, axis, far)
        from_near = lax.ppermute(down, axis, near)
        low = jnp.where(odd, from_near, from_far)
        high = jnp.where(odd, from_far, from_near)
    else:
        forward = [(i, (i + 1) % count) for i in range(count)]
        low = lax.ppermute(last, axis, forward)
        high = lax.ppermute(first, axis, [(b, a) for a, b in forward])
    return jnp.concatenate([low, block, high], axis=dim)


def dot(a, b, dims, precision=None):
    return lax.dot_general(a, b, dims, precision=precision, preferred_element_type=jnp.float32)


def split(values):
    high = values.astype(jnp.bfloat16)
    return high, (values - high.astype(jnp.float32)).astype(jnp.bfloat16)


def kernel(
    cells, merged, rad,
    region, zrow_ref, embed, filters, w_up, w_energy,
    energies, own, other,
    emb_pad, table, onehot, stage, anchors, adj_table, act,
):
    nax, nay = cells[0] + 2, cells[1] + 2
    groups = region.shape[2] // 4
    slots = energies.shape[-1]
    nspec, width = embed.shape
    spec = emb_pad.shape[0]
    neighbours = [(dx, dy) for dx in (-1, 0, 1) for dy in (-1, 0, 1)]
    bf = jnp.bfloat16

    emb_pad[...] = jnp.zeros_like(emb_pad)
    emb_pad[0:nspec, :] = embed[...].astype(jnp.float32)
    emb = emb_pad[...]
    rows = dot(emb.astype(bf), filters[...], NN).astype(bf)
    for k in range(rad):
        table[k * spec:(k + 1) * spec, :] = rows[:, k * width:(k + 1) * width]
    energy_row = jnp.broadcast_to(w_energy[...], (8, width))
    readout = dot(energy_row, w_up[...].astype(jnp.float32), NT, lax.Precision.HIGHEST)
    emb_energy = dot(energy_row, emb, NT, lax.Precision.HIGHEST)

    ids = lax.broadcasted_iota(jnp.int32, (spec, LANES), 0).astype(jnp.float32)
    for x in range(region.shape[0]):
        for y in range(region.shape[1]):
            for g in range(groups):
                marked = region[x, y, g * 4 + 3:g * 4 + 4, :]
                onehot[(x * region.shape[1] + y) * groups + g] = (marked == ids).astype(bf)

    for q in range(4):
        for x in range(nax):
            stage[q, x * nay:(x + 1) * nay, :] = region[1 + x, 1:1 + nay, q, :]
        columns = stage[q].T
        for a in range(nax * nay):
            anchors[a, q] = jnp.broadcast_to(columns[0:slots, a:a + 1], (slots, LANES))

    def target(x, y, g, shift):
        row = region[x, y, g * 4:g * 4 + 3, :]
        return row[0:1] + shift[0], row[1:2] + shift[1], row[2:3]

    def z_image(dz, g):
        shift = zrow_ref[g:g + 1, :]
        if merged:
            return jnp.where(dz > 0.0, dz - shift, dz + shift)
        return dz + shift

    def onehot_at(x, y, g):
        return onehot[(x * region.shape[1] + y) * groups + g]

    step = 16
    chunks = [slice(r, r + step) for r in range(0, slots, step)]
    diagonal = lax.broadcasted_iota(jnp.int32, (slots, LANES), 0) == lax.broadcasted_iota(
        jnp.int32, (slots, LANES), 1
    )

    def message_at(a, carry):
        ax, ay = a // nay, a % nay
        parts = []
        for dx, dy in neighbours:
            for g in range(groups):
                tx, ty, tz = target(ax + 1 + dx, ay + 1 + dy, g, (dx, dy))
                weights = [[] for _ in range(rad)]
                for c in chunks:
                    ex = tx - anchors[a, 0, c, :]
                    ey = ty - anchors[a, 1, c, :]
                    dz = tz - anchors[a, 2, c, :]
                    if merged:
                        ez = jnp.abs(dz) - zrow_ref[g:g + 1, :]
                    else:
                        ez = dz + zrow_ref[g:g + 1, :]
                    s = ex * ex + ey * ey + ez * ez
                    f = jnp.maximum(1.0 - s, 0.0)
                    e = jnp.exp(-0.5 * s)
                    w = e * (f * f)
                    if dx == 0 and dy == 0 and g == 0:
                        w = jnp.where(diagonal[c], 0.0, w)
                    e = e * e
                    for k in range(rad):
                        if k == 1:
                            w = w * e
                        elif k > 1:
                            e = e * e * e
                            w = w * e
                        weights[k].append(w.astype(bf))
                parts.append(jnp.concatenate([jnp.concatenate(w, axis=0) for w in weights], axis=0))
        hots = [
            onehot_at(ax + 1 + dx, ay + 1 + dy, g) for dx, dy in neighbours for g in range(groups)
        ]
        sums = dot(jnp.concatenate(parts, axis=1), jnp.concatenate(hots, axis=1), NT)
        by_filter = jnp.concatenate([sums[k * slots:(k + 1) * slots] for k in range(rad)], axis=1)
        halves = dot(jnp.concatenate(split(by_filter), axis=0), table[...], NN)
        message = MSG_SCALE * (halves[0:slots] + halves[slots:])
        sigmoid = 1.0 / (1.0 + jnp.exp(-message))
        act[a] = (message * sigmoid).astype(bf)
        slope = sigmoid * (1.0 + message * (1.0 - sigmoid)) * readout[0:1]
        adjoint = jnp.where(anchors[a, 3] >= 0.0, slope, 0.0).astype(bf)
        high, low = split(dot(adjoint, table[...], NT))
        for k in range(rad):
            at = slice(k * slots, (k + 1) * slots)
            adj_table[a, at, 0:spec] = high[:, k * spec:(k + 1) * spec]
            adj_table[a, at, spec:] = low[:, k * spec:(k + 1) * spec]
        return carry

    lax.fori_loop(0, nax * nay, message_at, 0)

    def pairs(a, x, y, g, shift, gains, c):
        tx, ty, tz = target(x, y, g, shift)
        ex = tx - anchors[a, 0, c, :]
        ey = ty - anchors[a, 1, c, :]
        ez = z_image(tz - anchors[a, 2, c, :], g)
        s = ex * ex + ey * ey + ez * ez
        f = jnp.maximum(1.0 - s, 0.0)
        e = jnp.exp(-0.5 * s)
        total = None
        for k in range(rad):
            if k == 1:
                e = e * e * e
            elif k > 1:
                e = e * e * e
            gain = gains[k * slots + c.start:k * slots + c.stop, :]
            term = (e * gain) * (0.5 * 3.0 ** k * f + 2.0)
            total = term if total is None else total + term
        return total * f, (ex, ey, ez)

    scale = -2.0 * MSG_SCALE

    def both(hot):
        return jnp.concatenate([hot, hot], axis=0)

    def forces_at(o, carry):
        ox, oy = o // cells[1], o % cells[1]
        a = (ox + 1) * nay + oy + 1
        sums = [[None] * len(chunks) for _ in range(3)]
        for dx, dy in neighbours:
            for g in range(groups):
                x, y = ox + 2 + dx, oy + 2 + dy
                gains = dot(adj_table[a], both(onehot_at(x, y, g)), NN)
                for n, c in enumerate(chunks):
                    p, displace = pairs(a, x, y, g, (dx, dy), gains, c)
                    for q in range(3):
                        term = p * displace[q]
                        sums[q][n] = term if sums[q][n] is None else sums[q][n] + term
        ones = jnp.ones((8, LANES), jnp.float32)
        mine = [dot(ones, jnp.concatenate(sums[q], axis=0), NT, lax.Precision.HIGHEST)[0:1] for q in range(3)]
        back = []
        for g in range(groups):
            sums = [None] * 3
            for dx, dy in neighbours:
                b = (ox + 1 - dx) * nay + oy + 1 - dy
                gains = dot(adj_table[b], both(onehot_at(ox + 2, oy + 2, g)), NN)
                for c in chunks:
                    p, displace = pairs(b, ox + 2, oy + 2, g, (dx, dy), gains, c)
                    for q in range(3):
                        term = p * displace[q]
                        sums[q] = term if sums[q] is None else sums[q] + term
            back.append([jnp.sum(v, axis=0, keepdims=True) for v in sums])
        row = []
        for q in range(3):
            row.append(scale * (mine[q] - back[0][q][:, 0:slots]))
        own[pl.ds(o, 1), :] = jnp.concatenate(row, axis=1)
        for g in range(groups):
            halves = [(1, slots)] if g == 0 else [(0, 0)]
            for _, start in halves:
                other[g, pl.ds(o, 1), :] = jnp.concatenate(
                    [-scale * back[g][q][:, start:start + slots] for q in range(3)], axis=1
                )
        hot = onehot_at(ox + 2, oy + 2, 0).astype(jnp.float32)
        energy = dot(emb_energy, hot, NN, lax.Precision.HIGHEST)[0:1, 0:slots]
        energy += dot(readout, act[a].astype(jnp.float32), NT, lax.Precision.HIGHEST)[0:1]
        marked = region[ox + 2, oy + 2, 3:4, 0:slots]
        energies[pl.ds(o, 1), :] = jnp.where(marked >= 0.0, energy, 0.0)
        return carry

    lax.fori_loop(0, cells[0] * cells[1], forces_at, 0)


def on_device(positions, species, counts, embed, filters, w_up, w_energy):
    bx, by, bz = positions.shape[:3]
    slots = species.shape[-1]
    width = embed.shape[1]
    rad = filters.shape[1] // width
    spec = -(-embed.shape[0] // LANES) * LANES
    depth = lax.axis_size("gz")
    merged = depth * bz == 2
    occupied = jnp.arange(slots, dtype=jnp.int32) < counts[..., None]
    marked = jnp.where(occupied, species, -1).astype(jnp.float32)
    block = jnp.concatenate(
        [positions.reshape(bx, by, 3, slots), marked.reshape(bx, by, 1, slots)], axis=2
    )
    upward = [(i, (i + 1) % depth) for i in range(depth)]
    downward = [(b, a) for a, b in upward]
    low = lax.ppermute(block, "gz", upward)
    zero = jnp.zeros((slots,), jnp.float32)
    if merged:
        block = jnp.concatenate([block, low], axis=3)
        zrow = jnp.concatenate([zero, zero + 1.0])[None]
    else:
        high = lax.ppermute(block, "gz", downward)
        empty = jnp.full_like(block, -1.0)
        block = jnp.concatenate(
            [jnp.concatenate([block, low], axis=3), jnp.concatenate([high, empty], axis=3)], axis=2
        )
        zrow = jnp.stack([jnp.concatenate([zero, zero - 1.0]), jnp.concatenate([zero + 1.0, zero])])
    groups = block.shape[2] // 4
    block = exchange(block, "gx", 0, HALO)
    region = exchange(block, "gy", 1, HALO)

    anchors = (bx + 2) * (by + 2)
    cells = bx * by
    columns = region.shape[0] * region.shape[1] * groups
    energies, own, other = pl.pallas_call(
        functools.partial(kernel, (bx, by), merged, rad),
        out_shape=(
            jax.ShapeDtypeStruct((cells, slots), jnp.float32),
            jax.ShapeDtypeStruct((cells, 3 * slots), jnp.float32),
            jax.ShapeDtypeStruct((groups, cells, 3 * slots), jnp.float32),
        ),
        in_specs=[pl.BlockSpec(memory_space=pltpu.VMEM)] * 6,
        out_specs=[pl.BlockSpec(memory_space=pltpu.VMEM)] * 3,
        scratch_shapes=[
            pltpu.VMEM((spec, width), jnp.float32),
            pltpu.VMEM((rad * spec, width), jnp.bfloat16),
            pltpu.VMEM((columns, spec, LANES), jnp.bfloat16),
            pltpu.VMEM((4, LANES, LANES), jnp.float32),
            pltpu.VMEM((anchors, 4, slots, LANES), jnp.float32),
            pltpu.VMEM((anchors, rad * slots, 2 * spec), jnp.bfloat16),
            pltpu.VMEM((anchors, slots, width), jnp.bfloat16),
        ],
        compiler_params=pltpu.CompilerParams(vmem_limit_bytes=48 * 1024 * 1024),
    )(region, zrow, embed, filters, w_up, w_energy.reshape(1, width))

    forces = own + lax.ppermute(other[0], "gz", downward)
    if not merged:
        forces = forces + lax.ppermute(other[1], "gz", upward)
    return energies.reshape(species.shape), forces.reshape(positions.shape)


def solution(mesh):
    in_specs = (
        P("gx", "gy", "gz", None),
        P("gx", "gy", "gz", None),
        P("gx", "gy", "gz"),
        P(),
        P(),
        P(),
        P(),
    )
    out_specs = (P("gx", "gy", "gz", None), P("gx", "gy", "gz", None))
    return jax.shard_map(
        on_device, mesh=mesh, in_specs=in_specs, out_specs=out_specs, check_vma=False
    )
```

time: 227 us -> 41.5 us (0.18)
  local copies, waits for them, and re-layouts: 113 us -> 2.18 us
  other arithmetic: 48.3 us -> 1.04 us
  matrix products: 24.1 us -> 0 us
  Pallas kernels: 0 us -> 20 us
  starting transfers between devices: 22.6 us -> 8.46 us
  loops' own time: 10.7 us -> 0 us
  waiting for transfers between devices: 5.78 us -> 8.93 us
    dynamic_slice x109 -> x0, local copies, waits for them, and re-layouts: 54.3 us -> none  [window(): lax.dynamic_slice(padded, starts, tuple(cell_shape) + padded.shape[3:])]
    reduce_sum x109 -> x0, other arithmetic: 39.2 us -> none  [the longest x27 19.6 us: force_step(): jnp.sum(radial_slope * (outward + inward), axis=-1)]
    dot_general x84 -> x0, matrix products: 24.1 us -> none  [the longest x27 9.91 us: message_step(): jnp.einsum('abcip,abcpd->abcid', weights, target_feat, preferred_element_...]
    pallas_call x0 -> x1, Pallas kernels: none -> 20 us  [on_device(): pl.pallas_call(functools.partial(kernel, (bx, by), merged, rad), out_shap...]
    ppermute x18 -> x6, starting transfers between devices: 22.6 us -> 8.46 us  [the longest x2 7.4 us: exchange(): from_far = lax.ppermute(up, axis, far)]
    mul x189 -> x0, local copies, waits for them, and re-layouts: 13.7 us -> none  [the longest x81 5.47 us: radial(): decaying = jnp.exp(-decay_rates * dist_sq[..., None])]
    another operation x2 -> x0, loops' own time: 10.7 us -> none  [the longest x1 5.51 us: on_device(): lax.fori_loop(0, 27, force_step, jnp.zeros(cell_shape + (3, slot_count),...]
    sub x108 -> x0, local copies, waits for them, and re-layouts: 8.95 us -> none  [geometry(): displace = target[..., :, None, :] - anchor[..., :, :, None] + shift_vec]
  transfers between devices with their start and end apart: 18 -> 6, of which waited for: 6 -> 6; matrix products, arithmetic and copies ran while one was open for 4% -> 0% of each run, Pallas kernels for 0% -> 0%
where the time goes in v1:
time: 41.5 us; the launch traced here: 41.3 us
  Pallas kernels  20 us (48%)
  waiting for transfers between devices  8.93 us (22%)
  starting transfers between devices  8.46 us (20%)
  local copies, waits for them, and re-layouts  2.18 us (5%)
  other arithmetic  1.04 us (3%)
  between operations  0.68 us (2%)
    pallas_call x1, Pallas kernels, on_device(): pl.pallas_call(functools.partial(kernel, (bx, by), merged, rad), out_shap...  20 us
    ppermute x2, starting transfers between devices, exchange(): from_far = lax.ppermute(up, axis, far)  7.4 us
    ppermute x2, waiting for transfers between devices, exchange(): from_near = lax.ppermute(down, axis, near)  3.82 us
    ppermute x2, waiting for transfers between devices, exchange(): from_far = lax.ppermute(up, axis, far)  3.11 us
    unnamed x14, local copies, waits for them, and re-layouts  1.49 us
    ppermute x1, waiting for transfers between devices, on_device(): forces = own + lax.ppermute(other[0], 'gz', downward)  1.16 us
  transfers between devices with their start and end apart: 6, of which 6 were waited for; matrix products, arithmetic and copies ran while one was open for 0% of the time, Pallas kernels for 0%

profile of v1, /device:TPU:0, one launch (start us, length us, event | category | flops | bytes accessed | tf_op | source)
XLA Modules:
  0.0 41.3 jit_solution(15000093338411314939)
XLA Ops:
  0.6 0.7 %reduce = f32[2,2,192]{2,1,0:T(2,128)S(1)} reduce(f32[2,2,1,192]{3,2,1,0:T(1,128)} %param.7, f32[]{:T(128)} %constant.34), dimensions={2}, to_apply=%param.7.reduce_sub_computation | reduce | bytes 6148 | tf_op args[0]
  1.3 0.0 copy-start.5
  1.4 0.1 reshape.27
  1.4 0.0 copy-start.6
  1.4 0.6 %copy-done.5 = s32[2,2,1,64]{3,2,1,0:T(1,128)S(1)} copy-done((s32[2,2,1,64]{3,2,1,0:T(1,128)S(1)}, s32[2,2,1,64]{3,2,1,0:T(1,128)}, u32[]{:S(2)}) %copy-start.5) | copy-done | bytes 1048
  2.0 0.1 copy-done.6
  2.1 0.1 fusion
  2.2 0.5 %collective-permute-start = (f32[2,2,4,64]{3,2,1,0:T(4,128)S(1)}, f32[2,2,4,64]{3,2,1,0:T(4,128)S(1)}, u32[]{:S(2)}, u32[]{:S(2)}) collective-permute-start(f32[2,2,4,64]{3,2,1,0:T(4,128)S(1)} %pad_maximum_fusion.2), channel_id=1, source_target_pairs={{0,1},{1,0},{2,3},{3,2},{4,5},{5,4},{6,7},{7,6},{8,9},{9,8},{10,11... | collective-permute-start | bytes 12296 | tf_op jit(solution)/shard_map/ppermute | solution.py:241
  2.7 0.8 %collective-permute-done = f32[2,2,4,64]{3,2,1,0:T(4,128)S(1)} collective-permute-done((f32[2,2,4,64]{3,2,1,0:T(4,128)S(1)}, f32[2,2,4,64]{3,2,1,0:T(4,128)S(1)}, u32[]{:S(2)}, u32[]{:S(2)}) %collective-permute-start) | collective-permute-done | bytes 4128 | tf_op jit(solution)/shard_map/ppermute | solution.py:241
  3.5 0.1 pad_maximum_fusion.3
  3.6 3.8 %collective-permute-start.2 = (f32[2,2,4,128]{3,2,1,0:T(4,128)S(1)}, f32[2,2,4,128]{3,2,1,0:T(4,128)S(1)}, u32[]{:S(2)}, u32[]{:S(2)}) collective-permute-start(f32[2,2,4,128]{3,2,1,0:T(4,128)S(1)} %pad_maximum_fusion.3), channel_id=1, source_target_pairs={{0,24},{8,16},{16,8},{24,0},{1,25},{9,17},{17,9},{25,1},{2,26},{10... | collective-permute-start | bytes 24584 | tf_op jit(solution)/shard_map/ppermute | solution.py:28
  7.4 0.5 %collective-permute-start.1 = (f32[2,2,4,128]{3,2,1,0:T(4,128)S(1)}, f32[2,2,4,128]{3,2,1,0:T(4,128)S(1)}, u32[]{:S(2)}, u32[]{:S(2)}) collective-permute-start(f32[2,2,4,128]{3,2,1,0:T(4,128)S(1)} %pad_maximum_fusion.3), channel_id=1, source_target_pairs={{0,8},{8,0},{16,24},{24,16},{1,9},{9,1},{17,25},{25,17},{2,10},{10... | collective-permute-start | bytes 24584 | tf_op jit(solution)/shard_map/ppermute | solution.py:29
  8.0 1.1 %collective-permute-done.2 = f32[2,2,4,128]{3,2,1,0:T(4,128)S(1)} collective-permute-done((f32[2,2,4,128]{3,2,1,0:T(4,128)S(1)}, f32[2,2,4,128]{3,2,1,0:T(4,128)S(1)}, u32[]{:S(2)}, u32[]{:S(2)}) %collective-permute-start.2) | collective-permute-done | bytes 8224 | tf_op jit(solution)/shard_map/ppermute | solution.py:28
  9.0 2.0 %collective-permute-done.1 = f32[2,2,4,128]{3,2,1,0:T(4,128)S(1)} collective-permute-done((f32[2,2,4,128]{3,2,1,0:T(4,128)S(1)}, f32[2,2,4,128]{3,2,1,0:T(4,128)S(1)}, u32[]{:S(2)}, u32[]{:S(2)}) %collective-permute-start.1) | collective-permute-done | bytes 8224 | tf_op jit(solution)/shard_map/ppermute | solution.py:29
  11.1 0.1 pad_maximum_fusion.1
  11.2 3.6 %collective-permute-start.4 = (f32[6,2,4,128]{3,2,1,0:T(4,128)S(1)}, f32[6,2,4,128]{3,2,1,0:T(4,128)S(1)}, u32[]{:S(2)}, u32[]{:S(2)}) collective-permute-start(f32[6,2,4,128]{3,2,1,0:T(4,128)S(1)} %pad_maximum_fusion.1), channel_id=1, source_target_pairs={{0,6},{2,4},{4,2},{6,0},{1,7},{3,5},{5,3},{7,1},{8,14},{10,12},{12... | collective-permute-start | bytes 73736 | tf_op jit(solution)/shard_map/ppermute | solution.py:28
  14.8 0.0 collective-permute-start.3
  14.8 2.0 %collective-permute-done.4 = f32[6,2,4,128]{3,2,1,0:T(4,128)S(1)} collective-permute-done((f32[6,2,4,128]{3,2,1,0:T(4,128)S(1)}, f32[6,2,4,128]{3,2,1,0:T(4,128)S(1)}, u32[]{:S(2)}, u32[]{:S(2)}) %collective-permute-start.4) | collective-permute-done | bytes 24608 | tf_op jit(solution)/shard_map/ppermute | solution.py:28
  16.8 1.8 %collective-permute-done.3 = f32[6,2,4,128]{3,2,1,0:T(4,128)S(1)} collective-permute-done((f32[6,2,4,128]{3,2,1,0:T(4,128)S(1)}, f32[6,2,4,128]{3,2,1,0:T(4,128)S(1)}, u32[]{:S(2)}, u32[]{:S(2)}) %collective-permute-start.3) | collective-permute-done | bytes 24608 | tf_op jit(solution)/shard_map/ppermute | solution.py:29
  18.6 0.0 copy-start
  18.6 0.0 copy-start.1
  18.6 0.0 copy-start.2
  18.6 0.1 pad_maximum_fusion.region
  18.7 0.8 %copy-done = bf16[128,512]{1,0:T(8,128)(2,1)S(1)} copy-done((bf16[128,512]{1,0:T(8,128)(2,1)S(1)}, bf16[128,512]{1,0:T(8,128)(2,1)}, u32[]{:S(2)}) %copy-start) | copy-done | bytes 131096
  19.5 0.0 copy-done.1
  19.5 0.0 copy-done.2
  19.5 0.0 copy-done.3
  19.5 0.0 copy-done.4
  19.5 20.0 %shard_map.86 = (f32[4,64]{1,0:T(4,128)}, f32[4,192]{1,0:T(4,128)S(1)}, f32[1,4,192]{2,1,0:T(4,128)S(1)}) custom-call(f32[6,6,4,128]{3,2,1,0:T(4,128)S(1)} %pad_maximum_fusion.region, f32[1,128]{1,0:T(1,128)S(1)} %copy-done.4, bf16[89,128]{1,0:T(8,128)(2,1)S(1)} %copy-done.2, bf16[128,512]{1,0:T(8,128)(2,1)S(1)} %copy-done, bf16[128,128]{1,0:T(8,128)(2,1)S(1)} %copy-done.1, ...), custom_call_target="tpu_custom_call" | custom-call | tf_op jit(solution)/shard_map/pallas_call | solution.py:260
  39.5 0.0 collective-permute-start.5
  39.5 1.2 %collective-permute-done.5 = f32[4,192]{1,0:T(4,128)S(1)} collective-permute-done((f32[4,192]{1,0:T(4,128)S(1)}, f32[4,192]{1,0:T(4,128)S(1)}, u32[]{:S(2)}, u32[]{:S(2)}) %collective-permute-start.5) | collective-permute-done | bytes 3104 | tf_op jit(solution)/shard_map/ppermute | solution.py:281
  40.7 0.6 %reshape.31 = f32[2,2,1,192]{3,2,1,0:T(1,128)} reshape(f32[4,192]{1,0:T(4,128)S(1)} %add.12) | data formatting | bytes 6144 | tf_op jit(solution)/shard_map/reshape | solution.py:284
  (6 shorter events, 0.0 us)
Async XLA Ops:
  1.3 0.7 %copy-start.5 = (s32[2,2,1,64]{3,2,1,0:T(1,128)S(1)}, s32[2,2,1,64]{3,2,1,0:T(1,128)}, u32[]{:S(2)}) copy-start(s32[2,2,1,64]{3,2,1,0:T(1,128)} %param.8) | copy-start | bytes 3076
  1.4 0.7 %copy-start.6 = (s32[2,2,1]{1,2,0:T(1,128)S(1)}, s32[2,2,1]{1,2,0:T(1,128)}, u32[]{:S(2)}) copy-start(s32[2,2,1]{1,2,0:T(1,128)} %param.9) | copy-start | bytes 52
  2.2 1.3 %collective-permute-start = (f32[2,2,4,64]{3,2,1,0:T(4,128)S(1)}, f32[2,2,4,64]{3,2,1,0:T(4,128)S(1)}, u32[]{:S(2)}, u32[]{:S(2)}) collective-permute-start(f32[2,2,4,64]{3,2,1,0:T(4,128)S(1)} %pad_maximum_fusion.2), channel_id=1, source_target_pairs={{0,1},{1,0},{2,3},{3,2},{4,5},{5,4},{6,7},{7,6},{8,9},{9,8},{10,11... | collective-permute-start | bytes 12296 | tf_op jit(solution)/shard_map/ppermute | solution.py:241
  3.6 5.4 %collective-permute-start.2 = (f32[2,2,4,128]{3,2,1,0:T(4,128)S(1)}, f32[2,2,4,128]{3,2,1,0:T(4,128)S(1)}, u32[]{:S(2)}, u32[]{:S(2)}) collective-permute-start(f32[2,2,4,128]{3,2,1,0:T(4,128)S(1)} %pad_maximum_fusion.3), channel_id=1, source_target_pairs={{0,24},{8,16},{16,8},{24,0},{1,25},{9,17},{17,9},{25,1},{2,26},{10... | collective-permute-start | bytes 24584 | tf_op jit(solution)/shard_map/ppermute | solution.py:28
  7.4 3.7 %collective-permute-start.1 = (f32[2,2,4,128]{3,2,1,0:T(4,128)S(1)}, f32[2,2,4,128]{3,2,1,0:T(4,128)S(1)}, u32[]{:S(2)}, u32[]{:S(2)}) collective-permute-start(f32[2,2,4,128]{3,2,1,0:T(4,128)S(1)} %pad_maximum_fusion.3), channel_id=1, source_target_pairs={{0,8},{8,0},{16,24},{24,16},{1,9},{9,1},{17,25},{25,17},{2,10},{10... | collective-permute-start | bytes 24584 | tf_op jit(solution)/shard_map/ppermute | solution.py:29
  11.2 5.6 %collective-permute-start.4 = (f32[6,2,4,128]{3,2,1,0:T(4,128)S(1)}, f32[6,2,4,128]{3,2,1,0:T(4,128)S(1)}, u32[]{:S(2)}, u32[]{:S(2)}) collective-permute-start(f32[6,2,4,128]{3,2,1,0:T(4,128)S(1)} %pad_maximum_fusion.1), channel_id=1, source_target_pairs={{0,6},{2,4},{4,2},{6,0},{1,7},{3,5},{5,3},{7,1},{8,14},{10,12},{12... | collective-permute-start | bytes 73736 | tf_op jit(solution)/shard_map/ppermute | solution.py:28
  14.8 3.8 %collective-permute-start.3 = (f32[6,2,4,128]{3,2,1,0:T(4,128)S(1)}, f32[6,2,4,128]{3,2,1,0:T(4,128)S(1)}, u32[]{:S(2)}, u32[]{:S(2)}) collective-permute-start(f32[6,2,4,128]{3,2,1,0:T(4,128)S(1)} %pad_maximum_fusion.1), channel_id=1, source_target_pairs={{0,2},{2,0},{4,6},{6,4},{1,3},{3,1},{5,7},{7,5},{8,10},{10,8},{12,... | collective-permute-start | bytes 73736 | tf_op jit(solution)/shard_map/ppermute | solution.py:29
  18.6 0.9 %copy-start = (bf16[128,512]{1,0:T(8,128)(2,1)S(1)}, bf16[128,512]{1,0:T(8,128)(2,1)}, u32[]{:S(2)}) copy-start(bf16[128,512]{1,0:T(8,128)(2,1)} %filters.1) | copy-start | bytes 393220
  18.6 0.9 %copy-start.1 = (bf16[128,128]{1,0:T(8,128)(2,1)S(1)}, bf16[128,128]{1,0:T(8,128)(2,1)}, u32[]{:S(2)}) copy-start(bf16[128,128]{1,0:T(8,128)(2,1)} %w_up.1) | copy-start | bytes 98308
  18.6 0.9 %copy-start.2 = (bf16[89,128]{1,0:T(8,128)(2,1)S(1)}, bf16[89,128]{1,0:T(8,128)(2,1)}, u32[]{:S(2)}) copy-start(bf16[89,128]{1,0:T(8,128)(2,1)} %embed.1) | copy-start | bytes 68356
  18.7 0.8 %copy-start.3 = (f32[128]{0:T(128)S(1)}, f32[128]{0:T(128)}, u32[]{:S(2)}) copy-start(f32[128]{0:T(128)} %param.13) | copy-start | bytes 1540
  18.7 0.8 %copy-start.4 = (f32[1,128]{1,0:T(1,128)S(1)}, f32[1,128]{1,0:T(1,128)}, u32[]{:S(2)}) copy-start(f32[1,128]{1,0:T(1,128)} %constant.30.clone.1.zrow_ref) | copy-start | bytes 1540
  39.5 1.2 %collective-permute-start.5 = (f32[4,192]{1,0:T(4,128)S(1)}, f32[4,192]{1,0:T(4,128)S(1)}, u32[]{:S(2)}, u32[]{:S(2)}) collective-permute-start(f32[4,192]{1,0:T(4,128)S(1)} %bitcast.15), channel_id=1, source_target_pairs={{1,0},{0,1},{3,2},{2,3},{5,4},{4,5},{7,6},{6,7},{9,8},{8,9},{11,10... | collective-permute-start | bytes 9224 | tf_op jit(solution)/shard_map/ppermute | solution.py:281

commit v2 on v1

v2 whole, which is shorter than its diff:
```python
import functools

import jax
import jax.numpy as jnp
from jax import lax
from jax.experimental import pallas as pl
from jax.experimental.pallas import tpu as pltpu
from jax.sharding import PartitionSpec as P

MSG_SCALE = 0.1
HALO = 2
LANES = 128
NT = (((1,), (1,)), ((), ()))
NN = (((1,), (0,)), ((), ()))


def exchange(block, axis, dim, width):
    count = lax.axis_size(axis)
    first = lax.slice_in_dim(block, 0, width, axis=dim)
    last = lax.slice_in_dim(block, block.shape[dim] - width, None, axis=dim)
    if count % 2 == 0:
        odd = lax.axis_index(axis) % 2 == 1
        whole = block.shape[dim] == width
        up = block if whole else jnp.where(odd, last, first)
        down = block if whole else jnp.where(odd, first, last)
        far = [(i, (i + 1) % count if i % 2 else (i - 1) % count) for i in range(count)]
        near = [(i, i - 1 if i % 2 else i + 1) for i in range(count)]
        from_far = lax.ppermute(up, axis, far)
        from_near = lax.ppermute(down, axis, near)
        low = jnp.where(odd, from_near, from_far)
        high = jnp.where(odd, from_far, from_near)
    else:
        forward = [(i, (i + 1) % count) for i in range(count)]
        low = lax.ppermute(last, axis, forward)
        high = lax.ppermute(first, axis, [(b, a) for a, b in forward])
    return jnp.concatenate([low, block, high], axis=dim)


def dot(a, b, dims, precision=None):
    return lax.dot_general(a, b, dims, precision=precision, preferred_element_type=jnp.float32)


def split(values):
    high = values.astype(jnp.bfloat16)
    return high, (values - high.astype(jnp.float32)).astype(jnp.bfloat16)


def thirds(rows):
    high = rows.astype(jnp.bfloat16)
    middle, low = split(rows - high.astype(jnp.float32))
    at = lax.broadcasted_iota(jnp.int32, rows.shape, 0)
    parts = [part.astype(jnp.float32) for part in (high, middle, low)]
    kept = jnp.where(at == 0, parts[0], jnp.where(at == 1, parts[1], jnp.where(at == 2, parts[2], 0.0)))
    return kept.astype(jnp.bfloat16)


def kernel(
    cells, merged, rad,
    region, zrow_ref, embed, filters, w_up, w_energy,
    energies, own, other,
    emb_pad, table, onehot, stage, anchors, adj_table, mixed, act, weights_a, weights_b, kept, back, mine,
):
    nax, nay = cells[0] + 2, cells[1] + 2
    groups = region.shape[2] // 4
    slots = energies.shape[-1]
    nspec, width = embed.shape
    spec = emb_pad.shape[0]
    neighbours = [(dx, dy) for dx in (-1, 0, 1) for dy in (-1, 0, 1)]
    bf = jnp.bfloat16

    emb_pad[...] = jnp.zeros_like(emb_pad)
    emb_pad[0:nspec, :] = embed[...].astype(jnp.float32)
    emb = emb_pad[...]
    rows = dot(emb.astype(bf), filters[...], NN).astype(bf)
    for k in range(rad):
        table[k * spec:(k + 1) * spec, :] = rows[:, k * width:(k + 1) * width]
    energy_row = jnp.broadcast_to(w_energy[...], (8, width))
    readout = dot(energy_row, w_up[...].astype(jnp.float32), NT, lax.Precision.HIGHEST)
    emb_energy = dot(energy_row, emb, NT, lax.Precision.HIGHEST)

    ids = lax.broadcasted_iota(jnp.int32, (spec, LANES), 0).astype(jnp.float32)
    for x in range(region.shape[0]):
        for y in range(region.shape[1]):
            for g in range(groups):
                marked = region[x, y, g * 4 + 3:g * 4 + 4, :]
                onehot[(x * region.shape[1] + y) * groups + g] = (marked == ids).astype(bf)

    for q in range(4):
        for x in range(nax):
            stage[q, x * nay:(x + 1) * nay, :] = region[1 + x, 1:1 + nay, q, :]
        columns = stage[q].T
        for a in range(nax * nay):
            anchors[a, q] = jnp.broadcast_to(columns[0:slots, a:a + 1], (slots, LANES))

    def target(x, y, g, shift):
        row = region[x, y, g * 4:g * 4 + 3, :]
        return row[0:1] + shift[0], row[1:2] + shift[1], row[2:3]

    def z_image(dz, g):
        shift = zrow_ref[g:g + 1, :]
        if merged:
            return jnp.where(dz > 0.0, dz - shift, dz + shift)
        return dz + shift

    def onehot_at(x, y, g):
        return onehot[(x * region.shape[1] + y) * groups + g]

    step = 16
    chunks = [slice(r, r + step) for r in range(0, slots, step)]
    diagonal = lax.broadcasted_iota(jnp.int32, (slots, LANES), 0) == lax.broadcasted_iota(
        jnp.int32, (slots, LANES), 1
    )

    offsets = [(dx, dy, g) for dx, dy in neighbours for g in range(groups)]

    def weigh(a, buffer, n):
        ax, ay = a // nay, a % nay
        dx, dy, g = offsets[n]
        tx, ty, tz = target(ax + 1 + dx, ay + 1 + dy, g, (dx, dy))
        lanes = slice(n * LANES, (n + 1) * LANES)
        for c in chunks:
            ex = tx - anchors[a, 0, c, :]
            ey = ty - anchors[a, 1, c, :]
            dz = tz - anchors[a, 2, c, :]
            if merged:
                ez = jnp.abs(dz) - zrow_ref[g:g + 1, :]
            else:
                ez = dz + zrow_ref[g:g + 1, :]
            s = ex * ex + ey * ey + ez * ez
            f = jnp.maximum(1.0 - s, 0.0)
            e = jnp.exp(-0.5 * s)
            kept[a, n, 0, c, :] = f
            kept[a, n, 1, c, :] = e
            w = e * (f * f)
            if dx == 0 and dy == 0 and g == 0:
                w = jnp.where(diagonal[c], 0.0, w)
            e = e * e
            for k in range(rad):
                if k == 1:
                    w = w * e
                elif k > 1:
                    e = e * e * e
                    w = w * e
                buffer[k * slots + c.start:k * slots + c.stop, lanes] = w.astype(bf)

    def gather(a, buffer, n, total):
        ax, ay = a // nay, a % nay
        some = offsets[n:n + 2]
        hots = [onehot_at(ax + 1 + dx, ay + 1 + dy, g) for dx, dy, g in some]
        term = dot(buffer[:, n * LANES:(n + len(some)) * LANES], jnp.concatenate(hots, axis=1), NT)
        return term if total is None else total + term

    def keep(a, sums):
        for k in range(rad):
            high, low = split(sums[k * slots:(k + 1) * slots])
            mixed[a, 0:slots, k * spec:(k + 1) * spec] = high
            mixed[a, slots:, k * spec:(k + 1) * spec] = low

    def overlap(a, buffer, before, buffer_before):
        total = None
        for n in range(0, len(offsets), 2):
            total = gather(before, buffer_before, n, total)
            weigh(a, buffer, n)
            if n + 1 < len(offsets):
                weigh(a, buffer, n + 1)
        keep(before, total)

    def message_at(t, carry):
        a = 2 * t
        overlap(a, weights_a, jnp.maximum(a - 1, 0), weights_b)
        overlap(a + 1, weights_b, a, weights_a)
        return carry

    weights_b[...] = jnp.zeros_like(weights_b)
    lax.fori_loop(0, nax * nay // 2, message_at, 0)
    total = None
    for n in range(0, len(offsets), 2):
        total = gather(nax * nay - 1, weights_b, n, total)
    keep(nax * nay - 1, total)

    batch = 4

    def adjoint_at(t, carry):
        group = [t * batch + i for i in range(batch)]
        halves = dot(jnp.concatenate([mixed[a] for a in group], axis=0), table[...], NN)
        adjoints = []
        for i, a in enumerate(group):
            at = 2 * slots * i
            message = MSG_SCALE * (halves[at:at + slots] + halves[at + slots:at + 2 * slots])
            sigmoid = 1.0 / (1.0 + jnp.exp(-message))
            act[a] = (message * sigmoid).astype(bf)
            slope = sigmoid * (1.0 + message * (1.0 - sigmoid)) * readout[0:1]
            adjoints.append(jnp.where(anchors[a, 3] >= 0.0, slope, 0.0).astype(bf))
        turned = dot(jnp.concatenate(adjoints, axis=0), table[...], NT)
        for i, a in enumerate(group):
            for n, c in enumerate(chunks):
                high, low = split(turned[slots * i + c.start:slots * i + c.stop])
                for k in range(rad):
                    at = slice((n * rad + k) * step, (n * rad + k + 1) * step)
                    adj_table[a, at, 0:spec] = high[:, k * spec:(k + 1) * spec]
                    adj_table[a, at, spec:] = low[:, k * spec:(k + 1) * spec]
        return carry

    lax.fori_loop(0, nax * nay // batch, adjoint_at, 0, unroll=True)

    def pairs(a, n, x, y, gains, r):
        c = chunks[r]
        dx, dy, g = offsets[n]
        tx, ty, tz = target(x, y, g, (dx, dy))
        ex = tx - anchors[a, 0, c, :]
        ey = ty - anchors[a, 1, c, :]
        ez = z_image(tz - anchors[a, 2, c, :], g)
        f = kept[a, n, 0, c, :]
        e = kept[a, n, 1, c, :]
        e2 = e * e
        plain = None
        for k in range(rad):
            if k == 1:
                e = e * e2
            elif k > 1:
                e2 = e2 * e2 * e2
                e = e * e2
            term = e * gains[k * step:(k + 1) * step]
            scaled = (0.125 * 3.0 ** k) * term
            plain, steep = (term, scaled) if plain is None else (plain + term, steep + scaled)
        return f * (f * steep * 2.0 + plain), (ex, ey, ez)

    def both(hots):
        hots = jnp.concatenate(hots, axis=1)
        return jnp.concatenate([hots, hots], axis=0)

    def chunk_of(a, r):
        return adj_table[a, r * rad * step:(r + 1) * rad * step, :]

    scale = -4.0 * MSG_SCALE
    back[...] = jnp.zeros_like(back)
    wide = 2

    def add_back(column, forces):
        for q in range(3):
            back[column, q] += forces[q]

    def fold(values):
        return sum(values[i:i + 8] for i in range(8, step, 8)) + values[0:8]

    def forces_at(o, carry):
        ox, oy = o // cells[1], o % cells[1]
        a = (ox + 1) * nay + oy + 1
        sums = [[None] * len(chunks) for _ in range(3)]
        for first in range(0, len(offsets), wide):
            some = list(range(first, min(first + wide, len(offsets))))
            spots = [(ox + 2 + offsets[n][0], oy + 2 + offsets[n][1]) for n in some]
            hots = both([onehot_at(x, y, offsets[n][2]) for n, (x, y) in zip(some, spots)])
            totals = [[None] * 3 for _ in some]
            for r in range(len(chunks)):
                gains = dot(chunk_of(a, r), hots, NN)
                for i, (n, (x, y)) in enumerate(zip(some, spots)):
                    p, displace = pairs(a, n, x, y, gains[:, i * LANES:(i + 1) * LANES], r)
                    for q in range(3):
                        term = p * displace[q]
                        sums[q][r] = term if sums[q][r] is None else sums[q][r] + term
                        term = fold(term)
                        totals[i][q] = term if totals[i][q] is None else totals[i][q] + term
            for i, (n, (x, y)) in enumerate(zip(some, spots)):
                add_back((x * region.shape[1] + y) * groups + offsets[n][2], totals[i])
        for q in range(3):
            for r, c in enumerate(chunks):
                mine[o, q, c, :] = sums[q][r]
        return carry

    lax.fori_loop(0, cells[0] * cells[1], forces_at, 0)

    for ax in range(nax):
        for ay in range(nay):
            if 0 < ax < nax - 1 and 0 < ay < nay - 1:
                continue
            a = ax * nay + ay
            some = [
                n for n, (dx, dy, g) in enumerate(offsets)
                if 0 < ax + dx < nax - 1 and 0 < ay + dy < nay - 1
            ]
            for first in range(0, len(some), wide):
                part = some[first:first + wide]
                spots = [(ax + 1 + offsets[n][0], ay + 1 + offsets[n][1]) for n in part]
                hots = both([onehot_at(x, y, offsets[n][2]) for n, (x, y) in zip(part, spots)])
                totals = [[None] * 3 for _ in part]
                for r in range(len(chunks)):
                    gains = dot(chunk_of(a, r), hots, NN)
                    for i, (n, (x, y)) in enumerate(zip(part, spots)):
                        p, displace = pairs(a, n, x, y, gains[:, i * LANES:(i + 1) * LANES], r)
                        for q in range(3):
                            term = fold(p * displace[q])
                            totals[i][q] = term if totals[i][q] is None else totals[i][q] + term
                for i, (n, (x, y)) in enumerate(zip(part, spots)):
                    add_back((x * region.shape[1] + y) * groups + offsets[n][2], totals[i])

    inner = [(ox, oy) for ox in range(cells[0]) for oy in range(cells[1])]
    high, low = split(mine[...].reshape(len(inner) * 3 * slots, LANES))
    ones = jnp.ones((8, 2 * LANES), bf)
    rows = dot(ones, jnp.concatenate([high, low], axis=1), NT)[0:1]
    for o, (ox, oy) in enumerate(inner):
        column = ((ox + 2) * region.shape[1] + oy + 2) * groups
        sums = [jnp.sum(back[column, q], axis=0, keepdims=True)[:, 0:slots] for q in range(3)]
        for q in range(3):
            at = (o * 3 + q) * slots
            own[o:o + 1, q * slots:(q + 1) * slots] = scale * (rows[:, at:at + slots] - sums[q])
        for g in range(groups):
            start = slots if g == 0 else 0
            for q in range(3):
                row = jnp.sum(back[column + g, q], axis=0, keepdims=True)
                other[g, o:o + 1, q * slots:(q + 1) * slots] = -scale * row[:, start:start + slots]

    hots = jnp.concatenate([onehot_at(ox + 2, oy + 2, 0)[:, 0:slots] for ox, oy in inner], axis=1)
    acts = jnp.concatenate([act[(ox + 1) * nay + oy + 1] for ox, oy in inner], axis=0)
    energy = dot(thirds(emb_energy), hots, NN) + dot(thirds(readout), acts, NT)
    energy = jnp.sum(energy, axis=0, keepdims=True)
    for o, (ox, oy) in enumerate(inner):
        marked = region[ox + 2, oy + 2, 3:4, 0:slots]
        energies[o:o + 1, :] = jnp.where(marked >= 0.0, energy[:, o * slots:(o + 1) * slots], 0.0)


def layer(region, zrow, embed, filters, w_up, w_energy, block, merged, slots):
    width = embed.shape[1]
    rad = filters.shape[1] // width
    spec = -(-embed.shape[0] // LANES) * LANES
    groups = region.shape[2] // 4
    anchors = (block[0] + 2) * (block[1] + 2)
    cells = block[0] * block[1]
    columns = region.shape[0] * region.shape[1] * groups
    return pl.pallas_call(
        functools.partial(kernel, block, merged, rad),
        out_shape=(
            jax.ShapeDtypeStruct((cells, slots), jnp.float32),
            jax.ShapeDtypeStruct((cells, 3 * slots), jnp.float32),
            jax.ShapeDtypeStruct((groups, cells, 3 * slots), jnp.float32),
        ),
        in_specs=[pl.BlockSpec(memory_space=pltpu.VMEM)] * 6,
        out_specs=[pl.BlockSpec(memory_space=pltpu.VMEM)] * 3,
        scratch_shapes=[
            pltpu.VMEM((spec, width), jnp.float32),
            pltpu.VMEM((rad * spec, width), jnp.bfloat16),
            pltpu.VMEM((columns, spec, LANES), jnp.bfloat16),
            pltpu.VMEM((4, LANES, LANES), jnp.float32),
            pltpu.VMEM((anchors, 4, slots, LANES), jnp.float32),
            pltpu.VMEM((anchors, rad * slots, 2 * spec), jnp.bfloat16),
            pltpu.VMEM((anchors, 2 * slots, rad * spec), jnp.bfloat16),
            pltpu.VMEM((anchors, slots, width), jnp.bfloat16),
            pltpu.VMEM((rad * slots, 9 * groups * LANES), jnp.bfloat16),
            pltpu.VMEM((rad * slots, 9 * groups * LANES), jnp.bfloat16),
            pltpu.VMEM((anchors, 9 * groups, 2, slots, LANES), jnp.float32),
            pltpu.VMEM((columns, 3, 8, LANES), jnp.float32),
            pltpu.VMEM((cells, 3, slots, LANES), jnp.float32),
        ],
        compiler_params=pltpu.CompilerParams(vmem_limit_bytes=48 * 1024 * 1024),
    )(region, zrow, embed, filters, w_up, w_energy)


def on_device(positions, species, counts, embed, filters, w_up, w_energy):
    bx, by, bz = positions.shape[:3]
    slots = species.shape[-1]
    width = embed.shape[1]
    depth = lax.axis_size("gz")
    merged = depth * bz == 2
    occupied = jnp.arange(slots, dtype=jnp.int32) < counts[..., None]
    marked = jnp.where(occupied, species, -1).astype(jnp.float32)
    block = jnp.concatenate(
        [positions.reshape(bx, by, 3, slots), marked.reshape(bx, by, 1, slots)], axis=2
    )
    upward = [(i, (i + 1) % depth) for i in range(depth)]
    downward = [(b, a) for a, b in upward]
    low = lax.ppermute(block, "gz", upward)
    zero = jnp.zeros((slots,), jnp.float32)
    if merged:
        block = jnp.concatenate([block, low], axis=3)
        zrow = jnp.concatenate([zero, zero + 1.0])[None]
    else:
        high = lax.ppermute(block, "gz", downward)
        empty = jnp.full_like(block, -1.0)
        block = jnp.concatenate(
            [jnp.concatenate([block, low], axis=3), jnp.concatenate([high, empty], axis=3)], axis=2
        )
        zrow = jnp.stack([jnp.concatenate([zero, zero - 1.0]), jnp.concatenate([zero + 1.0, zero])])
    block = exchange(block, "gx", 0, HALO)
    region = exchange(block, "gy", 1, HALO)

    energies, own, other = layer(
        region, zrow, embed, filters, w_up, w_energy.reshape(1, width), (bx, by), merged, slots
    )

    forces = own + lax.ppermute(other[0], "gz", downward)
    if not merged:
        forces = forces + lax.ppermute(other[1], "gz", upward)
    return energies.reshape(species.shape), forces.reshape(positions.shape)


def solution(mesh):
    in_specs = (
        P("gx", "gy", "gz", None),
        P("gx", "gy", "gz", None),
        P("gx", "gy", "gz"),
        P(),
        P(),
        P(),
        P(),
    )
    out_specs = (P("gx", "gy", "gz", None), P("gx", "gy", "gz", None))
    return jax.shard_map(
        on_device, mesh=mesh, in_specs=in_specs, out_specs=out_specs, check_vma=False
    )
```

time: 41.5 us -> 36 us (0.87)
  Pallas kernels: 20 us -> 14.5 us
    pallas_call x1, Pallas kernels: 20 us -> 14.5 us  [layer(): pl.pallas_call(functools.partial(kernel, block, merged, rad), out_shape=(...]
where the time goes in v2:
time: 36 us; the launch traced here: 35.8 us
  Pallas kernels  14.5 us (40%)
  waiting for transfers between devices  8.93 us (25%)
  starting transfers between devices  8.46 us (24%)
  local copies, waits for them, and re-layouts  2.18 us (6%)
  other arithmetic  1.04 us (3%)
  between operations  0.68 us (2%)
    pallas_call x1, Pallas kernels, layer(): pl.pallas_call(functools.partial(kernel, block, merged, rad), out_shape=(...  14.5 us
    ppermute x2, starting transfers between devices, exchange(): from_far = lax.ppermute(up, axis, far)  7.4 us
    ppermute x2, waiting for transfers between devices, exchange(): from_near = lax.ppermute(down, axis, near)  3.82 us
    ppermute x2, waiting for transfers between devices, exchange(): from_far = lax.ppermute(up, axis, far)  3.11 us
    unnamed x14, local copies, waits for them, and re-layouts  1.49 us
    ppermute x1, waiting for transfers between devices, on_device(): forces = own + lax.ppermute(other[0], 'gz', downward)  1.16 us
    ppermute x1, waiting for transfers between devices, on_device(): low = lax.ppermute(block, 'gz', upward)  0.83 us
  transfers between devices with their start and end apart: 6, of which 6 were waited for; matrix products, arithmetic and copies ran while one was open for 0% of the time, Pallas kernels for 0%

profile of v2, /device:TPU:0, one launch (start us, length us, event | category | flops | bytes accessed | tf_op | source)
XLA Modules:
  0.0 35.8 jit_solution(17547714619246747026)
XLA Ops:
  0.6 0.7 %reduce = f32[2,2,192]{2,1,0:T(2,128)S(1)} reduce(f32[2,2,1,192]{3,2,1,0:T(1,128)} %param.7, f32[]{:T(128)} %constant.34), dimensions={2}, to_apply=%param.7.reduce_sub_computation | reduce | bytes 6148 | tf_op args[0]
  1.3 0.0 copy-start.5
  1.4 0.1 reshape.27
  1.4 0.0 copy-start.6
  1.4 0.6 %copy-done.5 = s32[2,2,1,64]{3,2,1,0:T(1,128)S(1)} copy-done((s32[2,2,1,64]{3,2,1,0:T(1,128)S(1)}, s32[2,2,1,64]{3,2,1,0:T(1,128)}, u32[]{:S(2)}) %copy-start.5) | copy-done | bytes 1048
  2.0 0.1 copy-done.6
  2.1 0.1 fusion
  2.2 0.5 %collective-permute-start = (f32[2,2,4,64]{3,2,1,0:T(4,128)S(1)}, f32[2,2,4,64]{3,2,1,0:T(4,128)S(1)}, u32[]{:S(2)}, u32[]{:S(2)}) collective-permute-start(f32[2,2,4,64]{3,2,1,0:T(4,128)S(1)} %pad_maximum_fusion.2), channel_id=1, source_target_pairs={{0,1},{1,0},{2,3},{3,2},{4,5},{5,4},{6,7},{7,6},{8,9},{9,8},{10,11... | collective-permute-start | bytes 12296 | tf_op jit(solution)/shard_map/ppermute | solution.py:371
  2.7 0.8 %collective-permute-done = f32[2,2,4,64]{3,2,1,0:T(4,128)S(1)} collective-permute-done((f32[2,2,4,64]{3,2,1,0:T(4,128)S(1)}, f32[2,2,4,64]{3,2,1,0:T(4,128)S(1)}, u32[]{:S(2)}, u32[]{:S(2)}) %collective-permute-start) | collective-permute-done | bytes 4128 | tf_op jit(solution)/shard_map/ppermute | solution.py:371
  3.5 0.1 pad_maximum_fusion.3
  3.6 3.8 %collective-permute-start.2 = (f32[2,2,4,128]{3,2,1,0:T(4,128)S(1)}, f32[2,2,4,128]{3,2,1,0:T(4,128)S(1)}, u32[]{:S(2)}, u32[]{:S(2)}) collective-permute-start(f32[2,2,4,128]{3,2,1,0:T(4,128)S(1)} %pad_maximum_fusion.3), channel_id=1, source_target_pairs={{0,24},{8,16},{16,8},{24,0},{1,25},{9,17},{17,9},{25,1},{2,26},{10... | collective-permute-start | bytes 24584 | tf_op jit(solution)/shard_map/ppermute | solution.py:28
  7.4 0.5 %collective-permute-start.1 = (f32[2,2,4,128]{3,2,1,0:T(4,128)S(1)}, f32[2,2,4,128]{3,2,1,0:T(4,128)S(1)}, u32[]{:S(2)}, u32[]{:S(2)}) collective-permute-start(f32[2,2,4,128]{3,2,1,0:T(4,128)S(1)} %pad_maximum_fusion.3), channel_id=1, source_target_pairs={{0,8},{8,0},{16,24},{24,16},{1,9},{9,1},{17,25},{25,17},{2,10},{10... | collective-permute-start | bytes 24584 | tf_op jit(solution)/shard_map/ppermute | solution.py:29
  8.0 1.1 %collective-permute-done.2 = f32[2,2,4,128]{3,2,1,0:T(4,128)S(1)} collective-permute-done((f32[2,2,4,128]{3,2,1,0:T(4,128)S(1)}, f32[2,2,4,128]{3,2,1,0:T(4,128)S(1)}, u32[]{:S(2)}, u32[]{:S(2)}) %collective-permute-start.2) | collective-permute-done | bytes 8224 | tf_op jit(solution)/shard_map/ppermute | solution.py:28
  9.0 2.0 %collective-permute-done.1 = f32[2,2,4,128]{3,2,1,0:T(4,128)S(1)} collective-permute-done((f32[2,2,4,128]{3,2,1,0:T(4,128)S(1)}, f32[2,2,4,128]{3,2,1,0:T(4,128)S(1)}, u32[]{:S(2)}, u32[]{:S(2)}) %collective-permute-start.1) | collective-permute-done | bytes 8224 | tf_op jit(solution)/shard_map/ppermute | solution.py:29
  11.1 0.1 pad_maximum_fusion.1
  11.2 3.6 %collective-permute-start.4 = (f32[6,2,4,128]{3,2,1,0:T(4,128)S(1)}, f32[6,2,4,128]{3,2,1,0:T(4,128)S(1)}, u32[]{:S(2)}, u32[]{:S(2)}) collective-permute-start(f32[6,2,4,128]{3,2,1,0:T(4,128)S(1)} %pad_maximum_fusion.1), channel_id=1, source_target_pairs={{0,6},{2,4},{4,2},{6,0},{1,7},{3,5},{5,3},{7,1},{8,14},{10,12},{12... | collective-permute-start | bytes 73736 | tf_op jit(solution)/shard_map/ppermute | solution.py:28
  14.8 0.0 collective-permute-start.3
  14.8 2.0 %collective-permute-done.4 = f32[6,2,4,128]{3,2,1,0:T(4,128)S(1)} collective-permute-done((f32[6,2,4,128]{3,2,1,0:T(4,128)S(1)}, f32[6,2,4,128]{3,2,1,0:T(4,128)S(1)}, u32[]{:S(2)}, u32[]{:S(2)}) %collective-permute-start.4) | collective-permute-done | bytes 24608 | tf_op jit(solution)/shard_map/ppermute | solution.py:28
  16.8 1.8 %collective-permute-done.3 = f32[6,2,4,128]{3,2,1,0:T(4,128)S(1)} collective-permute-done((f32[6,2,4,128]{3,2,1,0:T(4,128)S(1)}, f32[6,2,4,128]{3,2,1,0:T(4,128)S(1)}, u32[]{:S(2)}, u32[]{:S(2)}) %collective-permute-start.3) | collective-permute-done | bytes 24608 | tf_op jit(solution)/shard_map/ppermute | solution.py:29
  18.6 0.0 copy-start
  18.6 0.0 copy-start.1
  18.6 0.0 copy-start.2
  18.6 0.1 pad_maximum_fusion.region
  18.7 0.8 %copy-done = bf16[128,512]{1,0:T(8,128)(2,1)S(1)} copy-done((bf16[128,512]{1,0:T(8,128)(2,1)S(1)}, bf16[128,512]{1,0:T(8,128)(2,1)}, u32[]{:S(2)}) %copy-start) | copy-done | bytes 131096
  19.5 0.0 copy-done.1
  19.5 0.0 copy-done.2
  19.5 0.0 copy-done.3
  19.5 0.0 copy-done.4
  19.5 14.5 %shard_map.86 = (f32[4,64]{1,0:T(4,128)}, f32[4,192]{1,0:T(4,128)S(1)}, f32[1,4,192]{2,1,0:T(4,128)S(1)}) custom-call(f32[6,6,4,128]{3,2,1,0:T(4,128)S(1)} %pad_maximum_fusion.region, f32[1,128]{1,0:T(1,128)S(1)} %copy-done.4, bf16[89,128]{1,0:T(8,128)(2,1)S(1)} %copy-done.2, bf16[128,512]{1,0:T(8,128)(2,1)S(1)} %copy-done, bf16[128,128]{1,0:T(8,128)(2,1)S(1)} %copy-done.1, ...), custom_call_target="tpu_custom_call" | custom-call | tf_op jit(solution)/shard_map/pallas_call | solution.py:330
  34.0 0.0 collective-permute-start.5
  34.0 1.2 %collective-permute-done.5 = f32[4,192]{1,0:T(4,128)S(1)} collective-permute-done((f32[4,192]{1,0:T(4,128)S(1)}, f32[4,192]{1,0:T(4,128)S(1)}, u32[]{:S(2)}, u32[]{:S(2)}) %collective-permute-start.5) | collective-permute-done | bytes 3104 | tf_op jit(solution)/shard_map/ppermute | solution.py:390
  35.2 0.6 %reshape.31 = f32[2,2,1,192]{3,2,1,0:T(1,128)} reshape(f32[4,192]{1,0:T(4,128)S(1)} %add.12) | data formatting | bytes 6144 | tf_op jit(solution)/shard_map/reshape | solution.py:393
  (6 shorter events, 0.0 us)
Async XLA Ops:
  1.3 0.7 %copy-start.5 = (s32[2,2,1,64]{3,2,1,0:T(1,128)S(1)}, s32[2,2,1,64]{3,2,1,0:T(1,128)}, u32[]{:S(2)}) copy-start(s32[2,2,1,64]{3,2,1,0:T(1,128)} %param.8) | copy-start | bytes 3076
  1.4 0.7 %copy-start.6 = (s32[2,2,1]{1,2,0:T(1,128)S(1)}, s32[2,2,1]{1,2,0:T(1,128)}, u32[]{:S(2)}) copy-start(s32[2,2,1]{1,2,0:T(1,128)} %param.9) | copy-start | bytes 52
  2.2 1.3 %collective-permute-start = (f32[2,2,4,64]{3,2,1,0:T(4,128)S(1)}, f32[2,2,4,64]{3,2,1,0:T(4,128)S(1)}, u32[]{:S(2)}, u32[]{:S(2)}) collective-permute-start(f32[2,2,4,64]{3,2,1,0:T(4,128)S(1)} %pad_maximum_fusion.2), channel_id=1, source_target_pairs={{0,1},{1,0},{2,3},{3,2},{4,5},{5,4},{6,7},{7,6},{8,9},{9,8},{10,11... | collective-permute-start | bytes 12296 | tf_op jit(solution)/shard_map/ppermute | solution.py:371
  3.6 5.4 %collective-permute-start.2 = (f32[2,2,4,128]{3,2,1,0:T(4,128)S(1)}, f32[2,2,4,128]{3,2,1,0:T(4,128)S(1)}, u32[]{:S(2)}, u32[]{:S(2)}) collective-permute-start(f32[2,2,4,128]{3,2,1,0:T(4,128)S(1)} %pad_maximum_fusion.3), channel_id=1, source_target_pairs={{0,24},{8,16},{16,8},{24,0},{1,25},{9,17},{17,9},{25,1},{2,26},{10... | collective-permute-start | bytes 24584 | tf_op jit(solution)/shard_map/ppermute | solution.py:28
  7.4 3.7 %collective-permute-start.1 = (f32[2,2,4,128]{3,2,1,0:T(4,128)S(1)}, f32[2,2,4,128]{3,2,1,0:T(4,128)S(1)}, u32[]{:S(2)}, u32[]{:S(2)}) collective-permute-start(f32[2,2,4,128]{3,2,1,0:T(4,128)S(1)} %pad_maximum_fusion.3), channel_id=1, source_target_pairs={{0,8},{8,0},{16,24},{24,16},{1,9},{9,1},{17,25},{25,17},{2,10},{10... | collective-permute-start | bytes 24584 | tf_op jit(solution)/shard_map/ppermute | solution.py:29
  11.2 5.6 %collective-permute-start.4 = (f32[6,2,4,128]{3,2,1,0:T(4,128)S(1)}, f32[6,2,4,128]{3,2,1,0:T(4,128)S(1)}, u32[]{:S(2)}, u32[]{:S(2)}) collective-permute-start(f32[6,2,4,128]{3,2,1,0:T(4,128)S(1)} %pad_maximum_fusion.1), channel_id=1, source_target_pairs={{0,6},{2,4},{4,2},{6,0},{1,7},{3,5},{5,3},{7,1},{8,14},{10,12},{12... | collective-permute-start | bytes 73736 | tf_op jit(solution)/shard_map/ppermute | solution.py:28
  14.8 3.8 %collective-permute-start.3 = (f32[6,2,4,128]{3,2,1,0:T(4,128)S(1)}, f32[6,2,4,128]{3,2,1,0:T(4,128)S(1)}, u32[]{:S(2)}, u32[]{:S(2)}) collective-permute-start(f32[6,2,4,128]{3,2,1,0:T(4,128)S(1)} %pad_maximum_fusion.1), channel_id=1, source_target_pairs={{0,2},{2,0},{4,6},{6,4},{1,3},{3,1},{5,7},{7,5},{8,10},{10,8},{12,... | collective-permute-start | bytes 73736 | tf_op jit(solution)/shard_map/ppermute | solution.py:29
  18.6 0.9 %copy-start = (bf16[128,512]{1,0:T(8,128)(2,1)S(1)}, bf16[128,512]{1,0:T(8,128)(2,1)}, u32[]{:S(2)}) copy-start(bf16[128,512]{1,0:T(8,128)(2,1)} %filters.1) | copy-start | bytes 393220
  18.6 0.9 %copy-start.1 = (bf16[128,128]{1,0:T(8,128)(2,1)S(1)}, bf16[128,128]{1,0:T(8,128)(2,1)}, u32[]{:S(2)}) copy-start(bf16[128,128]{1,0:T(8,128)(2,1)} %w_up.1) | copy-start | bytes 98308
  18.6 0.9 %copy-start.2 = (bf16[89,128]{1,0:T(8,128)(2,1)S(1)}, bf16[89,128]{1,0:T(8,128)(2,1)}, u32[]{:S(2)}) copy-start(bf16[89,128]{1,0:T(8,128)(2,1)} %embed.1) | copy-start | bytes 68356
  18.7 0.8 %copy-start.3 = (f32[128]{0:T(128)S(1)}, f32[128]{0:T(128)}, u32[]{:S(2)}) copy-start(f32[128]{0:T(128)} %param.13) | copy-start | bytes 1540
  18.7 0.8 %copy-start.4 = (f32[1,128]{1,0:T(1,128)S(1)}, f32[1,128]{1,0:T(1,128)}, u32[]{:S(2)}) copy-start(f32[1,128]{1,0:T(1,128)} %constant.30.clone.1.zrow_ref) | copy-start | bytes 1540
  34.0 1.2 %collective-permute-start.5 = (f32[4,192]{1,0:T(4,128)S(1)}, f32[4,192]{1,0:T(4,128)S(1)}, u32[]{:S(2)}, u32[]{:S(2)}) collective-permute-start(f32[4,192]{1,0:T(4,128)S(1)} %bitcast.15), channel_id=1, source_target_pairs={{1,0},{0,1},{3,2},{2,3},{5,4},{4,5},{7,6},{6,7},{9,8},{8,9},{11,10... | collective-permute-start | bytes 9224 | tf_op jit(solution)/shard_map/ppermute | solution.py:390

commit v3 on v0

v3 whole, which is shorter than its diff:
```python
import functools

import jax
import jax.numpy as jnp
from jax import lax
from jax.experimental import pallas as pl
from jax.experimental.pallas import tpu as pltpu
from jax.sharding import PartitionSpec as P

MSG_SCALE = 0.1
HALO = 2
FAR_VMEM = 36 * 1024 * 1024
LANES = 128
STEP = 16
WIDE = 2
LOG2E = 1.4426950408889634
NT = (((1,), (1,)), ((), ()))
NN = (((1,), (0,)), ((), ()))


def exchange(block, axis, dim, width):
    count = lax.axis_size(axis)
    first = lax.slice_in_dim(block, 0, width, axis=dim)
    last = lax.slice_in_dim(block, block.shape[dim] - width, None, axis=dim)
    if count % 2 == 0:
        odd = lax.axis_index(axis) % 2 == 1
        whole = block.shape[dim] == width
        up = block if whole else jnp.where(odd, last, first)
        down = block if whole else jnp.where(odd, first, last)
        far = [(i, (i + 1) % count if i % 2 else (i - 1) % count) for i in range(count)]
        near = [(i, i - 1 if i % 2 else i + 1) for i in range(count)]
        from_far = lax.ppermute(up, axis, far)
        from_near = lax.ppermute(down, axis, near)
        low = jnp.where(odd, from_near, from_far)
        high = jnp.where(odd, from_far, from_near)
    else:
        forward = [(i, (i + 1) % count) for i in range(count)]
        low = lax.ppermute(last, axis, forward)
        high = lax.ppermute(first, axis, [(b, a) for a, b in forward])
    return jnp.concatenate([low, block, high], axis=dim)


def dot(a, b, dims, precision=None):
    return lax.dot_general(a, b, dims, precision=precision, preferred_element_type=jnp.float32)


def split(values):
    high = values.astype(jnp.bfloat16)
    return high, (values - high.astype(jnp.float32)).astype(jnp.bfloat16)


def thirds(rows):
    high = rows.astype(jnp.bfloat16)
    middle, low = split(rows - high.astype(jnp.float32))
    at = lax.broadcasted_iota(jnp.int32, rows.shape, 0)
    parts = [part.astype(jnp.float32) for part in (high, middle, low)]
    kept = jnp.where(at == 0, parts[0], jnp.where(at == 1, parts[1], jnp.where(at == 2, parts[2], 0.0)))
    return kept.astype(jnp.bfloat16)


class Cells:
    def __init__(self, block, merged, rad, spec, slots):
        self.block, self.merged, self.rad, self.spec, self.slots = block, merged, rad, spec, slots
        self.groups = 1 if merged else 2
        self.nax, self.nay = block[0] + 2, block[1] + 2
        self.nx, self.ny = block[0] + 2 * HALO, block[1] + 2 * HALO
        self.offsets = [
            (dx, dy, g) for dx in (-1, 0, 1) for dy in (-1, 0, 1) for g in range(self.groups)
        ]
        self.rows = [slice(r, r + STEP) for r in range(0, slots, STEP)]

    def inner(self, ay):
        return 1 <= ay <= self.block[1]

    def split_offsets(self, ay):
        near = [n for n, (_, dy, _) in enumerate(self.offsets) if self.inner(ay) and self.inner(ay + dy)]
        return near, [n for n in range(len(self.offsets)) if n not in near]

    def z_shift(self, g):
        lane = lax.broadcasted_iota(jnp.int32, (1, LANES), 1)
        if self.merged:
            return jnp.where(lane < self.slots, 0.0, 1.0)
        if g == 0:
            return jnp.where(lane < self.slots, 0.0, -1.0)
        return jnp.where(lane < self.slots, 1.0, 0.0)


def place_anchors(z, stage, rows, out):
    for q in range(4):
        for i, (ref, x, y) in enumerate(rows):
            stage[q, i:i + 1, :] = ref[x, y, q:q + 1, :]
        columns = stage[q].T
        for i in range(len(rows)):
            out[i, q] = jnp.broadcast_to(columns[0:z.slots, i:i + 1], (z.slots, LANES))


def place_onehot(z, ref, x, y, g, out, at):
    ids = lax.broadcasted_iota(jnp.int32, (z.spec, LANES), 0).astype(jnp.float32)
    out[at] = (ref[x, y, g * 4 + 3:g * 4 + 4, :] == ids).astype(jnp.bfloat16)


def target(ref, x, y, offset):
    dx, dy, g = offset
    row = ref[x, y, g * 4:g * 4 + 3, :]
    return row[0:1] + dx, row[1:2] + dy, row[2:3]


def weigh(z, position, anchor, offset, buffer, lanes, keep):
    tx, ty, tz = position
    shift = z.z_shift(offset[2])
    for c in z.rows:
        ex = tx - anchor[0, c, :]
        ey = ty - anchor[1, c, :]
        dz = tz - anchor[2, c, :]
        ez = jnp.abs(dz) - shift if z.merged else dz + shift
        s = ex * ex + ey * ey + ez * ez
        f = jnp.maximum(1.0 - s, 0.0)
        power = s * (-0.5 * LOG2E)
        e = jnp.exp2(power)
        keep[0, c, :] = f
        keep[1, c, :] = e
        f = f * f
        if offset == (0, 0, 0):
            row = lax.broadcasted_iota(jnp.int32, (STEP, LANES), 0) + c.start
            lane = lax.broadcasted_iota(jnp.int32, (STEP, LANES), 1)
            f = jnp.where(row == lane, 0.0, f)
        for k in range(z.rad):
            if k:
                power = power * 3.0
                e = jnp.exp2(power)
            buffer[k * z.slots + c.start:k * z.slots + c.stop, lanes] = (e * f).astype(jnp.bfloat16)


def pack_kernel(counts_hbm, positions_hbm, species_hbm, out, counts, positions, species, arrived):
    arguments = [(counts_hbm, counts), (positions_hbm, positions), (species_hbm, species)]
    copies = [pltpu.make_async_copy(a, b, arrived.at[i]) for i, (a, b) in enumerate(arguments)]
    for copy in copies:
        copy.start()
    for copy in copies:
        copy.wait()
    slots = out.shape[3]
    lane = lax.broadcasted_iota(jnp.int32, (1, slots), 1)
    for x in range(out.shape[0]):
        for y in range(out.shape[1]):
            row = positions[x, y, 0:1, :]
            for q in range(3):
                out[x, y, q:q + 1, :] = row[:, q * slots:(q + 1) * slots]
            marked = jnp.where(lane < counts[x, y], species[x, y, 0:1, :], -1)
            out[x, y, 3:4, :] = marked.astype(jnp.float32)


def near_kernel(
    z, near, embed_hbm, filters_hbm, w_up_hbm, w_energy_hbm,
    table, readout, emb_energy, onehot, anchors, sums, kept,
    emb_pad, stage, embed, filters, w_up, w_energy, arrived, *buffers,
):
    nspec, width = embed.shape
    by = z.block[1]
    weights = [(embed_hbm, embed), (filters_hbm, filters), (w_up_hbm, w_up), (w_energy_hbm, w_energy)]
    copies = [pltpu.make_async_copy(a, b, arrived.at[i]) for i, (a, b) in enumerate(weights)]
    for copy in copies:
        copy.start()

    for x in range(z.nx):
        for y in range(by):
            for g in range(z.groups):
                place_onehot(z, near, x, y, g, onehot, (x * by + y) * z.groups + g)
    place_anchors(z, stage, [(near, ax + 1, y) for ax in range(z.nax) for y in range(by)], anchors)

    def message_at(ax, carry):
        for y in range(by):
            a = ax * by + y
            some = z.split_offsets(y + 1)[0]
            hots = []
            for i, n in enumerate(some):
                dx, dy, g = z.offsets[n]
                spot = target(near, ax + 1 + dx, y + dy, z.offsets[n])
                weigh(
                    z, spot, anchors.at[a], z.offsets[n], buffers[y],
                    slice(i * LANES, (i + 1) * LANES), kept.at[a, i],
                )
                hots.append(onehot[((ax + 1 + dx) * by + y + dy) * z.groups + g])
            weights = buffers[y][:, 0:len(some) * LANES]
            sums[a] = dot(weights, jnp.concatenate(hots, axis=1), NT)
        return carry

    lax.fori_loop(0, z.nax, message_at, 0)

    for copy in copies:
        copy.wait()
    emb_pad[...] = jnp.zeros_like(emb_pad)
    emb_pad[0:nspec, :] = embed[...].astype(jnp.float32)
    emb = emb_pad[...]
    rows = dot(emb.astype(jnp.bfloat16), filters[...], NN).astype(jnp.bfloat16)
    for k in range(z.rad):
        table[k * z.spec:(k + 1) * z.spec, :] = rows[:, k * width:(k + 1) * width]
    energy_row = jnp.broadcast_to(w_energy[...], (8, width))
    readout[...] = dot(energy_row, w_up[...].astype(jnp.float32), NT, lax.Precision.HIGHEST)
    emb_energy[...] = dot(energy_row, emb, NT, lax.Precision.HIGHEST)


def far_kernel(
    z, region, table, readout_ref, emb_energy_ref, onehot_near, anchors_near, sums_near, kept_near,
    energies, own, other,
    onehot_far, anchors_far, kept_far, stage, adj_table, mixed, act, back, mine, *buffers,
):
    by = z.block[1]
    bf = jnp.bfloat16
    slots, spec, rad = z.slots, z.spec, z.rad
    readout = readout_ref[...]
    outer = [y for y in range(z.ny) if not HALO <= y < HALO + by]

    for x in range(z.nx):
        for i, y in enumerate(outer):
            for g in range(z.groups):
                place_onehot(z, region, x, y, g, onehot_far, (x * len(outer) + i) * z.groups + g)
    place_anchors(
        z, stage, [(region, ax + 1, y) for ax in range(z.nax) for y in (1, z.ny - HALO)], anchors_far
    )

    def onehot_at(x, y, g):
        if y in outer:
            return onehot_far[(x * len(outer) + outer.index(y)) * z.groups + g]
        return onehot_near[(x * by + y - HALO) * z.groups + g]

    def anchor_at(ax, ay):
        if z.inner(ay):
            return anchors_near.at[ax * by + ay - 1]
        return anchors_far.at[ax * 2 + (ay > 0)]

    def kept_at(ax, ay, n):
        near, _ = z.split_offsets(ay)
        if n in near:
            return kept_near.at[ax * by + ay - 1, near.index(n)]
        return kept_far.at[ax * z.nay + ay, n]

    def message_at(ax, carry):
        for ay in range(z.nay):
            a = ax * z.nay + ay
            some = z.split_offsets(ay)[1]
            hots = []
            for i, n in enumerate(some):
                dx, dy, g = z.offsets[n]
                x, y = ax + 1 + dx, ay + 1 + dy
                weigh(
                    z, target(region, x, y, z.offsets[n]), anchor_at(ax, ay), z.offsets[n], buffers[ay],
                    slice(i * LANES, (i + 1) * LANES), kept_at(ax, ay, n),
                )
                hots.append(onehot_at(x, y, g))
            total = sums_near[ax * by + ay - 1] if z.inner(ay) else None
            if some:
                term = dot(buffers[ay][:, 0:len(some) * LANES], jnp.concatenate(hots, axis=1), NT)
                total = term if total is None else total + term
            for k in range(rad):
                high, low = split(total[k * slots:(k + 1) * slots])
                mixed[a, 0:slots, k * spec:(k + 1) * spec] = high
                mixed[a, slots:, k * spec:(k + 1) * spec] = low
        return carry

    lax.fori_loop(0, z.nax, message_at, 0)

    def adjoint_at(ax, carry):
        group = [ax * z.nay + ay for ay in range(z.nay)]
        halves = dot(jnp.concatenate([mixed[a] for a in group], axis=0), table[...], NN)
        adjoints = []
        for ay, a in enumerate(group):
            at = 2 * slots * ay
            message = MSG_SCALE * (halves[at:at + slots] + halves[at + slots:at + 2 * slots])
            sigmoid = 1.0 / (1.0 + jnp.exp(-message))
            act[a] = (message * sigmoid).astype(bf)
            slope = sigmoid * (1.0 + message * (1.0 - sigmoid)) * readout[0:1]
            adjoints.append(jnp.where(anchor_at(ax, ay)[3] >= 0.0, slope, 0.0).astype(bf))
        turned = dot(jnp.concatenate(adjoints, axis=0), table[...], NT)
        for ay, a in enumerate(group):
            for r, c in enumerate(z.rows):
                high, low = split(turned[slots * ay + c.start:slots * ay + c.stop])
                for k in range(rad):
                    at = slice((r * rad + k) * STEP, (r * rad + k + 1) * STEP)
                    adj_table[a, at, 0:spec] = high[:, k * spec:(k + 1) * spec]
                    adj_table[a, at, spec:] = low[:, k * spec:(k + 1) * spec]
        return carry

    lax.fori_loop(0, z.nax, adjoint_at, 0, unroll=True)

    def pairs(ax, ay, n, gains, r):
        c = z.rows[r]
        dx, dy, g = z.offsets[n]
        tx, ty, tz = target(region, ax + 1 + dx, ay + 1 + dy, z.offsets[n])
        anchor, keep = anchor_at(ax, ay), kept_at(ax, ay, n)
        ex = tx - anchor[0, c, :]
        ey = ty - anchor[1, c, :]
        ez = tz - anchor[2, c, :]
        shift = z.z_shift(g)
        ez = ez + jnp.where(ez > 0.0, -shift, shift) if z.merged else ez + shift
        f = keep[0, c, :]
        e = keep[1, c, :]
        e2 = e * e
        plain = None
        for k in range(rad):
            if k == 1:
                e = e * e2
            elif k > 1:
                e2 = e2 * e2 * e2
                e = e * e2
            term = e * gains[k * STEP:(k + 1) * STEP]
            scaled = (0.25 * 3.0 ** k) * term
            plain, steep = (term, scaled) if plain is None else (plain + term, steep + scaled)
        return f * (f * steep + plain), (ex, ey, ez)

    def blocks(ax, ay, some, sums):
        a = ax * z.nay + ay
        for first in range(0, len(some), WIDE):
            part = some[first:first + WIDE]
            spots = [(ax + 1 + z.offsets[n][0], ay + 1 + z.offsets[n][1], z.offsets[n][2]) for n in part]
            hots = jnp.concatenate([onehot_at(*spot) for spot in spots], axis=1)
            hots = jnp.concatenate([hots, hots], axis=0)
            totals = [[None] * 3 for _ in part]
            for r in range(len(z.rows)):
                gains = dot(adj_table[a, r * rad * STEP:(r + 1) * rad * STEP, :], hots, NN)
                for i, n in enumerate(part):
                    p, displace = pairs(ax, ay, n, gains[:, i * LANES:(i + 1) * LANES], r)
                    for q in range(3):
                        term = p * displace[q]
                        if sums is not None:
                            sums[q][r] = term if sums[q][r] is None else sums[q][r] + term
                        term = sum(term[j:j + 8] for j in range(8, STEP, 8)) + term[0:8]
                        totals[i][q] = term if totals[i][q] is None else totals[i][q] + term
            for (x, y, g), total in zip(spots, totals):
                for q in range(3):
                    back[(x * z.ny + y) * z.groups + g, q] += total[q]

    back[...] = jnp.zeros_like(back)

    def forces_at(ox, carry):
        for oy in range(by):
            sums = [[None] * len(z.rows) for _ in range(3)]
            blocks(ox + 1, oy + 1, range(len(z.offsets)), sums)
            for q in range(3):
                for r, c in enumerate(z.rows):
                    mine[ox * by + oy, q, c, :] = sums[q][r]
        return carry

    lax.fori_loop(0, z.block[0], forces_at, 0)

    for ax in range(z.nax):
        for ay in range(z.nay):
            if 0 < ax < z.nax - 1 and z.inner(ay):
                continue
            blocks(ax, ay, [
                n for n, (dx, dy, _) in enumerate(z.offsets) if 0 < ax + dx < z.nax - 1 and z.inner(ay + dy)
            ], None)

    scale = -4.0 * MSG_SCALE
    cells = [(ox, oy) for ox in range(z.block[0]) for oy in range(by)]
    high, low = split(mine[...].reshape(len(cells) * 3 * slots, LANES))
    ones = jnp.ones((8, 2 * LANES), bf)
    rows = dot(ones, jnp.concatenate([high, low], axis=1), NT)[0:1]
    for o, (ox, oy) in enumerate(cells):
        column = ((ox + HALO) * z.ny + oy + HALO) * z.groups
        sums = [jnp.sum(back[column, q], axis=0, keepdims=True)[:, 0:slots] for q in range(3)]
        for q in range(3):
            at = (o * 3 + q) * slots
            own[ox, oy, :, q * slots:(q + 1) * slots] = scale * (rows[:, at:at + slots] - sums[q])
        for g in range(z.groups):
            start = slots if g == 0 else 0
            for q in range(3):
                row = jnp.sum(back[column + g, q], axis=0, keepdims=True)
                other[g, ox, oy, :, q * slots:(q + 1) * slots] = -scale * row[:, start:start + slots]

    hots = jnp.concatenate([onehot_at(ox + HALO, oy + HALO, 0)[:, 0:slots] for ox, oy in cells], axis=1)
    acts = jnp.concatenate([act[(ox + 1) * z.nay + oy + 1] for ox, oy in cells], axis=0)
    energy = dot(thirds(emb_energy_ref[...]), hots, NN) + dot(thirds(readout), acts, NT)
    energy = jnp.sum(energy, axis=0, keepdims=True)
    for o, (ox, oy) in enumerate(cells):
        marked = region[ox + HALO, oy + HALO, 3:4, 0:slots]
        energies[ox, oy, :, :] = jnp.where(marked >= 0.0, energy[:, o * slots:(o + 1) * slots], 0.0)


VMEM = pl.BlockSpec(memory_space=pltpu.VMEM)
HBM = pl.BlockSpec(memory_space=pltpu.HBM)


def in_hbm(*arrays):
    return [pltpu.with_memory_space_constraint(array, pltpu.HBM) for array in arrays]


def pack(positions, species, counts):
    bx, by, _, slots = species.shape
    return pl.pallas_call(
        pack_kernel,
        out_shape=jax.ShapeDtypeStruct((bx, by, 4, slots), jnp.float32),
        in_specs=[HBM] * 3,
        out_specs=VMEM,
        scratch_shapes=[
            pltpu.SMEM(counts.shape, counts.dtype),
            pltpu.VMEM(positions.shape, positions.dtype),
            pltpu.VMEM(species.shape, species.dtype),
            pltpu.SemaphoreType.DMA((3,)),
        ],
        compiler_params=pltpu.CompilerParams(vmem_limit_bytes=1024 * 1024),
    )(*in_hbm(counts, positions, species))


def near_layer(z, near, embed, filters, w_up, w_energy):
    width = embed.shape[1]
    by = z.block[1]
    cells, most = z.nax * by, max(len(z.split_offsets(y + 1)[0]) for y in range(by))
    shapes = [
        ((z.rad * z.spec, width), jnp.bfloat16),
        ((8, width), jnp.float32),
        ((8, z.spec), jnp.float32),
        ((z.nx * by * z.groups, z.spec, LANES), jnp.bfloat16),
        ((cells, 4, z.slots, LANES), jnp.float32),
        ((cells, z.rad * z.slots, z.spec), jnp.float32),
        ((cells, most, 2, z.slots, LANES), jnp.float32),
    ]
    flops = 2 * cells * most * z.rad * z.slots * LANES * z.spec
    return pl.pallas_call(
        functools.partial(near_kernel, z),
        out_shape=[jax.ShapeDtypeStruct(*shape) for shape in shapes],
        in_specs=[VMEM] + [HBM] * 4,
        out_specs=[VMEM] * len(shapes),
        scratch_shapes=[
            pltpu.VMEM((z.spec, width), jnp.float32),
            pltpu.VMEM((4, LANES, LANES), jnp.float32),
            pltpu.VMEM(embed.shape, embed.dtype),
            pltpu.VMEM(filters.shape, filters.dtype),
            pltpu.VMEM(w_up.shape, w_up.dtype),
            pltpu.VMEM(w_energy.shape, w_energy.dtype),
            pltpu.SemaphoreType.DMA((4,)),
        ] + [pltpu.VMEM((z.rad * z.slots, most * LANES), jnp.bfloat16)] * by,
        compiler_params=pltpu.CompilerParams(vmem_limit_bytes=12 * 1024 * 1024),
        cost_estimate=pl.CostEstimate(flops=flops, bytes_accessed=1 << 20, transcendentals=0),
    )(near, *in_hbm(embed, filters, w_up, w_energy))


def far_layer(z, region, *near):
    width = near[0].shape[1]
    cells, anchors = z.block[0] * z.block[1], z.nax * z.nay
    columns = z.nx * z.ny * z.groups
    return pl.pallas_call(
        functools.partial(far_kernel, z),
        out_shape=(
            jax.ShapeDtypeStruct(z.block + (1, z.slots), jnp.float32),
            jax.ShapeDtypeStruct(z.block + (1, 3 * z.slots), jnp.float32),
            jax.ShapeDtypeStruct((z.groups,) + z.block + (1, 3 * z.slots), jnp.float32),
        ),
        in_specs=[VMEM] * (1 + len(near)),
        out_specs=[VMEM] * 3,
        scratch_shapes=[
            pltpu.VMEM((z.nx * 2 * HALO * z.groups, z.spec, LANES), jnp.bfloat16),
            pltpu.VMEM((z.nax * 2, 4, z.slots, LANES), jnp.float32),
            pltpu.VMEM((anchors, len(z.offsets), 2, z.slots, LANES), jnp.float32),
            pltpu.VMEM((4, LANES, LANES), jnp.float32),
            pltpu.VMEM((anchors, z.rad * z.slots, 2 * z.spec), jnp.bfloat16),
            pltpu.VMEM((anchors, 2 * z.slots, z.rad * z.spec), jnp.bfloat16),
            pltpu.VMEM((anchors, z.slots, width), jnp.bfloat16),
            pltpu.VMEM((columns, 3, 8, LANES), jnp.float32),
            pltpu.VMEM((cells, 3, z.slots, LANES), jnp.float32),
        ] + [pltpu.VMEM((z.rad * z.slots, len(z.offsets) * LANES), jnp.bfloat16)] * z.nay,
        compiler_params=pltpu.CompilerParams(vmem_limit_bytes=FAR_VMEM),
    )(region, *near)


def on_device(positions, species, counts, embed, filters, w_up, w_energy):
    bx, by = positions.shape[:2]
    slots = species.shape[-1]
    width = embed.shape[1]
    depth = lax.axis_size("gz")
    merged = depth * positions.shape[2] == 2
    spec = -(-embed.shape[0] // LANES) * LANES
    z = Cells((bx, by), merged, filters.shape[1] // width, spec, slots)
    block = pack(positions, species, counts.reshape(bx, by))
    upward = [(i, (i + 1) % depth) for i in range(depth)]
    downward = [(b, a) for a, b in upward]
    low = lax.ppermute(block, "gz", upward)
    if merged:
        block = jnp.concatenate([block, low], axis=3)
    else:
        high = lax.ppermute(block, "gz", downward)
        empty = jnp.full_like(block, -1.0)
        block = jnp.concatenate(
            [jnp.concatenate([block, low], axis=3), jnp.concatenate([high, empty], axis=3)], axis=2
        )
    block = exchange(block, "gx", 0, HALO)
    near = near_layer(z, block, embed, filters, w_up, w_energy.reshape(1, width))
    region = exchange(block, "gy", 1, HALO)
    energies, own, other = far_layer(z, region, *near)

    forces = own + lax.ppermute(other[0], "gz", downward)
    if not merged:
        forces = forces + lax.ppermute(other[1], "gz", upward)
    return energies, forces


def solution(mesh):
    in_specs = (
        P("gx", "gy", "gz", None),
        P("gx", "gy", "gz", None),
        P("gx", "gy", "gz"),
        P(),
        P(),
        P(),
        P(),
    )
    out_specs = (P("gx", "gy", "gz", None), P("gx", "gy", "gz", None))
    return jax.shard_map(
        on_device, mesh=mesh, in_specs=in_specs, out_specs=out_specs, check_vma=False
    )
```

time: 227 us -> 32.1 us (0.14)
  local copies, waits for them, and re-layouts: 113 us -> 0 us
  other arithmetic: 48.3 us -> 0.84 us
  matrix products: 24.1 us -> 0 us
  Pallas kernels: 0 us -> 16.5 us
  starting transfers between devices: 22.6 us -> 8.45 us
  loops' own time: 10.7 us -> 0 us
    dynamic_slice x109 -> x0, local copies, waits for them, and re-layouts: 54.3 us -> none  [window(): lax.dynamic_slice(padded, starts, tuple(cell_shape) + padded.shape[3:])]
    reduce_sum x109 -> x0, other arithmetic: 39.2 us -> none  [the longest x27 19.6 us: force_step(): jnp.sum(radial_slope * (outward + inward), axis=-1)]
    dot_general x84 -> x0, matrix products: 24.1 us -> none  [the longest x27 9.91 us: message_step(): jnp.einsum('abcip,abcpd->abcid', weights, target_feat, preferred_element_...]
    pallas_call x0 -> x3, Pallas kernels: none -> 16.5 us  [the longest x1 12.3 us: far_layer(): pl.pallas_call(functools.partial(far_kernel, z), out_shape=(jax.ShapeDtyp...]
    ppermute x18 -> x6, starting transfers between devices: 22.6 us -> 8.45 us  [the longest x2 7.39 us: exchange(): from_far = lax.ppermute(up, axis, far)]
    mul x189 -> x0, local copies, waits for them, and re-layouts: 13.7 us -> none  [the longest x81 5.47 us: radial(): decaying = jnp.exp(-decay_rates * dist_sq[..., None])]
    another operation x2 -> x0, loops' own time: 10.7 us -> none  [the longest x1 5.51 us: on_device(): lax.fori_loop(0, 27, force_step, jnp.zeros(cell_shape + (3, slot_count),...]
    sub x108 -> x0, local copies, waits for them, and re-layouts: 8.95 us -> none  [geometry(): displace = target[..., :, None, :] - anchor[..., :, :, None] + shift_vec]
  transfers between devices with their start and end apart: 18 -> 6, of which waited for: 6 -> 5; matrix products, arithmetic and copies ran while one was open for 4% -> 0% of each run, Pallas kernels for 0% -> 11%
where the time goes in v3:
time: 32.1 us; the launch traced here: 31.9 us
  Pallas kernels  16.5 us (51%)
  starting transfers between devices  8.45 us (26%)
  waiting for transfers between devices  5.44 us (17%)
  other arithmetic  0.84 us (3%)
  between operations  0.66 us (2%)
    pallas_call x1, Pallas kernels, far_layer(): pl.pallas_call(functools.partial(far_kernel, z), out_shape=(jax.ShapeDtyp...  12.3 us
    ppermute x2, starting transfers between devices, exchange(): from_far = lax.ppermute(up, axis, far)  7.39 us
    pallas_call x1, Pallas kernels, near_layer(): pl.pallas_call(functools.partial(near_kernel, z), out_shape=[jax.ShapeDty...  3.48 us
    ppermute x2, waiting for transfers between devices, exchange(): from_near = lax.ppermute(down, axis, near)  2.35 us
    ppermute x1, waiting for transfers between devices, on_device(): forces = own + lax.ppermute(other[0], 'gz', downward)  1.16 us
    ppermute x2, waiting for transfers between devices, exchange(): from_far = lax.ppermute(up, axis, far)  1.1 us
    ppermute x1, waiting for transfers between devices, on_device(): low = lax.ppermute(block, 'gz', upward)  0.83 us
    pallas_call x1, Pallas kernels, pack(): pl.pallas_call(pack_kernel, out_shape=jax.ShapeDtypeStruct((bx, by, 4, sl...  0.8 us
  transfers between devices with their start and end apart: 6, of which 5 were waited for; matrix products, arithmetic and copies ran while one was open for 0% of the time, Pallas kernels for 11%

profile of v3, /device:TPU:0, one launch (start us, length us, event | category | flops | bytes accessed | tf_op | source)
XLA Modules:
  0.0 31.9 jit_solution(18211360843789936146)
XLA Ops:
  0.6 0.8 %shard_map.86 = f32[2,2,4,64]{3,2,1,0:T(4,128)S(1)} custom-call(s32[2,2]{1,0:T(2,128)} %bitcast.22, f32[2,2,1,192]{3,2,1,0:T(1,128)} %positions_hbm.1, s32[2,2,1,64]{3,2,1,0:T(1,128)} %species_hbm.1), custom_call_target="tpu_custom_call" | custom-call | tf_op jit(solution)/shard_map/pallas_call | solution.py:389
  1.4 0.5 %collective-permute-start = (f32[2,2,4,64]{3,2,1,0:T(4,128)S(1)}, f32[2,2,4,64]{3,2,1,0:T(4,128)S(1)}, u32[]{:S(2)}, u32[]{:S(2)}) collective-permute-start(f32[2,2,4,64]{3,2,1,0:T(4,128)S(1)} %shard_map.86), channel_id=1, source_target_pairs={{0,1},{1,0},{2,3},{3,2},{4,5},{5,4},{6,7},{7,6},{8,9},{9,8},{10,11... | collective-permute-start | bytes 12296 | tf_op jit(solution)/shard_map/ppermute | solution.py:476
  2.0 0.8 %collective-permute-done = f32[2,2,4,64]{3,2,1,0:T(4,128)S(1)} collective-permute-done((f32[2,2,4,64]{3,2,1,0:T(4,128)S(1)}, f32[2,2,4,64]{3,2,1,0:T(4,128)S(1)}, u32[]{:S(2)}, u32[]{:S(2)}) %collective-permute-start) | collective-permute-done | bytes 4128 | tf_op jit(solution)/shard_map/ppermute | solution.py:476
  2.8 0.1 pad_maximum_fusion.2
  2.9 3.8 %collective-permute-start.2 = (f32[2,2,4,128]{3,2,1,0:T(4,128)S(1)}, f32[2,2,4,128]{3,2,1,0:T(4,128)S(1)}, u32[]{:S(2)}, u32[]{:S(2)}) collective-permute-start(f32[2,2,4,128]{3,2,1,0:T(4,128)S(1)} %pad_maximum_fusion.2), channel_id=1, source_target_pairs={{0,24},{8,16},{16,8},{24,0},{1,25},{9,17},{17,9},{25,1},{2,26},{10... | collective-permute-start | bytes 24584 | tf_op jit(solution)/shard_map/ppermute | solution.py:32
  6.6 0.5 %collective-permute-start.1 = (f32[2,2,4,128]{3,2,1,0:T(4,128)S(1)}, f32[2,2,4,128]{3,2,1,0:T(4,128)S(1)}, u32[]{:S(2)}, u32[]{:S(2)}) collective-permute-start(f32[2,2,4,128]{3,2,1,0:T(4,128)S(1)} %pad_maximum_fusion.2), channel_id=1, source_target_pairs={{0,8},{8,0},{16,24},{24,16},{1,9},{9,1},{17,25},{25,17},{2,10},{10... | collective-permute-start | bytes 24584 | tf_op jit(solution)/shard_map/ppermute | solution.py:33
  7.2 1.1 %collective-permute-done.2 = f32[2,2,4,128]{3,2,1,0:T(4,128)S(1)} collective-permute-done((f32[2,2,4,128]{3,2,1,0:T(4,128)S(1)}, f32[2,2,4,128]{3,2,1,0:T(4,128)S(1)}, u32[]{:S(2)}, u32[]{:S(2)}) %collective-permute-start.2) | collective-permute-done | bytes 8224 | tf_op jit(solution)/shard_map/ppermute | solution.py:32
  8.3 2.0 %collective-permute-done.1 = f32[2,2,4,128]{3,2,1,0:T(4,128)S(1)} collective-permute-done((f32[2,2,4,128]{3,2,1,0:T(4,128)S(1)}, f32[2,2,4,128]{3,2,1,0:T(4,128)S(1)}, u32[]{:S(2)}, u32[]{:S(2)}) %collective-permute-start.1) | collective-permute-done | bytes 8224 | tf_op jit(solution)/shard_map/ppermute | solution.py:33
  10.3 0.1 pad_maximum_fusion.1.near
  10.4 3.6 %collective-permute-start.4 = (f32[6,2,4,128]{3,2,1,0:T(4,128)S(1)}, f32[6,2,4,128]{3,2,1,0:T(4,128)S(1)}, u32[]{:S(2)}, u32[]{:S(2)}) collective-permute-start(f32[6,2,4,128]{3,2,1,0:T(4,128)S(1)} %pad_maximum_fusion.1.near), channel_id=1, source_target_pairs={{0,6},{2,4},{4,2},{6,0},{1,7},{3,5},{5,3},{7,1},{8,14},{10,12},{12... | collective-permute-start | bytes 73736 | tf_op jit(solution)/shard_map/ppermute | solution.py:32
  14.0 0.0 collective-permute-start.3
  14.0 3.5 %shard_map.87 = (bf16[512,128]{1,0:T(8,128)(2,1)S(1)}, f32[8,128]{1,0:T(8,128)S(1)}, f32[8,128]{1,0:T(8,128)S(1)}, bf16[12,128,128]{2,1,0:T(8,128)(2,1)S(1)}, f3...) custom-call(f32[6,2,4,128]{3,2,1,0:T(4,128)S(1)} %pad_maximum_fusion.1.near, ...), custom_call_target="tpu_custom_call" | custom-call | flops 402653184 | bytes 1048576 | tf_op jit(solution)/shard_map/pallas_call | solution.py:418
  17.5 0.0 collective-permute-done.4
  17.5 0.3 %collective-permute-done.3 = f32[6,2,4,128]{3,2,1,0:T(4,128)S(1)} collective-permute-done((f32[6,2,4,128]{3,2,1,0:T(4,128)S(1)}, f32[6,2,4,128]{3,2,1,0:T(4,128)S(1)}, u32[]{:S(2)}, u32[]{:S(2)}) %collective-permute-start.3) | collective-permute-done | bytes 24608 | tf_op jit(solution)/shard_map/ppermute | solution.py:33
  17.8 0.1 pad_maximum_fusion.region
  17.9 12.3 %shard_map.88 = (f32[2,2,1,64]{3,2,1,0:T(1,128)}, f32[2,2,1,192]{3,2,1,0:T(1,128)S(1)}, f32[1,2,2,1,192]{4,3,2,1,0:T(1,128)S(1)}) custom-call(f32[6,6,4,128]{3,2,1,0:T(4,128)S(1)} %pad_maximum_fusion.region, bf16[512,128]{1,0:T(8,128)(2,1)S(1)} %get-tuple-element.12.table, f32[8,128]{1,0:T(8,128)S(1)} %get-tuple-element.13.readout_ref, ...), custom_call_target="tpu_custom_call" | custom-call | tf_op jit(solution)/shard_map/pallas_call | solution.py:441
  30.2 0.0 collective-permute-start.5
  30.2 1.2 %collective-permute-done.5 = f32[2,2,1,192]{3,2,1,0:T(1,128)S(1)} collective-permute-done((f32[2,2,1,192]{3,2,1,0:T(1,128)S(1)}, f32[2,2,1,192]{3,2,1,0:T(1,128)S(1)}, u32[]{:S(2)}, u32[]{:S(2)}) %collective-permute-start.5) | collective-permute-done | bytes 3104 | tf_op jit(solution)/shard_map/ppermute | solution.py:490
  31.3 0.6 %add.12 = f32[2,2,1,192]{3,2,1,0:T(1,128)} add(f32[2,2,1,192]{3,2,1,0:T(1,128)S(1)} %get-tuple-element.20, f32[2,2,1,192]{3,2,1,0:T(1,128)S(1)} %collective-permute-done.5) | non-fusion elementwise | flops 768 | bytes 9216 | tf_op jit(solution)/shard_map/add | solution.py:490
  (2 shorter events, 0.0 us)
Async XLA Ops:
  1.4 1.3 %collective-permute-start = (f32[2,2,4,64]{3,2,1,0:T(4,128)S(1)}, f32[2,2,4,64]{3,2,1,0:T(4,128)S(1)}, u32[]{:S(2)}, u32[]{:S(2)}) collective-permute-start(f32[2,2,4,64]{3,2,1,0:T(4,128)S(1)} %shard_map.86), channel_id=1, source_target_pairs={{0,1},{1,0},{2,3},{3,2},{4,5},{5,4},{6,7},{7,6},{8,9},{9,8},{10,11... | collective-permute-start | bytes 12296 | tf_op jit(solution)/shard_map/ppermute | solution.py:476
  2.9 5.4 %collective-permute-start.2 = (f32[2,2,4,128]{3,2,1,0:T(4,128)S(1)}, f32[2,2,4,128]{3,2,1,0:T(4,128)S(1)}, u32[]{:S(2)}, u32[]{:S(2)}) collective-permute-start(f32[2,2,4,128]{3,2,1,0:T(4,128)S(1)} %pad_maximum_fusion.2), channel_id=1, source_target_pairs={{0,24},{8,16},{16,8},{24,0},{1,25},{9,17},{17,9},{25,1},{2,26},{10... | collective-permute-start | bytes 24584 | tf_op jit(solution)/shard_map/ppermute | solution.py:32
  6.6 3.7 %collective-permute-start.1 = (f32[2,2,4,128]{3,2,1,0:T(4,128)S(1)}, f32[2,2,4,128]{3,2,1,0:T(4,128)S(1)}, u32[]{:S(2)}, u32[]{:S(2)}) collective-permute-start(f32[2,2,4,128]{3,2,1,0:T(4,128)S(1)} %pad_maximum_fusion.2), channel_id=1, source_target_pairs={{0,8},{8,0},{16,24},{24,16},{1,9},{9,1},{17,25},{25,17},{2,10},{10... | collective-permute-start | bytes 24584 | tf_op jit(solution)/shard_map/ppermute | solution.py:33
  10.4 7.1 %collective-permute-start.4 = (f32[6,2,4,128]{3,2,1,0:T(4,128)S(1)}, f32[6,2,4,128]{3,2,1,0:T(4,128)S(1)}, u32[]{:S(2)}, u32[]{:S(2)}) collective-permute-start(f32[6,2,4,128]{3,2,1,0:T(4,128)S(1)} %pad_maximum_fusion.1.near), channel_id=1, source_target_pairs={{0,6},{2,4},{4,2},{6,0},{1,7},{3,5},{5,3},{7,1},{8,14},{10,12},{12... | collective-permute-start | bytes 73736 | tf_op jit(solution)/shard_map/ppermute | solution.py:32
  14.0 3.8 %collective-permute-start.3 = (f32[6,2,4,128]{3,2,1,0:T(4,128)S(1)}, f32[6,2,4,128]{3,2,1,0:T(4,128)S(1)}, u32[]{:S(2)}, u32[]{:S(2)}) collective-permute-start(f32[6,2,4,128]{3,2,1,0:T(4,128)S(1)} %pad_maximum_fusion.1.near), channel_id=1, source_target_pairs={{0,2},{2,0},{4,6},{6,4},{1,3},{3,1},{5,7},{7,5},{8,10},{10,8},{12,... | collective-permute-start | bytes 73736 | tf_op jit(solution)/shard_map/ppermute | solution.py:33
  30.2 1.2 %collective-permute-start.5 = (f32[2,2,1,192]{3,2,1,0:T(1,128)S(1)}, f32[2,2,1,192]{3,2,1,0:T(1,128)S(1)}, u32[]{:S(2)}, u32[]{:S(2)}) collective-permute-start(f32[2,2,1,192]{3,2,1,0:T(1,128)S(1)} %bitcast.11), channel_id=1, source_target_pairs={{1,0},{0,1},{3,2},{2,3},{5,4},{4,5},{7,6},{6,7},{9,8},{8,9},{11,10... | collective-permute-start | bytes 9224 | tf_op jit(solution)/shard_map/ppermute | solution.py:490

commit v4 on v3

--- a/solution.py
+++ b/solution.py
@@ -12,7 +12,8 @@
 FAR_VMEM = 36 * 1024 * 1024
 LANES = 128
 STEP = 16
-WIDE = 2
+WIDE = 4
+BATCH = 4
 LOG2E = 1.4426950408889634
 NT = (((1,), (1,)), ((), ()))
 NN = (((1,), (0,)), ((), ()))
@@ -115,8 +116,7 @@
         ez = jnp.abs(dz) - shift if z.merged else dz + shift
         s = ex * ex + ey * ey + ez * ez
         f = jnp.maximum(1.0 - s, 0.0)
-        power = s * (-0.5 * LOG2E)
-        e = jnp.exp2(power)
+        e = jnp.exp2(s * (-0.5 * LOG2E))
         keep[0, c, :] = f
         keep[1, c, :] = e
         f = f * f
@@ -125,10 +125,15 @@
             lane = lax.broadcasted_iota(jnp.int32, (STEP, LANES), 1)
             f = jnp.where(row == lane, 0.0, f)
         for k in range(z.rad):
-            if k:
-                power = power * 3.0
-                e = jnp.exp2(power)
-            buffer[k * z.slots + c.start:k * z.slots + c.stop, lanes] = (e * f).astype(jnp.bfloat16)
+            if k == 0:
+                w = e * f
+                e = e * e
+            elif k == 1:
+                w = w * e
+            else:
+                e = e * e * e
+                w = w * e
+            buffer[k * z.slots + c.start:k * z.slots + c.stop, lanes] = w.astype(jnp.bfloat16)
 
 
 def pack_kernel(counts_hbm, positions_hbm, species_hbm, out, counts, positions, species, arrived):
@@ -252,35 +257,32 @@
                 term = dot(buffers[ay][:, 0:len(some) * LANES], jnp.concatenate(hots, axis=1), NT)
                 total = term if total is None else total + term
             for k in range(rad):
-                high, low = split(total[k * slots:(k + 1) * slots])
-                mixed[a, 0:slots, k * spec:(k + 1) * spec] = high
-                mixed[a, slots:, k * spec:(k + 1) * spec] = low
+                mixed[a, :, k * spec:(k + 1) * spec] = total[k * slots:(k + 1) * slots].astype(bf)
         return carry
 
     lax.fori_loop(0, z.nax, message_at, 0)
 
-    def adjoint_at(ax, carry):
-        group = [ax * z.nay + ay for ay in range(z.nay)]
-        halves = dot(jnp.concatenate([mixed[a] for a in group], axis=0), table[...], NN)
+    def adjoint_of(group):
+        cells = [ax * z.nay + ay for ax, ay in group]
+        messages = dot(jnp.concatenate([mixed[a] for a in cells], axis=0), table[...], NN)
         adjoints = []
-        for ay, a in enumerate(group):
-            at = 2 * slots * ay
-            message = MSG_SCALE * (halves[at:at + slots] + halves[at + slots:at + 2 * slots])
+        for i, (a, spot) in enumerate(zip(cells, group)):
+            message = MSG_SCALE * messages[i * slots:(i + 1) * slots]
             sigmoid = 1.0 / (1.0 + jnp.exp(-message))
             act[a] = (message * sigmoid).astype(bf)
             slope = sigmoid * (1.0 + message * (1.0 - sigmoid)) * readout[0:1]
-            adjoints.append(jnp.where(anchor_at(ax, ay)[3] >= 0.0, slope, 0.0).astype(bf))
+            adjoints.append(jnp.where(anchor_at(*spot)[3] >= 0.0, slope, 0.0).astype(bf))
         turned = dot(jnp.concatenate(adjoints, axis=0), table[...], NT)
-        for ay, a in enumerate(group):
+        for i, a in enumerate(cells):
             for r, c in enumerate(z.rows):
-                high, low = split(turned[slots * ay + c.start:slots * ay + c.stop])
+                high, low = split(turned[slots * i + c.start:slots * i + c.stop])
                 for k in range(rad):
                     at = slice((r * rad + k) * STEP, (r * rad + k + 1) * STEP)
                     adj_table[a, at, 0:spec] = high[:, k * spec:(k + 1) * spec]
                     adj_table[a, at, spec:] = low[:, k * spec:(k + 1) * spec]
-        return carry
-
-    lax.fori_loop(0, z.nax, adjoint_at, 0, unroll=True)
+
+    for first in range(0, z.nax, BATCH):
+        adjoint_of([(ax, ay) for ax in range(first, min(first + BATCH, z.nax)) for ay in range(z.nay)])
 
     def pairs(ax, ay, n, gains, r):
         c = z.rows[r]
@@ -315,10 +317,11 @@
             hots = jnp.concatenate([onehot_at(*spot) for spot in spots], axis=1)
             hots = jnp.concatenate([hots, hots], axis=0)
             totals = [[None] * 3 for _ in part]
+            gains = dot(adj_table[a], hots, NN)
             for r in range(len(z.rows)):
-                gains = dot(adj_table[a, r * rad * STEP:(r + 1) * rad * STEP, :], hots, NN)
+                some_gains = gains[r * rad * STEP:(r + 1) * rad * STEP]
                 for i, n in enumerate(part):
-                    p, displace = pairs(ax, ay, n, gains[:, i * LANES:(i + 1) * LANES], r)
+                    p, displace = pairs(ax, ay, n, some_gains[:, i * LANES:(i + 1) * LANES], r)
                     for q in range(3):
                         term = p * displace[q]
                         if sums is not None:
@@ -453,7 +456,7 @@
             pltpu.VMEM((anchors, len(z.offsets), 2, z.slots, LANES), jnp.float32),
             pltpu.VMEM((4, LANES, LANES), jnp.float32),
             pltpu.VMEM((anchors, z.rad * z.slots, 2 * z.spec), jnp.bfloat16),
-            pltpu.VMEM((anchors, 2 * z.slots, z.rad * z.spec), jnp.bfloat16),
+            pltpu.VMEM((anchors, z.slots, z.rad * z.spec), jnp.bfloat16),
             pltpu.VMEM((anchors, z.slots, width), jnp.bfloat16),
             pltpu.VMEM((columns, 3, 8, LANES), jnp.float32),
             pltpu.VMEM((cells, 3, z.slots, LANES), jnp.float32),

time: 32.1 us -> 30.1 us (0.938)
  Pallas kernels: 16.5 us -> 14.4 us
    pallas_call x1, Pallas kernels: 12.3 us -> 10.3 us  [far_layer(): pl.pallas_call(functools.partial(far_kernel, z), out_shape=(jax.ShapeDtyp...]
where the time goes in v4:
time: 30.1 us; the launch traced here: 29.9 us
  Pallas kernels  14.4 us (48%)
  starting transfers between devices  8.45 us (28%)
  waiting for transfers between devices  5.54 us (18%)
  other arithmetic  0.84 us (3%)
  between operations  0.66 us (2%)
    pallas_call x1, Pallas kernels, far_layer(): pl.pallas_call(functools.partial(far_kernel, z), out_shape=(jax.ShapeDtyp...  10.3 us
    ppermute x2, starting transfers between devices, exchange(): from_far = lax.ppermute(up, axis, far)  7.39 us
    pallas_call x1, Pallas kernels, near_layer(): pl.pallas_call(functools.partial(near_kernel, z), out_shape=[jax.ShapeDty...  3.38 us
    ppermute x2, waiting for transfers between devices, exchange(): from_near = lax.ppermute(down, axis, near)  2.45 us
    ppermute x1, waiting for transfers between devices, on_device(): forces = own + lax.ppermute(other[0], 'gz', downward)  1.16 us
    ppermute x2, waiting for transfers between devices, exchange(): from_far = lax.ppermute(up, axis, far)  1.1 us
    ppermute x1, waiting for transfers between devices, on_device(): low = lax.ppermute(block, 'gz', upward)  0.83 us
    pallas_call x1, Pallas kernels, pack(): pl.pallas_call(pack_kernel, out_shape=jax.ShapeDtypeStruct((bx, by, 4, sl...  0.8 us
  transfers between devices with their start and end apart: 6, of which 5 were waited for; matrix products, arithmetic and copies ran while one was open for 0% of the time, Pallas kernels for 11%

profile of v4, /device:TPU:0, one launch (start us, length us, event | category | flops | bytes accessed | tf_op | source)
XLA Modules:
  0.0 29.9 jit_solution(8601886503855415132)
XLA Ops:
  0.6 0.8 %shard_map.86 = f32[2,2,4,64]{3,2,1,0:T(4,128)S(1)} custom-call(s32[2,2]{1,0:T(2,128)} %bitcast.22, f32[2,2,1,192]{3,2,1,0:T(1,128)} %positions_hbm.1, s32[2,2,1,64]{3,2,1,0:T(1,128)} %species_hbm.1), custom_call_target="tpu_custom_call" | custom-call | tf_op jit(solution)/shard_map/pallas_call | solution.py:392
  1.4 0.5 %collective-permute-start = (f32[2,2,4,64]{3,2,1,0:T(4,128)S(1)}, f32[2,2,4,64]{3,2,1,0:T(4,128)S(1)}, u32[]{:S(2)}, u32[]{:S(2)}) collective-permute-start(f32[2,2,4,64]{3,2,1,0:T(4,128)S(1)} %shard_map.86), channel_id=1, source_target_pairs={{0,1},{1,0},{2,3},{3,2},{4,5},{5,4},{6,7},{7,6},{8,9},{9,8},{10,11... | collective-permute-start | bytes 12296 | tf_op jit(solution)/shard_map/ppermute | solution.py:479
  2.0 0.8 %collective-permute-done = f32[2,2,4,64]{3,2,1,0:T(4,128)S(1)} collective-permute-done((f32[2,2,4,64]{3,2,1,0:T(4,128)S(1)}, f32[2,2,4,64]{3,2,1,0:T(4,128)S(1)}, u32[]{:S(2)}, u32[]{:S(2)}) %collective-permute-start) | collective-permute-done | bytes 4128 | tf_op jit(solution)/shard_map/ppermute | solution.py:479
  2.8 0.1 pad_maximum_fusion.2
  2.9 3.8 %collective-permute-start.2 = (f32[2,2,4,128]{3,2,1,0:T(4,128)S(1)}, f32[2,2,4,128]{3,2,1,0:T(4,128)S(1)}, u32[]{:S(2)}, u32[]{:S(2)}) collective-permute-start(f32[2,2,4,128]{3,2,1,0:T(4,128)S(1)} %pad_maximum_fusion.2), channel_id=1, source_target_pairs={{0,24},{8,16},{16,8},{24,0},{1,25},{9,17},{17,9},{25,1},{2,26},{10... | collective-permute-start | bytes 24584 | tf_op jit(solution)/shard_map/ppermute | solution.py:33
  6.6 0.5 %collective-permute-start.1 = (f32[2,2,4,128]{3,2,1,0:T(4,128)S(1)}, f32[2,2,4,128]{3,2,1,0:T(4,128)S(1)}, u32[]{:S(2)}, u32[]{:S(2)}) collective-permute-start(f32[2,2,4,128]{3,2,1,0:T(4,128)S(1)} %pad_maximum_fusion.2), channel_id=1, source_target_pairs={{0,8},{8,0},{16,24},{24,16},{1,9},{9,1},{17,25},{25,17},{2,10},{10... | collective-permute-start | bytes 24584 | tf_op jit(solution)/shard_map/ppermute | solution.py:34
  7.2 1.1 %collective-permute-done.2 = f32[2,2,4,128]{3,2,1,0:T(4,128)S(1)} collective-permute-done((f32[2,2,4,128]{3,2,1,0:T(4,128)S(1)}, f32[2,2,4,128]{3,2,1,0:T(4,128)S(1)}, u32[]{:S(2)}, u32[]{:S(2)}) %collective-permute-start.2) | collective-permute-done | bytes 8224 | tf_op jit(solution)/shard_map/ppermute | solution.py:33
  8.3 2.0 %collective-permute-done.1 = f32[2,2,4,128]{3,2,1,0:T(4,128)S(1)} collective-permute-done((f32[2,2,4,128]{3,2,1,0:T(4,128)S(1)}, f32[2,2,4,128]{3,2,1,0:T(4,128)S(1)}, u32[]{:S(2)}, u32[]{:S(2)}) %collective-permute-start.1) | collective-permute-done | bytes 8224 | tf_op jit(solution)/shard_map/ppermute | solution.py:34
  10.3 0.1 pad_maximum_fusion.1.near
  10.4 3.6 %collective-permute-start.4 = (f32[6,2,4,128]{3,2,1,0:T(4,128)S(1)}, f32[6,2,4,128]{3,2,1,0:T(4,128)S(1)}, u32[]{:S(2)}, u32[]{:S(2)}) collective-permute-start(f32[6,2,4,128]{3,2,1,0:T(4,128)S(1)} %pad_maximum_fusion.1.near), channel_id=1, source_target_pairs={{0,6},{2,4},{4,2},{6,0},{1,7},{3,5},{5,3},{7,1},{8,14},{10,12},{12... | collective-permute-start | bytes 73736 | tf_op jit(solution)/shard_map/ppermute | solution.py:33
  14.0 0.0 collective-permute-start.3
  14.0 3.4 %shard_map.87 = (bf16[512,128]{1,0:T(8,128)(2,1)S(1)}, f32[8,128]{1,0:T(8,128)S(1)}, f32[8,128]{1,0:T(8,128)S(1)}, bf16[12,128,128]{2,1,0:T(8,128)(2,1)S(1)}, f3...) custom-call(f32[6,2,4,128]{3,2,1,0:T(4,128)S(1)} %pad_maximum_fusion.1.near, ...), custom_call_target="tpu_custom_call" | custom-call | flops 402653184 | bytes 1048576 | tf_op jit(solution)/shard_map/pallas_call | solution.py:421
  17.4 0.0 collective-permute-done.4
  17.4 0.4 %collective-permute-done.3 = f32[6,2,4,128]{3,2,1,0:T(4,128)S(1)} collective-permute-done((f32[6,2,4,128]{3,2,1,0:T(4,128)S(1)}, f32[6,2,4,128]{3,2,1,0:T(4,128)S(1)}, u32[]{:S(2)}, u32[]{:S(2)}) %collective-permute-start.3) | collective-permute-done | bytes 24608 | tf_op jit(solution)/shard_map/ppermute | solution.py:34
  17.8 0.1 pad_maximum_fusion.region
  17.9 10.3 %shard_map.88 = (f32[2,2,1,64]{3,2,1,0:T(1,128)}, f32[2,2,1,192]{3,2,1,0:T(1,128)S(1)}, f32[1,2,2,1,192]{4,3,2,1,0:T(1,128)S(1)}) custom-call(f32[6,6,4,128]{3,2,1,0:T(4,128)S(1)} %pad_maximum_fusion.region, bf16[512,128]{1,0:T(8,128)(2,1)S(1)} %get-tuple-element.12.table, f32[8,128]{1,0:T(8,128)S(1)} %get-tuple-element.13.readout_ref, ...), custom_call_target="tpu_custom_call" | custom-call | tf_op jit(solution)/shard_map/pallas_call | solution.py:444
  28.2 0.0 collective-permute-start.5
  28.2 1.2 %collective-permute-done.5 = f32[2,2,1,192]{3,2,1,0:T(1,128)S(1)} collective-permute-done((f32[2,2,1,192]{3,2,1,0:T(1,128)S(1)}, f32[2,2,1,192]{3,2,1,0:T(1,128)S(1)}, u32[]{:S(2)}, u32[]{:S(2)}) %collective-permute-start.5) | collective-permute-done | bytes 3104 | tf_op jit(solution)/shard_map/ppermute | solution.py:493
  29.3 0.6 %add.12 = f32[2,2,1,192]{3,2,1,0:T(1,128)} add(f32[2,2,1,192]{3,2,1,0:T(1,128)S(1)} %get-tuple-element.20, f32[2,2,1,192]{3,2,1,0:T(1,128)S(1)} %collective-permute-done.5) | non-fusion elementwise | flops 768 | bytes 9216 | tf_op jit(solution)/shard_map/add | solution.py:493
  (2 shorter events, 0.0 us)
Async XLA Ops:
  1.4 1.3 %collective-permute-start = (f32[2,2,4,64]{3,2,1,0:T(4,128)S(1)}, f32[2,2,4,64]{3,2,1,0:T(4,128)S(1)}, u32[]{:S(2)}, u32[]{:S(2)}) collective-permute-start(f32[2,2,4,64]{3,2,1,0:T(4,128)S(1)} %shard_map.86), channel_id=1, source_target_pairs={{0,1},{1,0},{2,3},{3,2},{4,5},{5,4},{6,7},{7,6},{8,9},{9,8},{10,11... | collective-permute-start | bytes 12296 | tf_op jit(solution)/shard_map/ppermute | solution.py:479
  2.9 5.4 %collective-permute-start.2 = (f32[2,2,4,128]{3,2,1,0:T(4,128)S(1)}, f32[2,2,4,128]{3,2,1,0:T(4,128)S(1)}, u32[]{:S(2)}, u32[]{:S(2)}) collective-permute-start(f32[2,2,4,128]{3,2,1,0:T(4,128)S(1)} %pad_maximum_fusion.2), channel_id=1, source_target_pairs={{0,24},{8,16},{16,8},{24,0},{1,25},{9,17},{17,9},{25,1},{2,26},{10... | collective-permute-start | bytes 24584 | tf_op jit(solution)/shard_map/ppermute | solution.py:33
  6.6 3.7 %collective-permute-start.1 = (f32[2,2,4,128]{3,2,1,0:T(4,128)S(1)}, f32[2,2,4,128]{3,2,1,0:T(4,128)S(1)}, u32[]{:S(2)}, u32[]{:S(2)}) collective-permute-start(f32[2,2,4,128]{3,2,1,0:T(4,128)S(1)} %pad_maximum_fusion.2), channel_id=1, source_target_pairs={{0,8},{8,0},{16,24},{24,16},{1,9},{9,1},{17,25},{25,17},{2,10},{10... | collective-permute-start | bytes 24584 | tf_op jit(solution)/shard_map/ppermute | solution.py:34
  10.4 7.0 %collective-permute-start.4 = (f32[6,2,4,128]{3,2,1,0:T(4,128)S(1)}, f32[6,2,4,128]{3,2,1,0:T(4,128)S(1)}, u32[]{:S(2)}, u32[]{:S(2)}) collective-permute-start(f32[6,2,4,128]{3,2,1,0:T(4,128)S(1)} %pad_maximum_fusion.1.near), channel_id=1, source_target_pairs={{0,6},{2,4},{4,2},{6,0},{1,7},{3,5},{5,3},{7,1},{8,14},{10,12},{12... | collective-permute-start | bytes 73736 | tf_op jit(solution)/shard_map/ppermute | solution.py:33
  14.0 3.8 %collective-permute-start.3 = (f32[6,2,4,128]{3,2,1,0:T(4,128)S(1)}, f32[6,2,4,128]{3,2,1,0:T(4,128)S(1)}, u32[]{:S(2)}, u32[]{:S(2)}) collective-permute-start(f32[6,2,4,128]{3,2,1,0:T(4,128)S(1)} %pad_maximum_fusion.1.near), channel_id=1, source_target_pairs={{0,2},{2,0},{4,6},{6,4},{1,3},{3,1},{5,7},{7,5},{8,10},{10,8},{12,... | collective-permute-start | bytes 73736 | tf_op jit(solution)/shard_map/ppermute | solution.py:34
  28.2 1.2 %collective-permute-start.5 = (f32[2,2,1,192]{3,2,1,0:T(1,128)S(1)}, f32[2,2,1,192]{3,2,1,0:T(1,128)S(1)}, u32[]{:S(2)}, u32[]{:S(2)}) collective-permute-start(f32[2,2,1,192]{3,2,1,0:T(1,128)S(1)} %bitcast.11), channel_id=1, source_target_pairs={{1,0},{0,1},{3,2},{2,3},{5,4},{4,5},{7,6},{6,7},{9,8},{8,9},{11,10... | collective-permute-start | bytes 9224 | tf_op jit(solution)/shard_map/ppermute | solution.py:493

commit v5 on v4

--- a/solution.py
+++ b/solution.py
@@ -9,11 +9,13 @@
 
 MSG_SCALE = 0.1
 HALO = 2
-FAR_VMEM = 36 * 1024 * 1024
+FAR_VMEM = 30 * 1024 * 1024
+OWN_VMEM = 8 * 1024 * 1024
 LANES = 128
 STEP = 16
 WIDE = 4
 BATCH = 4
+FORCE_SCALE = 4.0 * MSG_SCALE
 LOG2E = 1.4426950408889634
 NT = (((1,), (1,)), ((), ()))
 NN = (((1,), (0,)), ((), ()))
@@ -72,6 +74,11 @@
 
     def inner(self, ay):
         return 1 <= ay <= self.block[1]
+
+    def cell(self, ax, ay):
+        if 1 <= ax <= self.block[0] and self.inner(ay):
+            return (ax - 1) * self.block[1] + ay - 1
+        return None
 
     def split_offsets(self, ay):
         near = [n for n, (_, dy, _) in enumerate(self.offsets) if self.inner(ay) and self.inner(ay + dy)]
@@ -204,16 +211,95 @@
     emb_energy[...] = dot(energy_row, emb, NT, lax.Precision.HIGHEST)
 
 
+class Store:
+    def __init__(self, z, onehot_near, onehot_far, anchors_near, anchors_far, kept_near, kept_own, kept_far):
+        self.z = z
+        self.onehots = (onehot_near, onehot_far)
+        self.anchors = (anchors_near, anchors_far)
+        self.kept = (kept_near, kept_own, kept_far)
+        self.outer = [y for y in range(z.ny) if not HALO <= y < HALO + z.block[1]]
+
+    def onehot(self, x, y, g):
+        z = self.z
+        if y in self.outer:
+            return self.onehots[1][(x * len(self.outer) + self.outer.index(y)) * z.groups + g]
+        return self.onehots[0][(x * z.block[1] + y - HALO) * z.groups + g]
+
+    def anchor(self, ax, ay):
+        if self.z.inner(ay):
+            return self.anchors[0].at[ax * self.z.block[1] + ay - 1]
+        return self.anchors[1].at[ax * 2 + (ay > 0)]
+
+    def radial(self, ax, ay, n):
+        if not self.z.inner(ay):
+            return self.kept[2].at[ax * 2 + (ay > 0), n]
+        near, far = self.z.split_offsets(ay)
+        if n in near:
+            return self.kept[0].at[ax * self.z.block[1] + ay - 1, near.index(n)]
+        return self.kept[1].at[ax * self.z.block[1] + ay - 1, far.index(n)]
+
+
+def pairs(z, store, region, ax, ay, n, gains, r):
+    c = z.rows[r]
+    dx, dy, g = z.offsets[n]
+    tx, ty, tz = target(region, ax + 1 + dx, ay + 1 + dy, z.offsets[n])
+    anchor, keep = store.anchor(ax, ay), store.radial(ax, ay, n)
+    ex = tx - anchor[0, c, :]
+    ey = ty - anchor[1, c, :]
+    ez = tz - anchor[2, c, :]
+    shift = z.z_shift(g)
+    ez = ez + jnp.where(ez > 0.0, -shift, shift) if z.merged else ez + shift
+    f = keep[0, c, :]
+    e = keep[1, c, :]
+    e2 = e * e
+    plain = None
+    for k in range(z.rad):
+        if k == 1:
+            e = e * e2
+        elif k > 1:
+            e2 = e2 * e2 * e2
+            e = e * e2
+        term = e * gains[k * STEP:(k + 1) * STEP]
+        scaled = (0.25 * 3.0 ** k) * term
+        plain, steep = (term, scaled) if plain is None else (plain + term, steep + scaled)
+    return f * (f * steep + plain), (ex, ey, ez)
+
+
+def blocks(z, store, region, adj_table, ax, ay, some, sums, back):
+    for first in range(0, len(some), WIDE):
+        part = some[first:first + WIDE]
+        spots = [(ax + 1 + z.offsets[n][0], ay + 1 + z.offsets[n][1], z.offsets[n][2]) for n in part]
+        hots = jnp.concatenate([store.onehot(*spot) for spot in spots], axis=1)
+        gains = dot(adj_table[...], jnp.concatenate([hots, hots], axis=0), NN)
+        totals = [[None] * 3 for _ in part]
+        for r in range(len(z.rows)):
+            some_gains = gains[r * z.rad * STEP:(r + 1) * z.rad * STEP]
+            for i, n in enumerate(part):
+                p, displace = pairs(z, store, region, ax, ay, n, some_gains[:, i * LANES:(i + 1) * LANES], r)
+                for q in range(3):
+                    term = p * displace[q]
+                    if sums is not None:
+                        sums[q][r] = term if sums[q][r] is None else sums[q][r] + term
+                    if back is not None:
+                        term = sum(term[j:j + 8] for j in range(8, STEP, 8)) + term[0:8]
+                        totals[i][q] = term if totals[i][q] is None else totals[i][q] + term
+        if back is not None:
+            for (x, y, g), total in zip(spots, totals):
+                for q in range(3):
+                    back[((x - HALO) * z.block[1] + y - HALO) * z.groups + g, q] += total[q]
+
+
 def far_kernel(
-    z, region, table, readout_ref, emb_energy_ref, onehot_near, anchors_near, sums_near, kept_near,
-    energies, own, other,
-    onehot_far, anchors_far, kept_far, stage, adj_table, mixed, act, back, mine, *buffers,
+    z, region, table, readout_ref, onehot_near, anchors_near, sums_near, kept_near,
+    other, part, mine, adj_own, act_own, onehot_far, kept_own,
+    anchors_far, kept_far, stage, adj_table, mixed, back, *buffers,
 ):
     by = z.block[1]
     bf = jnp.bfloat16
     slots, spec, rad = z.slots, z.spec, z.rad
     readout = readout_ref[...]
-    outer = [y for y in range(z.ny) if not HALO <= y < HALO + by]
+    store = Store(z, onehot_near, onehot_far, anchors_near, anchors_far, kept_near, kept_own, kept_far)
+    outer = store.outer
 
     for x in range(z.nx):
         for i, y in enumerate(outer):
@@ -222,22 +308,6 @@
     place_anchors(
         z, stage, [(region, ax + 1, y) for ax in range(z.nax) for y in (1, z.ny - HALO)], anchors_far
     )
-
-    def onehot_at(x, y, g):
-        if y in outer:
-            return onehot_far[(x * len(outer) + outer.index(y)) * z.groups + g]
-        return onehot_near[(x * by + y - HALO) * z.groups + g]
-
-    def anchor_at(ax, ay):
-        if z.inner(ay):
-            return anchors_near.at[ax * by + ay - 1]
-        return anchors_far.at[ax * 2 + (ay > 0)]
-
-    def kept_at(ax, ay, n):
-        near, _ = z.split_offsets(ay)
-        if n in near:
-            return kept_near.at[ax * by + ay - 1, near.index(n)]
-        return kept_far.at[ax * z.nay + ay, n]
 
     def message_at(ax, carry):
         for ay in range(z.nay):
@@ -248,10 +318,10 @@
                 dx, dy, g = z.offsets[n]
                 x, y = ax + 1 + dx, ay + 1 + dy
                 weigh(
-                    z, target(region, x, y, z.offsets[n]), anchor_at(ax, ay), z.offsets[n], buffers[ay],
-                    slice(i * LANES, (i + 1) * LANES), kept_at(ax, ay, n),
+                    z, target(region, x, y, z.offsets[n]), store.anchor(ax, ay), z.offsets[n], buffers[ay],
+                    slice(i * LANES, (i + 1) * LANES), store.radial(ax, ay, n),
                 )
-                hots.append(onehot_at(x, y, g))
+                hots.append(store.onehot(x, y, g))
             total = sums_near[ax * by + ay - 1] if z.inner(ay) else None
             if some:
                 term = dot(buffers[ay][:, 0:len(some) * LANES], jnp.concatenate(hots, axis=1), NT)
@@ -262,6 +332,11 @@
 
     lax.fori_loop(0, z.nax, message_at, 0)
 
+    def adj_at(ax, ay):
+        if 0 < ax < z.nax - 1 and z.inner(ay):
+            return adj_own.at[(ax - 1) * by + ay - 1]
+        return adj_table.at[ax * z.nay + ay]
+
     def adjoint_of(group):
         cells = [ax * z.nay + ay for ax, ay in group]
         messages = dot(jnp.concatenate([mixed[a] for a in cells], axis=0), table[...], NN)
@@ -269,110 +344,78 @@
         for i, (a, spot) in enumerate(zip(cells, group)):
             message = MSG_SCALE * messages[i * slots:(i + 1) * slots]
             sigmoid = 1.0 / (1.0 + jnp.exp(-message))
-            act[a] = (message * sigmoid).astype(bf)
+            ax, ay = spot
+            inside = 0 < ax < z.nax - 1 and z.inner(ay)
+            if inside:
+                act_own[(ax - 1) * by + ay - 1] = (message * sigmoid).astype(bf)
             slope = sigmoid * (1.0 + message * (1.0 - sigmoid)) * readout[0:1]
-            adjoints.append(jnp.where(anchor_at(*spot)[3] >= 0.0, slope, 0.0).astype(bf))
+            adjoints.append(jnp.where(store.anchor(*spot)[3] >= 0.0, slope, 0.0).astype(bf))
         turned = dot(jnp.concatenate(adjoints, axis=0), table[...], NT)
-        for i, a in enumerate(cells):
+        for i, spot in enumerate(group):
+            out = adj_at(*spot)
             for r, c in enumerate(z.rows):
                 high, low = split(turned[slots * i + c.start:slots * i + c.stop])
                 for k in range(rad):
                     at = slice((r * rad + k) * STEP, (r * rad + k + 1) * STEP)
-                    adj_table[a, at, 0:spec] = high[:, k * spec:(k + 1) * spec]
-                    adj_table[a, at, spec:] = low[:, k * spec:(k + 1) * spec]
+                    out[at, 0:spec] = high[:, k * spec:(k + 1) * spec]
+                    out[at, spec:] = low[:, k * spec:(k + 1) * spec]
 
     for first in range(0, z.nax, BATCH):
         adjoint_of([(ax, ay) for ax in range(first, min(first + BATCH, z.nax)) for ay in range(z.nay)])
 
-    def pairs(ax, ay, n, gains, r):
-        c = z.rows[r]
-        dx, dy, g = z.offsets[n]
-        tx, ty, tz = target(region, ax + 1 + dx, ay + 1 + dy, z.offsets[n])
-        anchor, keep = anchor_at(ax, ay), kept_at(ax, ay, n)
-        ex = tx - anchor[0, c, :]
-        ey = ty - anchor[1, c, :]
-        ez = tz - anchor[2, c, :]
-        shift = z.z_shift(g)
-        ez = ez + jnp.where(ez > 0.0, -shift, shift) if z.merged else ez + shift
-        f = keep[0, c, :]
-        e = keep[1, c, :]
-        e2 = e * e
-        plain = None
-        for k in range(rad):
-            if k == 1:
-                e = e * e2
-            elif k > 1:
-                e2 = e2 * e2 * e2
-                e = e * e2
-            term = e * gains[k * STEP:(k + 1) * STEP]
-            scaled = (0.25 * 3.0 ** k) * term
-            plain, steep = (term, scaled) if plain is None else (plain + term, steep + scaled)
-        return f * (f * steep + plain), (ex, ey, ez)
-
-    def blocks(ax, ay, some, sums):
-        a = ax * z.nay + ay
-        for first in range(0, len(some), WIDE):
-            part = some[first:first + WIDE]
-            spots = [(ax + 1 + z.offsets[n][0], ay + 1 + z.offsets[n][1], z.offsets[n][2]) for n in part]
-            hots = jnp.concatenate([onehot_at(*spot) for spot in spots], axis=1)
-            hots = jnp.concatenate([hots, hots], axis=0)
-            totals = [[None] * 3 for _ in part]
-            gains = dot(adj_table[a], hots, NN)
-            for r in range(len(z.rows)):
-                some_gains = gains[r * rad * STEP:(r + 1) * rad * STEP]
-                for i, n in enumerate(part):
-                    p, displace = pairs(ax, ay, n, some_gains[:, i * LANES:(i + 1) * LANES], r)
-                    for q in range(3):
-                        term = p * displace[q]
-                        if sums is not None:
-                            sums[q][r] = term if sums[q][r] is None else sums[q][r] + term
-                        term = sum(term[j:j + 8] for j in range(8, STEP, 8)) + term[0:8]
-                        totals[i][q] = term if totals[i][q] is None else totals[i][q] + term
-            for (x, y, g), total in zip(spots, totals):
-                for q in range(3):
-                    back[(x * z.ny + y) * z.groups + g, q] += total[q]
-
     back[...] = jnp.zeros_like(back)
-
-    def forces_at(ox, carry):
-        for oy in range(by):
-            sums = [[None] * len(z.rows) for _ in range(3)]
-            blocks(ox + 1, oy + 1, range(len(z.offsets)), sums)
-            for q in range(3):
-                for r, c in enumerate(z.rows):
-                    mine[ox * by + oy, q, c, :] = sums[q][r]
-        return carry
-
-    lax.fori_loop(0, z.block[0], forces_at, 0)
 
     for ax in range(z.nax):
         for ay in range(z.nay):
-            if 0 < ax < z.nax - 1 and z.inner(ay):
-                continue
-            blocks(ax, ay, [
-                n for n, (dx, dy, _) in enumerate(z.offsets) if 0 < ax + dx < z.nax - 1 and z.inner(ay + dy)
-            ], None)
-
-    scale = -4.0 * MSG_SCALE
-    cells = [(ox, oy) for ox in range(z.block[0]) for oy in range(by)]
+            o = z.cell(ax, ay)
+            some = [n for n, (dx, dy, _) in enumerate(z.offsets) if z.cell(ax + dx, ay + dy) is not None]
+            sums = None if o is None else [[None] * len(z.rows) for _ in range(3)]
+            blocks(z, store, region, adj_at(ax, ay), ax, ay, some, sums, back)
+            if o is not None:
+                for q in range(3):
+                    for r, c in enumerate(z.rows):
+                        mine[o, q, c, :] = sums[q][r]
+
+    for ox in range(z.block[0]):
+        for oy in range(by):
+            for g in range(z.groups):
+                start = slots if g == 0 else 0
+                for q in range(3):
+                    row = FORCE_SCALE * jnp.sum(back[(ox * by + oy) * z.groups + g, q], axis=0, keepdims=True)
+                    other[g, ox, oy, :, q * slots:(q + 1) * slots] = row[:, start:start + slots]
+                    if g == 0:
+                        part[ox, oy, :, q * slots:(q + 1) * slots] = row[:, 0:slots]
+
+
+def own_kernel(
+    z, region, readout, emb_energy, onehot_near, anchors_near, kept_near,
+    part, mine_part, adj_own, act_own, onehot_far, kept_own,
+    energies, own, mine,
+):
+    slots = z.slots
+    store = Store(z, onehot_near, onehot_far, anchors_near, None, kept_near, kept_own, None)
+    cells = [(ox, oy) for ox in range(z.block[0]) for oy in range(z.block[1])]
+    for o, (ox, oy) in enumerate(cells):
+        ax, ay = ox + 1, oy + 1
+        some = [n for n, (dx, dy, _) in enumerate(z.offsets) if z.cell(ax + dx, ay + dy) is None]
+        sums = [[mine_part[o, q, c, :] for c in z.rows] for q in range(3)]
+        blocks(z, store, region, adj_own.at[o], ax, ay, some, sums, None)
+        for q in range(3):
+            for r, c in enumerate(z.rows):
+                mine[o, q, c, :] = sums[q][r]
+
     high, low = split(mine[...].reshape(len(cells) * 3 * slots, LANES))
-    ones = jnp.ones((8, 2 * LANES), bf)
+    ones = jnp.ones((8, 2 * LANES), jnp.bfloat16)
     rows = dot(ones, jnp.concatenate([high, low], axis=1), NT)[0:1]
     for o, (ox, oy) in enumerate(cells):
-        column = ((ox + HALO) * z.ny + oy + HALO) * z.groups
-        sums = [jnp.sum(back[column, q], axis=0, keepdims=True)[:, 0:slots] for q in range(3)]
         for q in range(3):
             at = (o * 3 + q) * slots
-            own[ox, oy, :, q * slots:(q + 1) * slots] = scale * (rows[:, at:at + slots] - sums[q])
-        for g in range(z.groups):
-            start = slots if g == 0 else 0
-            for q in range(3):
-                row = jnp.sum(back[column + g, q], axis=0, keepdims=True)
-                other[g, ox, oy, :, q * slots:(q + 1) * slots] = -scale * row[:, start:start + slots]
-
-    hots = jnp.concatenate([onehot_at(ox + HALO, oy + HALO, 0)[:, 0:slots] for ox, oy in cells], axis=1)
-    acts = jnp.concatenate([act[(ox + 1) * z.nay + oy + 1] for ox, oy in cells], axis=0)
-    energy = dot(thirds(emb_energy_ref[...]), hots, NN) + dot(thirds(readout), acts, NT)
+            lanes = slice(q * slots, (q + 1) * slots)
+            own[ox, oy, :, lanes] = part[ox, oy, :, lanes] - FORCE_SCALE * rows[:, at:at + slots]
+
+    hots = jnp.concatenate([store.onehot(ox + HALO, oy + HALO, 0)[:, 0:slots] for ox, oy in cells], axis=1)
+    acts = jnp.concatenate([act_own[o] for o in range(len(cells))], axis=0)
+    energy = dot(thirds(emb_energy[...]), hots, NN) + dot(thirds(readout[...]), acts, NT)
     energy = jnp.sum(energy, axis=0, keepdims=True)
     for o, (ox, oy) in enumerate(cells):
         marked = region[ox + HALO, oy + HALO, 3:4, 0:slots]
@@ -437,32 +480,53 @@
     )(near, *in_hbm(embed, filters, w_up, w_energy))
 
 
-def far_layer(z, region, *near):
-    width = near[0].shape[1]
-    cells, anchors = z.block[0] * z.block[1], z.nax * z.nay
-    columns = z.nx * z.ny * z.groups
+def call(kernel, z, shapes, scratch, limit, operands):
     return pl.pallas_call(
-        functools.partial(far_kernel, z),
-        out_shape=(
-            jax.ShapeDtypeStruct(z.block + (1, z.slots), jnp.float32),
-            jax.ShapeDtypeStruct(z.block + (1, 3 * z.slots), jnp.float32),
-            jax.ShapeDtypeStruct((z.groups,) + z.block + (1, 3 * z.slots), jnp.float32),
-        ),
-        in_specs=[VMEM] * (1 + len(near)),
-        out_specs=[VMEM] * 3,
-        scratch_shapes=[
-            pltpu.VMEM((z.nx * 2 * HALO * z.groups, z.spec, LANES), jnp.bfloat16),
-            pltpu.VMEM((z.nax * 2, 4, z.slots, LANES), jnp.float32),
-            pltpu.VMEM((anchors, len(z.offsets), 2, z.slots, LANES), jnp.float32),
-            pltpu.VMEM((4, LANES, LANES), jnp.float32),
-            pltpu.VMEM((anchors, z.rad * z.slots, 2 * z.spec), jnp.bfloat16),
-            pltpu.VMEM((anchors, z.slots, z.rad * z.spec), jnp.bfloat16),
-            pltpu.VMEM((anchors, z.slots, width), jnp.bfloat16),
-            pltpu.VMEM((columns, 3, 8, LANES), jnp.float32),
-            pltpu.VMEM((cells, 3, z.slots, LANES), jnp.float32),
-        ] + [pltpu.VMEM((z.rad * z.slots, len(z.offsets) * LANES), jnp.bfloat16)] * z.nay,
-        compiler_params=pltpu.CompilerParams(vmem_limit_bytes=FAR_VMEM),
-    )(region, *near)
+        functools.partial(kernel, z),
+        out_shape=[jax.ShapeDtypeStruct(*shape) for shape in shapes],
+        in_specs=[VMEM] * len(operands),
+        out_specs=[VMEM] * len(shapes),
+        scratch_shapes=[pltpu.VMEM(*shape) for shape in scratch],
+        compiler_params=pltpu.CompilerParams(vmem_limit_bytes=limit),
+    )(*operands)
+
+
+def far_layer(z, region, near):
+    table, readout, emb_energy, onehot, anchors, sums, kept = near
+    width = table.shape[1]
+    cells, ring = z.block[0] * z.block[1], z.nax * z.nay
+    offsets, most = len(z.offsets), max(len(z.split_offsets(y + 1)[1]) for y in range(z.block[1]))
+    pair = (2, z.slots, LANES)
+    shapes = [
+        ((z.groups,) + z.block + (1, 3 * z.slots), jnp.float32),
+        (z.block + (1, 3 * z.slots), jnp.float32),
+        ((cells, 3, z.slots, LANES), jnp.float32),
+        ((cells, z.rad * z.slots, 2 * z.spec), jnp.bfloat16),
+        ((cells, z.slots, width), jnp.bfloat16),
+        ((z.nx * 2 * HALO * z.groups, z.spec, LANES), jnp.bfloat16),
+        ((z.nax * z.block[1], most) + pair, jnp.float32),
+    ]
+    scratch = [
+        ((z.nax * 2, 4, z.slots, LANES), jnp.float32),
+        ((z.nax * 2, offsets) + pair, jnp.float32),
+        ((4, LANES, LANES), jnp.float32),
+        ((ring, z.rad * z.slots, 2 * z.spec), jnp.bfloat16),
+        ((ring, z.slots, z.rad * z.spec), jnp.bfloat16),
+        ((cells * z.groups, 3, 8, LANES), jnp.float32),
+    ] + [((z.rad * z.slots, offsets * LANES), jnp.bfloat16)] * z.nay
+    operands = (region, table, readout, onehot, anchors, sums, kept)
+    return call(far_kernel, z, shapes, scratch, FAR_VMEM, operands)
+
+
+def own_layer(z, region, near, far):
+    table, readout, emb_energy, onehot, anchors, sums, kept = near
+    shapes = [
+        (z.block + (1, z.slots), jnp.float32),
+        (z.block + (1, 3 * z.slots), jnp.float32),
+    ]
+    scratch = [((z.block[0] * z.block[1], 3, z.slots, LANES), jnp.float32)]
+    operands = (region, readout, emb_energy, onehot, anchors, kept) + tuple(far)
+    return call(own_kernel, z, shapes, scratch, OWN_VMEM, operands)
 
 
 def on_device(positions, species, counts, embed, filters, w_up, w_energy):
@@ -488,7 +552,8 @@
     block = exchange(block, "gx", 0, HALO)
     near = near_layer(z, block, embed, filters, w_up, w_energy.reshape(1, width))
     region = exchange(block, "gy", 1, HALO)
-    energies, own, other = far_layer(z, region, *near)
+    other, *far = far_layer(z, region, near)
+    energies, own = own_layer(z, region, near, far)
 
     forces = own + lax.ppermute(other[0], "gz", downward)
     if not merged:

time: 30.1 us -> 28.7 us (0.953)
  waiting for transfers between devices: 5.54 us -> 4.38 us
    ppermute x1, waiting for transfers between devices: 1.16 us -> 0.01 us  [on_device(): forces = own + lax.ppermute(other[0], 'gz', downward)]
    pallas_call x1 -> x2, Pallas kernels: 10.3 us -> 9.98 us  [call(): pl.pallas_call(functools.partial(kernel, z), out_shape=[jax.ShapeDtypeStr...]
  transfers between devices with their start and end apart: 6 -> 6, of which waited for: 5 -> 4; matrix products, arithmetic and copies ran while one was open for 0% -> 0% of each run, Pallas kernels for 11% -> 19%
where the time goes in v5:
time: 28.7 us; the launch traced here: 28.5 us
  Pallas kernels  14.1 us (49%)
  starting transfers between devices  8.46 us (29%)
  waiting for transfers between devices  4.38 us (15%)
  other arithmetic  0.84 us (3%)
  between operations  0.67 us (2%)
    pallas_call x2, Pallas kernels, call(): pl.pallas_call(functools.partial(kernel, z), out_shape=[jax.ShapeDtypeStr...  9.98 us
    ppermute x2, starting transfers between devices, exchange(): from_far = lax.ppermute(up, axis, far)  7.39 us
    pallas_call x1, Pallas kernels, near_layer(): pl.pallas_call(functools.partial(near_kernel, z), out_shape=[jax.ShapeDty...  3.37 us
    ppermute x2, waiting for transfers between devices, exchange(): from_near = lax.ppermute(down, axis, near)  2.45 us
    ppermute x2, waiting for transfers between devices, exchange(): from_far = lax.ppermute(up, axis, far)  1.1 us
    ppermute x1, waiting for transfers between devices, on_device(): low = lax.ppermute(block, 'gz', upward)  0.83 us
    pallas_call x1, Pallas kernels, pack(): pl.pallas_call(pack_kernel, out_shape=jax.ShapeDtypeStruct((bx, by, 4, sl...  0.8 us
    add x1, other arithmetic, on_device(): forces = own + lax.ppermute(other[0], 'gz', downward)  0.6 us
  transfers between devices with their start and end apart: 6, of which 4 were waited for; matrix products, arithmetic and copies ran while one was open for 0% of the time, Pallas kernels for 19%

profile of v5, /device:TPU:0, one launch (start us, length us, event | category | flops | bytes accessed | tf_op | source)
XLA Modules:
  0.0 28.5 jit_solution(10067981332845372996)
XLA Ops:
  0.6 0.8 %shard_map.86 = f32[2,2,4,64]{3,2,1,0:T(4,128)S(1)} custom-call(s32[2,2]{1,0:T(2,128)} %bitcast.22, f32[2,2,1,192]{3,2,1,0:T(1,128)} %positions_hbm.1, s32[2,2,1,64]{3,2,1,0:T(1,128)} %species_hbm.1), custom_call_target="tpu_custom_call" | custom-call | tf_op jit(solution)/shard_map/pallas_call | solution.py:435
  1.4 0.5 %collective-permute-start = (f32[2,2,4,64]{3,2,1,0:T(4,128)S(1)}, f32[2,2,4,64]{3,2,1,0:T(4,128)S(1)}, u32[]{:S(2)}, u32[]{:S(2)}) collective-permute-start(f32[2,2,4,64]{3,2,1,0:T(4,128)S(1)} %shard_map.86), channel_id=1, source_target_pairs={{0,1},{1,0},{2,3},{3,2},{4,5},{5,4},{6,7},{7,6},{8,9},{9,8},{10,11... | collective-permute-start | bytes 12296 | tf_op jit(solution)/shard_map/ppermute | solution.py:543
  2.0 0.8 %collective-permute-done = f32[2,2,4,64]{3,2,1,0:T(4,128)S(1)} collective-permute-done((f32[2,2,4,64]{3,2,1,0:T(4,128)S(1)}, f32[2,2,4,64]{3,2,1,0:T(4,128)S(1)}, u32[]{:S(2)}, u32[]{:S(2)}) %collective-permute-start) | collective-permute-done | bytes 4128 | tf_op jit(solution)/shard_map/ppermute | solution.py:543
  2.8 0.1 pad_maximum_fusion.2
  2.9 3.8 %collective-permute-start.2 = (f32[2,2,4,128]{3,2,1,0:T(4,128)S(1)}, f32[2,2,4,128]{3,2,1,0:T(4,128)S(1)}, u32[]{:S(2)}, u32[]{:S(2)}) collective-permute-start(f32[2,2,4,128]{3,2,1,0:T(4,128)S(1)} %pad_maximum_fusion.2), channel_id=1, source_target_pairs={{0,24},{8,16},{16,8},{24,0},{1,25},{9,17},{17,9},{25,1},{2,26},{10... | collective-permute-start | bytes 24584 | tf_op jit(solution)/shard_map/ppermute | solution.py:35
  6.6 0.5 %collective-permute-start.1 = (f32[2,2,4,128]{3,2,1,0:T(4,128)S(1)}, f32[2,2,4,128]{3,2,1,0:T(4,128)S(1)}, u32[]{:S(2)}, u32[]{:S(2)}) collective-permute-start(f32[2,2,4,128]{3,2,1,0:T(4,128)S(1)} %pad_maximum_fusion.2), channel_id=1, source_target_pairs={{0,8},{8,0},{16,24},{24,16},{1,9},{9,1},{17,25},{25,17},{2,10},{10... | collective-permute-start | bytes 24584 | tf_op jit(solution)/shard_map/ppermute | solution.py:36
  7.2 1.1 %collective-permute-done.2 = f32[2,2,4,128]{3,2,1,0:T(4,128)S(1)} collective-permute-done((f32[2,2,4,128]{3,2,1,0:T(4,128)S(1)}, f32[2,2,4,128]{3,2,1,0:T(4,128)S(1)}, u32[]{:S(2)}, u32[]{:S(2)}) %collective-permute-start.2) | collective-permute-done | bytes 8224 | tf_op jit(solution)/shard_map/ppermute | solution.py:35
  8.3 2.0 %collective-permute-done.1 = f32[2,2,4,128]{3,2,1,0:T(4,128)S(1)} collective-permute-done((f32[2,2,4,128]{3,2,1,0:T(4,128)S(1)}, f32[2,2,4,128]{3,2,1,0:T(4,128)S(1)}, u32[]{:S(2)}, u32[]{:S(2)}) %collective-permute-start.1) | collective-permute-done | bytes 8224 | tf_op jit(solution)/shard_map/ppermute | solution.py:36
  10.3 0.1 pad_maximum_fusion.1.near
  10.4 3.6 %collective-permute-start.4 = (f32[6,2,4,128]{3,2,1,0:T(4,128)S(1)}, f32[6,2,4,128]{3,2,1,0:T(4,128)S(1)}, u32[]{:S(2)}, u32[]{:S(2)}) collective-permute-start(f32[6,2,4,128]{3,2,1,0:T(4,128)S(1)} %pad_maximum_fusion.1.near), channel_id=1, source_target_pairs={{0,6},{2,4},{4,2},{6,0},{1,7},{3,5},{5,3},{7,1},{8,14},{10,12},{12... | collective-permute-start | bytes 73736 | tf_op jit(solution)/shard_map/ppermute | solution.py:35
  14.0 0.0 collective-permute-start.3
  14.0 3.4 %shard_map.87 = (bf16[512,128]{1,0:T(8,128)(2,1)S(1)}, f32[8,128]{1,0:T(8,128)S(1)}, f32[8,128]{1,0:T(8,128)S(1)}, bf16[12,128,128]{2,1,0:T(8,128)(2,1)S(1)}, f3...) custom-call(f32[6,2,4,128]{3,2,1,0:T(4,128)S(1)} %pad_maximum_fusion.1.near, ...), custom_call_target="tpu_custom_call" | custom-call | flops 402653184 | bytes 1048576 | tf_op jit(solution)/shard_map/pallas_call | solution.py:464
  17.4 0.0 collective-permute-done.4
  17.4 0.4 %collective-permute-done.3 = f32[6,2,4,128]{3,2,1,0:T(4,128)S(1)} collective-permute-done((f32[6,2,4,128]{3,2,1,0:T(4,128)S(1)}, f32[6,2,4,128]{3,2,1,0:T(4,128)S(1)}, u32[]{:S(2)}, u32[]{:S(2)}) %collective-permute-start.3) | collective-permute-done | bytes 24608 | tf_op jit(solution)/shard_map/ppermute | solution.py:36
  17.8 0.1 pad_maximum_fusion.region
  17.9 8.1 %shard_map.88 = (f32[1,2,2,1,192]{4,3,2,1,0:T(1,128)S(1)}, f32[2,2,1,192]{3,2,1,0:T(1,128)S(1)}, f32[4,3,64,128]{3,2,1,0:T(8,128)S(1)}, bf16[4,256,256]{2,1,0:T(...) custom-call(f32[6,6,4,128]{3,2,1,0:T(4,128)S(1)} %pad_maximum_fusion, ...), custom_call_target="tpu_custom_call" | custom-call | tf_op jit(solution)/shard_map/pallas_call | solution.py:484
  26.0 0.0 collective-permute-start.5
  26.0 1.9 %shard_map.89 = (f32[2,2,1,64]{3,2,1,0:T(1,128)}, f32[2,2,1,192]{3,2,1,0:T(1,128)S(1)}) custom-call(f32[6,6,4,128]{3,2,1,0:T(4,128)S(1)} %pad_maximum_fusion.region, f32[8,128]{1,0:T(8,128)S(1)} %get-tuple-element.18.readout_ref.readout, f32[8,128]{1,0:T(8,128)S(1)} %get-tuple-element.19.emb_energy, bf16[12,128,128]{2,1,0:T(8,128)(2,1)S(1)} %get-tuple-element.20.onehot_near, ...), custom_call_target="tpu_custom_call" | custom-call | tf_op jit(solution)/shard_map/pallas_call | solution.py:484
  27.9 0.0 collective-permute-done.5
  27.9 0.6 %add.12 = f32[2,2,1,192]{3,2,1,0:T(1,128)} add(f32[2,2,1,192]{3,2,1,0:T(1,128)S(1)} %get-tuple-element.32, f32[2,2,1,192]{3,2,1,0:T(1,128)S(1)} %collective-permute-done.5) | non-fusion elementwise | flops 768 | bytes 9216 | tf_op jit(solution)/shard_map/add | solution.py:558
  (2 shorter events, 0.0 us)
Async XLA Ops:
  1.4 1.3 %collective-permute-start = (f32[2,2,4,64]{3,2,1,0:T(4,128)S(1)}, f32[2,2,4,64]{3,2,1,0:T(4,128)S(1)}, u32[]{:S(2)}, u32[]{:S(2)}) collective-permute-start(f32[2,2,4,64]{3,2,1,0:T(4,128)S(1)} %shard_map.86), channel_id=1, source_target_pairs={{0,1},{1,0},{2,3},{3,2},{4,5},{5,4},{6,7},{7,6},{8,9},{9,8},{10,11... | collective-permute-start | bytes 12296 | tf_op jit(solution)/shard_map/ppermute | solution.py:543
  2.9 5.4 %collective-permute-start.2 = (f32[2,2,4,128]{3,2,1,0:T(4,128)S(1)}, f32[2,2,4,128]{3,2,1,0:T(4,128)S(1)}, u32[]{:S(2)}, u32[]{:S(2)}) collective-permute-start(f32[2,2,4,128]{3,2,1,0:T(4,128)S(1)} %pad_maximum_fusion.2), channel_id=1, source_target_pairs={{0,24},{8,16},{16,8},{24,0},{1,25},{9,17},{17,9},{25,1},{2,26},{10... | collective-permute-start | bytes 24584 | tf_op jit(solution)/shard_map/ppermute | solution.py:35
  6.6 3.7 %collective-permute-start.1 = (f32[2,2,4,128]{3,2,1,0:T(4,128)S(1)}, f32[2,2,4,128]{3,2,1,0:T(4,128)S(1)}, u32[]{:S(2)}, u32[]{:S(2)}) collective-permute-start(f32[2,2,4,128]{3,2,1,0:T(4,128)S(1)} %pad_maximum_fusion.2), channel_id=1, source_target_pairs={{0,8},{8,0},{16,24},{24,16},{1,9},{9,1},{17,25},{25,17},{2,10},{10... | collective-permute-start | bytes 24584 | tf_op jit(solution)/shard_map/ppermute | solution.py:36
  10.4 7.0 %collective-permute-start.4 = (f32[6,2,4,128]{3,2,1,0:T(4,128)S(1)}, f32[6,2,4,128]{3,2,1,0:T(4,128)S(1)}, u32[]{:S(2)}, u32[]{:S(2)}) collective-permute-start(f32[6,2,4,128]{3,2,1,0:T(4,128)S(1)} %pad_maximum_fusion.1.near), channel_id=1, source_target_pairs={{0,6},{2,4},{4,2},{6,0},{1,7},{3,5},{5,3},{7,1},{8,14},{10,12},{12... | collective-permute-start | bytes 73736 | tf_op jit(solution)/shard_map/ppermute | solution.py:35
  14.0 3.8 %collective-permute-start.3 = (f32[6,2,4,128]{3,2,1,0:T(4,128)S(1)}, f32[6,2,4,128]{3,2,1,0:T(4,128)S(1)}, u32[]{:S(2)}, u32[]{:S(2)}) collective-permute-start(f32[6,2,4,128]{3,2,1,0:T(4,128)S(1)} %pad_maximum_fusion.1.near), channel_id=1, source_target_pairs={{0,2},{2,0},{4,6},{6,4},{1,3},{3,1},{5,7},{7,5},{8,10},{10,8},{12,... | collective-permute-start | bytes 73736 | tf_op jit(solution)/shard_map/ppermute | solution.py:36
  26.0 1.9 %collective-permute-start.5 = (f32[2,2,1,192]{3,2,1,0:T(1,128)S(1)}, f32[2,2,1,192]{3,2,1,0:T(1,128)S(1)}, u32[]{:S(2)}, u32[]{:S(2)}) collective-permute-start(f32[2,2,1,192]{3,2,1,0:T(1,128)S(1)} %bitcast.11), channel_id=1, source_target_pairs={{1,0},{0,1},{3,2},{2,3},{5,4},{4,5},{7,6},{6,7},{9,8},{8,9},{11,10... | collective-permute-start | bytes 9224 | tf_op jit(solution)/shard_map/ppermute | solution.py:558

commit v6 on v5

--- a/solution.py
+++ b/solution.py
@@ -14,6 +14,9 @@
 LANES = 128
 STEP = 16
 WIDE = 4
+LAG = 2
+GROUP = 2
+LATER = 0
 BATCH = 4
 FORCE_SCALE = 4.0 * MSG_SCALE
 LOG2E = 1.4426950408889634
@@ -113,9 +116,10 @@
     return row[0:1] + dx, row[1:2] + dy, row[2:3]
 
 
-def weigh(z, position, anchor, offset, buffer, lanes, keep):
+def weigh(z, position, anchor, offset, keep):
     tx, ty, tz = position
     shift = z.z_shift(offset[2])
+    weights = [[] for _ in range(z.rad)]
     for c in z.rows:
         ex = tx - anchor[0, c, :]
         ey = ty - anchor[1, c, :]
@@ -140,7 +144,21 @@
             else:
                 e = e * e * e
                 w = w * e
-            buffer[k * z.slots + c.start:k * z.slots + c.stop, lanes] = w.astype(jnp.bfloat16)
+            weights[k].append(w.astype(jnp.bfloat16))
+    return jnp.concatenate([part for parts in weights for part in parts], axis=0)
+
+
+def grouped(values):
+    return [values[i:i + GROUP] for i in range(0, len(values), GROUP)]
+
+
+def staggered(tasks, first, second, lag):
+    results = []
+    for t in range(len(tasks) + lag):
+        if t < len(tasks):
+            results.append(first(*tasks[t]))
+        if t >= lag:
+            second(results[t - lag], *tasks[t - lag])
 
 
 def pack_kernel(counts_hbm, positions_hbm, species_hbm, out, counts, positions, species, arrived):
@@ -164,7 +182,7 @@
 def near_kernel(
     z, near, embed_hbm, filters_hbm, w_up_hbm, w_energy_hbm,
     table, readout, emb_energy, onehot, anchors, sums, kept,
-    emb_pad, stage, embed, filters, w_up, w_energy, arrived, *buffers,
+    emb_pad, stage, embed, filters, w_up, w_energy, arrived,
 ):
     nspec, width = embed.shape
     by = z.block[1]
@@ -180,20 +198,26 @@
     place_anchors(z, stage, [(near, ax + 1, y) for ax in range(z.nax) for y in range(by)], anchors)
 
     def message_at(ax, carry):
+        totals = {}
+
+        def weigh_some(y, some):
+            weights = []
+            for n in some:
+                dx, dy, _ = z.offsets[n]
+                keep = kept.at[ax * by + y, z.split_offsets(y + 1)[0].index(n)]
+                spot = target(near, ax + 1 + dx, y + dy, z.offsets[n])
+                weights.append(weigh(z, spot, anchors.at[ax * by + y], z.offsets[n], keep))
+            return jnp.concatenate(weights, axis=1)
+
+        def gather_some(weights, y, some):
+            spots = [z.offsets[n] for n in some]
+            hots = [onehot[((ax + 1 + dx) * by + y + dy) * z.groups + g] for dx, dy, g in spots]
+            term = dot(weights, jnp.concatenate(hots, axis=1), NT)
+            totals[y] = totals[y] + term if y in totals else term
+
+        staggered([(y, some) for y in range(by) for some in grouped(z.split_offsets(y + 1)[0])], weigh_some, gather_some, LAG)
         for y in range(by):
-            a = ax * by + y
-            some = z.split_offsets(y + 1)[0]
-            hots = []
-            for i, n in enumerate(some):
-                dx, dy, g = z.offsets[n]
-                spot = target(near, ax + 1 + dx, y + dy, z.offsets[n])
-                weigh(
-                    z, spot, anchors.at[a], z.offsets[n], buffers[y],
-                    slice(i * LANES, (i + 1) * LANES), kept.at[a, i],
-                )
-                hots.append(onehot[((ax + 1 + dx) * by + y + dy) * z.groups + g])
-            weights = buffers[y][:, 0:len(some) * LANES]
-            sums[a] = dot(weights, jnp.concatenate(hots, axis=1), NT)
+            sums[ax * by + y] = totals[y]
         return carry
 
     lax.fori_loop(0, z.nax, message_at, 0)
@@ -265,12 +289,20 @@
     return f * (f * steep + plain), (ex, ey, ez)
 
 
-def blocks(z, store, region, adj_table, ax, ay, some, sums, back):
-    for first in range(0, len(some), WIDE):
-        part = some[first:first + WIDE]
-        spots = [(ax + 1 + z.offsets[n][0], ay + 1 + z.offsets[n][1], z.offsets[n][2]) for n in part]
-        hots = jnp.concatenate([store.onehot(*spot) for spot in spots], axis=1)
-        gains = dot(adj_table[...], jnp.concatenate([hots, hots], axis=0), NN)
+def blocks(z, store, region, work, back):
+    tasks = [
+        (ax, ay, table, some[first:first + WIDE], sums)
+        for ax, ay, table, some, sums in work for first in range(0, len(some), WIDE)
+    ]
+
+    def spots_of(ax, ay, part):
+        return [(ax + 1 + z.offsets[n][0], ay + 1 + z.offsets[n][1], z.offsets[n][2]) for n in part]
+
+    def multiply(ax, ay, table, part, sums):
+        hots = jnp.concatenate([store.onehot(*spot) for spot in spots_of(ax, ay, part)], axis=1)
+        return dot(table[...], jnp.concatenate([hots, hots], axis=0), NN)
+
+    def add_forces(gains, ax, ay, table, part, sums):
         totals = [[None] * 3 for _ in part]
         for r in range(len(z.rows)):
             some_gains = gains[r * z.rad * STEP:(r + 1) * z.rad * STEP]
@@ -284,15 +316,17 @@
                         term = sum(term[j:j + 8] for j in range(8, STEP, 8)) + term[0:8]
                         totals[i][q] = term if totals[i][q] is None else totals[i][q] + term
         if back is not None:
-            for (x, y, g), total in zip(spots, totals):
+            for (x, y, g), total in zip(spots_of(ax, ay, part), totals):
                 for q in range(3):
                     back[((x - HALO) * z.block[1] + y - HALO) * z.groups + g, q] += total[q]
+
+    staggered(tasks, multiply, add_forces, LATER)
 
 
 def far_kernel(
     z, region, table, readout_ref, onehot_near, anchors_near, sums_near, kept_near,
     other, part, mine, adj_own, act_own, onehot_far, kept_own,
-    anchors_far, kept_far, stage, adj_table, mixed, back, *buffers,
+    anchors_far, kept_far, stage, adj_table, mixed, back,
 ):
     by = z.block[1]
     bf = jnp.bfloat16
@@ -310,24 +344,27 @@
     )
 
     def message_at(ax, carry):
+        totals = {ay: sums_near[ax * by + ay - 1] for ay in range(z.nay) if z.inner(ay)}
+
+        def weigh_some(ay, some):
+            weights = []
+            for n in some:
+                dx, dy, _ = z.offsets[n]
+                spot = target(region, ax + 1 + dx, ay + 1 + dy, z.offsets[n])
+                weights.append(weigh(z, spot, store.anchor(ax, ay), z.offsets[n], store.radial(ax, ay, n)))
+            return jnp.concatenate(weights, axis=1)
+
+        def gather_some(weights, ay, some):
+            spots = [z.offsets[n] for n in some]
+            hots = [store.onehot(ax + 1 + dx, ay + 1 + dy, g) for dx, dy, g in spots]
+            term = dot(weights, jnp.concatenate(hots, axis=1), NT)
+            totals[ay] = totals[ay] + term if ay in totals else term
+
+        staggered([(ay, some) for ay in range(z.nay) for some in grouped(z.split_offsets(ay)[1])], weigh_some, gather_some, LAG)
         for ay in range(z.nay):
-            a = ax * z.nay + ay
-            some = z.split_offsets(ay)[1]
-            hots = []
-            for i, n in enumerate(some):
-                dx, dy, g = z.offsets[n]
-                x, y = ax + 1 + dx, ay + 1 + dy
-                weigh(
-                    z, target(region, x, y, z.offsets[n]), store.anchor(ax, ay), z.offsets[n], buffers[ay],
-                    slice(i * LANES, (i + 1) * LANES), store.radial(ax, ay, n),
-                )
-                hots.append(store.onehot(x, y, g))
-            total = sums_near[ax * by + ay - 1] if z.inner(ay) else None
-            if some:
-                term = dot(buffers[ay][:, 0:len(some) * LANES], jnp.concatenate(hots, axis=1), NT)
-                total = term if total is None else total + term
             for k in range(rad):
-                mixed[a, :, k * spec:(k + 1) * spec] = total[k * slots:(k + 1) * slots].astype(bf)
+                part_sum = totals[ay][k * slots:(k + 1) * slots].astype(bf)
+                mixed[ax * z.nay + ay, :, k * spec:(k + 1) * spec] = part_sum
         return carry
 
     lax.fori_loop(0, z.nax, message_at, 0)
@@ -365,16 +402,18 @@
 
     back[...] = jnp.zeros_like(back)
 
+    work = []
     for ax in range(z.nax):
         for ay in range(z.nay):
-            o = z.cell(ax, ay)
             some = [n for n, (dx, dy, _) in enumerate(z.offsets) if z.cell(ax + dx, ay + dy) is not None]
-            sums = None if o is None else [[None] * len(z.rows) for _ in range(3)]
-            blocks(z, store, region, adj_at(ax, ay), ax, ay, some, sums, back)
-            if o is not None:
-                for q in range(3):
-                    for r, c in enumerate(z.rows):
-                        mine[o, q, c, :] = sums[q][r]
+            sums = None if z.cell(ax, ay) is None else [[None] * len(z.rows) for _ in range(3)]
+            work.append((ax, ay, adj_at(ax, ay), some, sums))
+    blocks(z, store, region, work, back)
+    for ax, ay, _, _, sums in work:
+        if sums is not None:
+            for q in range(3):
+                for r, c in enumerate(z.rows):
+                    mine[z.cell(ax, ay), q, c, :] = sums[q][r]
 
     for ox in range(z.block[0]):
         for oy in range(by):
@@ -395,11 +434,13 @@
     slots = z.slots
     store = Store(z, onehot_near, onehot_far, anchors_near, None, kept_near, kept_own, None)
     cells = [(ox, oy) for ox in range(z.block[0]) for oy in range(z.block[1])]
+    work = []
     for o, (ox, oy) in enumerate(cells):
-        ax, ay = ox + 1, oy + 1
-        some = [n for n, (dx, dy, _) in enumerate(z.offsets) if z.cell(ax + dx, ay + dy) is None]
+        some = [n for n, (dx, dy, _) in enumerate(z.offsets) if z.cell(ox + 1 + dx, oy + 1 + dy) is None]
         sums = [[mine_part[o, q, c, :] for c in z.rows] for q in range(3)]
-        blocks(z, store, region, adj_own.at[o], ax, ay, some, sums, None)
+        work.append((ox + 1, oy + 1, adj_own.at[o], some, sums))
+    blocks(z, store, region, work, None)
+    for o, (_, _, _, _, sums) in enumerate(work):
         for q in range(3):
             for r, c in enumerate(z.rows):
                 mine[o, q, c, :] = sums[q][r]
@@ -474,7 +515,7 @@
             pltpu.VMEM(w_up.shape, w_up.dtype),
             pltpu.VMEM(w_energy.shape, w_energy.dtype),
             pltpu.SemaphoreType.DMA((4,)),
-        ] + [pltpu.VMEM((z.rad * z.slots, most * LANES), jnp.bfloat16)] * by,
+        ],
         compiler_params=pltpu.CompilerParams(vmem_limit_bytes=12 * 1024 * 1024),
         cost_estimate=pl.CostEstimate(flops=flops, bytes_accessed=1 << 20, transcendentals=0),
     )(near, *in_hbm(embed, filters, w_up, w_energy))
@@ -513,7 +554,7 @@
         ((ring, z.rad * z.slots, 2 * z.spec), jnp.bfloat16),
         ((ring, z.slots, z.rad * z.spec), jnp.bfloat16),
         ((cells * z.groups, 3, 8, LANES), jnp.float32),
-    ] + [((z.rad * z.slots, offsets * LANES), jnp.bfloat16)] * z.nay
+    ]
     operands = (region, table, readout, onehot, anchors, sums, kept)
     return call(far_kernel, z, shapes, scratch, FAR_VMEM, operands)
 

time: 28.7 us -> 27.8 us (0.969)
  Pallas kernels: 14.1 us -> 12.9 us
  waiting for transfers between devices: 4.38 us -> 4.72 us
    pallas_call x2, Pallas kernels: 9.98 us -> 9.02 us  [call(): pl.pallas_call(functools.partial(kernel, z), out_shape=[jax.ShapeDtypeStr...]
    pallas_call x1, Pallas kernels: 3.37 us -> 3.03 us  [near_layer(): pl.pallas_call(functools.partial(near_kernel, z), out_shape=[jax.ShapeDty...]
    ppermute x2, waiting for transfers between devices: 2.45 us -> 2.79 us  [exchange(): from_near = lax.ppermute(down, axis, near)]
  transfers between devices with their start and end apart: 6 -> 6, of which waited for: 4 -> 4; matrix products, arithmetic and copies ran while one was open for 0% -> 0% of each run, Pallas kernels for 19% -> 18%
where the time goes in v6:
time: 27.8 us; the launch traced here: 27.5 us
  Pallas kernels  12.9 us (46%)
  starting transfers between devices  8.46 us (30%)
  waiting for transfers between devices  4.72 us (17%)
  other arithmetic  0.84 us (3%)
  between operations  0.67 us (2%)
    pallas_call x2, Pallas kernels, call(): pl.pallas_call(functools.partial(kernel, z), out_shape=[jax.ShapeDtypeStr...  9.02 us
    ppermute x2, starting transfers between devices, exchange(): from_far = lax.ppermute(up, axis, far)  7.39 us
    pallas_call x1, Pallas kernels, near_layer(): pl.pallas_call(functools.partial(near_kernel, z), out_shape=[jax.ShapeDty...  3.03 us
    ppermute x2, waiting for transfers between devices, exchange(): from_near = lax.ppermute(down, axis, near)  2.79 us
    ppermute x2, waiting for transfers between devices, exchange(): from_far = lax.ppermute(up, axis, far)  1.1 us
    ppermute x1, waiting for transfers between devices, on_device(): low = lax.ppermute(block, 'gz', upward)  0.83 us
    pallas_call x1, Pallas kernels, pack(): pl.pallas_call(pack_kernel, out_shape=jax.ShapeDtypeStruct((bx, by, 4, sl...  0.8 us
    add x1, other arithmetic, on_device(): forces = own + lax.ppermute(other[0], 'gz', downward)  0.6 us
  transfers between devices with their start and end apart: 6, of which 4 were waited for; matrix products, arithmetic and copies ran while one was open for 0% of the time, Pallas kernels for 18%

profile of v6, /device:TPU:0, one launch (start us, length us, event | category | flops | bytes accessed | tf_op | source)
XLA Modules:
  0.0 27.5 jit_solution(2033194293699385377)
XLA Ops:
  0.6 0.8 %shard_map.86 = f32[2,2,4,64]{3,2,1,0:T(4,128)S(1)} custom-call(s32[2,2]{1,0:T(2,128)} %bitcast.22, f32[2,2,1,192]{3,2,1,0:T(1,128)} %positions_hbm.1, s32[2,2,1,64]{3,2,1,0:T(1,128)} %species_hbm.1), custom_call_target="tpu_custom_call" | custom-call | tf_op jit(solution)/shard_map/pallas_call | solution.py:476
  1.4 0.5 %collective-permute-start = (f32[2,2,4,64]{3,2,1,0:T(4,128)S(1)}, f32[2,2,4,64]{3,2,1,0:T(4,128)S(1)}, u32[]{:S(2)}, u32[]{:S(2)}) collective-permute-start(f32[2,2,4,64]{3,2,1,0:T(4,128)S(1)} %shard_map.86), channel_id=1, source_target_pairs={{0,1},{1,0},{2,3},{3,2},{4,5},{5,4},{6,7},{7,6},{8,9},{9,8},{10,11... | collective-permute-start | bytes 12296 | tf_op jit(solution)/shard_map/ppermute | solution.py:584
  2.0 0.8 %collective-permute-done = f32[2,2,4,64]{3,2,1,0:T(4,128)S(1)} collective-permute-done((f32[2,2,4,64]{3,2,1,0:T(4,128)S(1)}, f32[2,2,4,64]{3,2,1,0:T(4,128)S(1)}, u32[]{:S(2)}, u32[]{:S(2)}) %collective-permute-start) | collective-permute-done | bytes 4128 | tf_op jit(solution)/shard_map/ppermute | solution.py:584
  2.8 0.1 pad_maximum_fusion.2
  2.9 3.8 %collective-permute-start.2 = (f32[2,2,4,128]{3,2,1,0:T(4,128)S(1)}, f32[2,2,4,128]{3,2,1,0:T(4,128)S(1)}, u32[]{:S(2)}, u32[]{:S(2)}) collective-permute-start(f32[2,2,4,128]{3,2,1,0:T(4,128)S(1)} %pad_maximum_fusion.2), channel_id=1, source_target_pairs={{0,24},{8,16},{16,8},{24,0},{1,25},{9,17},{17,9},{25,1},{2,26},{10... | collective-permute-start | bytes 24584 | tf_op jit(solution)/shard_map/ppermute | solution.py:38
  6.6 0.5 %collective-permute-start.1 = (f32[2,2,4,128]{3,2,1,0:T(4,128)S(1)}, f32[2,2,4,128]{3,2,1,0:T(4,128)S(1)}, u32[]{:S(2)}, u32[]{:S(2)}) collective-permute-start(f32[2,2,4,128]{3,2,1,0:T(4,128)S(1)} %pad_maximum_fusion.2), channel_id=1, source_target_pairs={{0,8},{8,0},{16,24},{24,16},{1,9},{9,1},{17,25},{25,17},{2,10},{10... | collective-permute-start | bytes 24584 | tf_op jit(solution)/shard_map/ppermute | solution.py:39
  7.2 1.1 %collective-permute-done.2 = f32[2,2,4,128]{3,2,1,0:T(4,128)S(1)} collective-permute-done((f32[2,2,4,128]{3,2,1,0:T(4,128)S(1)}, f32[2,2,4,128]{3,2,1,0:T(4,128)S(1)}, u32[]{:S(2)}, u32[]{:S(2)}) %collective-permute-start.2) | collective-permute-done | bytes 8224 | tf_op jit(solution)/shard_map/ppermute | solution.py:38
  8.3 2.0 %collective-permute-done.1 = f32[2,2,4,128]{3,2,1,0:T(4,128)S(1)} collective-permute-done((f32[2,2,4,128]{3,2,1,0:T(4,128)S(1)}, f32[2,2,4,128]{3,2,1,0:T(4,128)S(1)}, u32[]{:S(2)}, u32[]{:S(2)}) %collective-permute-start.1) | collective-permute-done | bytes 8224 | tf_op jit(solution)/shard_map/ppermute | solution.py:39
  10.3 0.1 pad_maximum_fusion.1.near
  10.4 3.6 %collective-permute-start.4 = (f32[6,2,4,128]{3,2,1,0:T(4,128)S(1)}, f32[6,2,4,128]{3,2,1,0:T(4,128)S(1)}, u32[]{:S(2)}, u32[]{:S(2)}) collective-permute-start(f32[6,2,4,128]{3,2,1,0:T(4,128)S(1)} %pad_maximum_fusion.1.near), channel_id=1, source_target_pairs={{0,6},{2,4},{4,2},{6,0},{1,7},{3,5},{5,3},{7,1},{8,14},{10,12},{12... | collective-permute-start | bytes 73736 | tf_op jit(solution)/shard_map/ppermute | solution.py:38
  14.0 0.0 collective-permute-start.3
  14.0 3.0 %shard_map.87 = (bf16[512,128]{1,0:T(8,128)(2,1)S(1)}, f32[8,128]{1,0:T(8,128)S(1)}, f32[8,128]{1,0:T(8,128)S(1)}, bf16[12,128,128]{2,1,0:T(8,128)(2,1)S(1)}, f3...) custom-call(f32[6,2,4,128]{3,2,1,0:T(4,128)S(1)} %pad_maximum_fusion.1.near, ...), custom_call_target="tpu_custom_call" | custom-call | flops 402653184 | bytes 1048576 | tf_op jit(solution)/shard_map/pallas_call | solution.py:505
  17.0 0.0 collective-permute-done.4
  17.0 0.8 %collective-permute-done.3 = f32[6,2,4,128]{3,2,1,0:T(4,128)S(1)} collective-permute-done((f32[6,2,4,128]{3,2,1,0:T(4,128)S(1)}, f32[6,2,4,128]{3,2,1,0:T(4,128)S(1)}, u32[]{:S(2)}, u32[]{:S(2)}) %collective-permute-start.3) | collective-permute-done | bytes 24608 | tf_op jit(solution)/shard_map/ppermute | solution.py:39
  17.8 0.1 pad_maximum_fusion.region
  17.9 7.1 %shard_map.88 = (f32[1,2,2,1,192]{4,3,2,1,0:T(1,128)S(1)}, f32[2,2,1,192]{3,2,1,0:T(1,128)S(1)}, f32[4,3,64,128]{3,2,1,0:T(8,128)S(1)}, bf16[4,256,256]{2,1,0:T(...) custom-call(f32[6,6,4,128]{3,2,1,0:T(4,128)S(1)} %pad_maximum_fusion, ...), custom_call_target="tpu_custom_call" | custom-call | tf_op jit(solution)/shard_map/pallas_call | solution.py:525
  25.0 0.0 collective-permute-start.5
  25.0 1.9 %shard_map.89 = (f32[2,2,1,64]{3,2,1,0:T(1,128)}, f32[2,2,1,192]{3,2,1,0:T(1,128)S(1)}) custom-call(f32[6,6,4,128]{3,2,1,0:T(4,128)S(1)} %pad_maximum_fusion.region, f32[8,128]{1,0:T(8,128)S(1)} %get-tuple-element.18.readout_ref.readout, f32[8,128]{1,0:T(8,128)S(1)} %get-tuple-element.19.emb_energy, bf16[12,128,128]{2,1,0:T(8,128)(2,1)S(1)} %get-tuple-element.20.onehot_near, ...), custom_call_target="tpu_custom_call" | custom-call | tf_op jit(solution)/shard_map/pallas_call | solution.py:525
  26.9 0.0 collective-permute-done.5
  26.9 0.6 %add.12 = f32[2,2,1,192]{3,2,1,0:T(1,128)} add(f32[2,2,1,192]{3,2,1,0:T(1,128)S(1)} %get-tuple-element.32, f32[2,2,1,192]{3,2,1,0:T(1,128)S(1)} %collective-permute-done.5) | non-fusion elementwise | flops 768 | bytes 9216 | tf_op jit(solution)/shard_map/add | solution.py:599
  (2 shorter events, 0.0 us)
Async XLA Ops:
  1.4 1.3 %collective-permute-start = (f32[2,2,4,64]{3,2,1,0:T(4,128)S(1)}, f32[2,2,4,64]{3,2,1,0:T(4,128)S(1)}, u32[]{:S(2)}, u32[]{:S(2)}) collective-permute-start(f32[2,2,4,64]{3,2,1,0:T(4,128)S(1)} %shard_map.86), channel_id=1, source_target_pairs={{0,1},{1,0},{2,3},{3,2},{4,5},{5,4},{6,7},{7,6},{8,9},{9,8},{10,11... | collective-permute-start | bytes 12296 | tf_op jit(solution)/shard_map/ppermute | solution.py:584
  2.9 5.4 %collective-permute-start.2 = (f32[2,2,4,128]{3,2,1,0:T(4,128)S(1)}, f32[2,2,4,128]{3,2,1,0:T(4,128)S(1)}, u32[]{:S(2)}, u32[]{:S(2)}) collective-permute-start(f32[2,2,4,128]{3,2,1,0:T(4,128)S(1)} %pad_maximum_fusion.2), channel_id=1, source_target_pairs={{0,24},{8,16},{16,8},{24,0},{1,25},{9,17},{17,9},{25,1},{2,26},{10... | collective-permute-start | bytes 24584 | tf_op jit(solution)/shard_map/ppermute | solution.py:38
  6.6 3.7 %collective-permute-start.1 = (f32[2,2,4,128]{3,2,1,0:T(4,128)S(1)}, f32[2,2,4,128]{3,2,1,0:T(4,128)S(1)}, u32[]{:S(2)}, u32[]{:S(2)}) collective-permute-start(f32[2,2,4,128]{3,2,1,0:T(4,128)S(1)} %pad_maximum_fusion.2), channel_id=1, source_target_pairs={{0,8},{8,0},{16,24},{24,16},{1,9},{9,1},{17,25},{25,17},{2,10},{10... | collective-permute-start | bytes 24584 | tf_op jit(solution)/shard_map/ppermute | solution.py:39
  10.4 6.7 %collective-permute-start.4 = (f32[6,2,4,128]{3,2,1,0:T(4,128)S(1)}, f32[6,2,4,128]{3,2,1,0:T(4,128)S(1)}, u32[]{:S(2)}, u32[]{:S(2)}) collective-permute-start(f32[6,2,4,128]{3,2,1,0:T(4,128)S(1)} %pad_maximum_fusion.1.near), channel_id=1, source_target_pairs={{0,6},{2,4},{4,2},{6,0},{1,7},{3,5},{5,3},{7,1},{8,14},{10,12},{12... | collective-permute-start | bytes 73736 | tf_op jit(solution)/shard_map/ppermute | solution.py:38
  14.0 3.8 %collective-permute-start.3 = (f32[6,2,4,128]{3,2,1,0:T(4,128)S(1)}, f32[6,2,4,128]{3,2,1,0:T(4,128)S(1)}, u32[]{:S(2)}, u32[]{:S(2)}) collective-permute-start(f32[6,2,4,128]{3,2,1,0:T(4,128)S(1)} %pad_maximum_fusion.1.near), channel_id=1, source_target_pairs={{0,2},{2,0},{4,6},{6,4},{1,3},{3,1},{5,7},{7,5},{8,10},{10,8},{12,... | collective-permute-start | bytes 73736 | tf_op jit(solution)/shard_map/ppermute | solution.py:39
  25.0 1.9 %collective-permute-start.5 = (f32[2,2,1,192]{3,2,1,0:T(1,128)S(1)}, f32[2,2,1,192]{3,2,1,0:T(1,128)S(1)}, u32[]{:S(2)}, u32[]{:S(2)}) collective-permute-start(f32[2,2,1,192]{3,2,1,0:T(1,128)S(1)} %bitcast.11), channel_id=1, source_target_pairs={{1,0},{0,1},{3,2},{2,3},{5,4},{4,5},{7,6},{6,7},{9,8},{8,9},{11,10... | collective-permute-start | bytes 9224 | tf_op jit(solution)/shard_map/ppermute | solution.py:599

commit v7 on v6

--- a/solution.py
+++ b/solution.py
@@ -17,7 +17,7 @@
 LAG = 2
 GROUP = 2
 LATER = 0
-BATCH = 4
+BEHIND = 0
 FORCE_SCALE = 4.0 * MSG_SCALE
 LOG2E = 1.4426950408889634
 NT = (((1,), (1,)), ((), ()))
@@ -326,7 +326,7 @@
 def far_kernel(
     z, region, table, readout_ref, onehot_near, anchors_near, sums_near, kept_near,
     other, part, mine, adj_own, act_own, onehot_far, kept_own,
-    anchors_far, kept_far, stage, adj_table, mixed, back,
+    anchors_far, kept_far, stage, adj_table, back,
 ):
     by = z.block[1]
     bf = jnp.bfloat16
@@ -343,7 +343,7 @@
         z, stage, [(region, ax + 1, y) for ax in range(z.nax) for y in (1, z.ny - HALO)], anchors_far
     )
 
-    def message_at(ax, carry):
+    def message_at(ax):
         totals = {ay: sums_near[ax * by + ay - 1] for ay in range(z.nay) if z.inner(ay)}
 
         def weigh_some(ay, some):
@@ -361,30 +361,26 @@
             totals[ay] = totals[ay] + term if ay in totals else term
 
         staggered([(ay, some) for ay in range(z.nay) for some in grouped(z.split_offsets(ay)[1])], weigh_some, gather_some, LAG)
-        for ay in range(z.nay):
-            for k in range(rad):
-                part_sum = totals[ay][k * slots:(k + 1) * slots].astype(bf)
-                mixed[ax * z.nay + ay, :, k * spec:(k + 1) * spec] = part_sum
-        return carry
-
-    lax.fori_loop(0, z.nax, message_at, 0)
+        return [
+            jnp.concatenate(
+                [totals[ay][k * slots:(k + 1) * slots].astype(bf) for k in range(rad)], axis=1
+            ) for ay in range(z.nay)
+        ]
 
     def adj_at(ax, ay):
         if 0 < ax < z.nax - 1 and z.inner(ay):
             return adj_own.at[(ax - 1) * by + ay - 1]
         return adj_table.at[ax * z.nay + ay]
 
-    def adjoint_of(group):
-        cells = [ax * z.nay + ay for ax, ay in group]
-        messages = dot(jnp.concatenate([mixed[a] for a in cells], axis=0), table[...], NN)
+    def adjoint_of(mixed, ax):
+        group = [(ax, ay) for ay in range(z.nay)]
+        messages = dot(jnp.concatenate(mixed, axis=0), table[...], NN)
         adjoints = []
-        for i, (a, spot) in enumerate(zip(cells, group)):
+        for i, spot in enumerate(group):
             message = MSG_SCALE * messages[i * slots:(i + 1) * slots]
             sigmoid = 1.0 / (1.0 + jnp.exp(-message))
-            ax, ay = spot
-            inside = 0 < ax < z.nax - 1 and z.inner(ay)
-            if inside:
-                act_own[(ax - 1) * by + ay - 1] = (message * sigmoid).astype(bf)
+            if z.cell(*spot) is not None:
+                act_own[z.cell(*spot)] = (message * sigmoid).astype(bf)
             slope = sigmoid * (1.0 + message * (1.0 - sigmoid)) * readout[0:1]
             adjoints.append(jnp.where(store.anchor(*spot)[3] >= 0.0, slope, 0.0).astype(bf))
         turned = dot(jnp.concatenate(adjoints, axis=0), table[...], NT)
@@ -397,8 +393,7 @@
                     out[at, 0:spec] = high[:, k * spec:(k + 1) * spec]
                     out[at, spec:] = low[:, k * spec:(k + 1) * spec]
 
-    for first in range(0, z.nax, BATCH):
-        adjoint_of([(ax, ay) for ax in range(first, min(first + BATCH, z.nax)) for ay in range(z.nay)])
+    staggered([(ax,) for ax in range(z.nax)], message_at, adjoint_of, BEHIND)
 
     back[...] = jnp.zeros_like(back)
 
@@ -552,7 +547,6 @@
         ((z.nax * 2, offsets) + pair, jnp.float32),
         ((4, LANES, LANES), jnp.float32),
         ((ring, z.rad * z.slots, 2 * z.spec), jnp.bfloat16),
-        ((ring, z.slots, z.rad * z.spec), jnp.bfloat16),
         ((cells * z.groups, 3, 8, LANES), jnp.float32),
     ]
     operands = (region, table, readout, onehot, anchors, sums, kept)

time: 27.8 us -> 26.6 us (0.957)
  Pallas kernels: 12.9 us -> 11.7 us
    pallas_call x2, Pallas kernels: 9.02 us -> 7.9 us  [call(): pl.pallas_call(functools.partial(kernel, z), out_shape=[jax.ShapeDtypeStr...]
  transfers between devices with their start and end apart: 6 -> 6, of which waited for: 4 -> 4; matrix products, arithmetic and copies ran while one was open for 0% -> 0% of each run, Pallas kernels for 18% -> 19%
where the time goes in v7:
time: 26.6 us; the launch traced here: 26.4 us
  Pallas kernels  11.7 us (44%)
  starting transfers between devices  8.46 us (32%)
  waiting for transfers between devices  4.72 us (18%)
  other arithmetic  0.84 us (3%)
  between operations  0.67 us (3%)
    pallas_call x2, Pallas kernels, call(): pl.pallas_call(functools.partial(kernel, z), out_shape=[jax.ShapeDtypeStr...  7.9 us
    ppermute x2, starting transfers between devices, exchange(): from_far = lax.ppermute(up, axis, far)  7.39 us
    pallas_call x1, Pallas kernels, near_layer(): pl.pallas_call(functools.partial(near_kernel, z), out_shape=[jax.ShapeDty...  3.03 us
    ppermute x2, waiting for transfers between devices, exchange(): from_near = lax.ppermute(down, axis, near)  2.79 us
    ppermute x2, waiting for transfers between devices, exchange(): from_far = lax.ppermute(up, axis, far)  1.1 us
    ppermute x1, waiting for transfers between devices, on_device(): low = lax.ppermute(block, 'gz', upward)  0.83 us
    pallas_call x1, Pallas kernels, pack(): pl.pallas_call(pack_kernel, out_shape=jax.ShapeDtypeStruct((bx, by, 4, sl...  0.8 us
    add x1, other arithmetic, on_device(): forces = own + lax.ppermute(other[0], 'gz', downward)  0.6 us
  transfers between devices with their start and end apart: 6, of which 4 were waited for; matrix products, arithmetic and copies ran while one was open for 0% of the time, Pallas kernels for 19%

profile of v7, /device:TPU:0, one launch (start us, length us, event | category | flops | bytes accessed | tf_op | source)
XLA Modules:
  0.0 26.4 jit_solution(2541873627566163603)
XLA Ops:
  0.6 0.8 %shard_map.86 = f32[2,2,4,64]{3,2,1,0:T(4,128)S(1)} custom-call(s32[2,2]{1,0:T(2,128)} %bitcast.22, f32[2,2,1,192]{3,2,1,0:T(1,128)} %positions_hbm.1, s32[2,2,1,64]{3,2,1,0:T(1,128)} %species_hbm.1), custom_call_target="tpu_custom_call" | custom-call | tf_op jit(solution)/shard_map/pallas_call | solution.py:471
  1.4 0.5 %collective-permute-start = (f32[2,2,4,64]{3,2,1,0:T(4,128)S(1)}, f32[2,2,4,64]{3,2,1,0:T(4,128)S(1)}, u32[]{:S(2)}, u32[]{:S(2)}) collective-permute-start(f32[2,2,4,64]{3,2,1,0:T(4,128)S(1)} %shard_map.86), channel_id=1, source_target_pairs={{0,1},{1,0},{2,3},{3,2},{4,5},{5,4},{6,7},{7,6},{8,9},{9,8},{10,11... | collective-permute-start | bytes 12296 | tf_op jit(solution)/shard_map/ppermute | solution.py:578
  2.0 0.8 %collective-permute-done = f32[2,2,4,64]{3,2,1,0:T(4,128)S(1)} collective-permute-done((f32[2,2,4,64]{3,2,1,0:T(4,128)S(1)}, f32[2,2,4,64]{3,2,1,0:T(4,128)S(1)}, u32[]{:S(2)}, u32[]{:S(2)}) %collective-permute-start) | collective-permute-done | bytes 4128 | tf_op jit(solution)/shard_map/ppermute | solution.py:578
  2.8 0.1 pad_maximum_fusion.2
  2.9 3.8 %collective-permute-start.2 = (f32[2,2,4,128]{3,2,1,0:T(4,128)S(1)}, f32[2,2,4,128]{3,2,1,0:T(4,128)S(1)}, u32[]{:S(2)}, u32[]{:S(2)}) collective-permute-start(f32[2,2,4,128]{3,2,1,0:T(4,128)S(1)} %pad_maximum_fusion.2), channel_id=1, source_target_pairs={{0,24},{8,16},{16,8},{24,0},{1,25},{9,17},{17,9},{25,1},{2,26},{10... | collective-permute-start | bytes 24584 | tf_op jit(solution)/shard_map/ppermute | solution.py:38
  6.6 0.5 %collective-permute-start.1 = (f32[2,2,4,128]{3,2,1,0:T(4,128)S(1)}, f32[2,2,4,128]{3,2,1,0:T(4,128)S(1)}, u32[]{:S(2)}, u32[]{:S(2)}) collective-permute-start(f32[2,2,4,128]{3,2,1,0:T(4,128)S(1)} %pad_maximum_fusion.2), channel_id=1, source_target_pairs={{0,8},{8,0},{16,24},{24,16},{1,9},{9,1},{17,25},{25,17},{2,10},{10... | collective-permute-start | bytes 24584 | tf_op jit(solution)/shard_map/ppermute | solution.py:39
  7.2 1.1 %collective-permute-done.2 = f32[2,2,4,128]{3,2,1,0:T(4,128)S(1)} collective-permute-done((f32[2,2,4,128]{3,2,1,0:T(4,128)S(1)}, f32[2,2,4,128]{3,2,1,0:T(4,128)S(1)}, u32[]{:S(2)}, u32[]{:S(2)}) %collective-permute-start.2) | collective-permute-done | bytes 8224 | tf_op jit(solution)/shard_map/ppermute | solution.py:38
  8.3 2.0 %collective-permute-done.1 = f32[2,2,4,128]{3,2,1,0:T(4,128)S(1)} collective-permute-done((f32[2,2,4,128]{3,2,1,0:T(4,128)S(1)}, f32[2,2,4,128]{3,2,1,0:T(4,128)S(1)}, u32[]{:S(2)}, u32[]{:S(2)}) %collective-permute-start.1) | collective-permute-done | bytes 8224 | tf_op jit(solution)/shard_map/ppermute | solution.py:39
  10.3 0.1 pad_maximum_fusion.1.near
  10.4 3.6 %collective-permute-start.4 = (f32[6,2,4,128]{3,2,1,0:T(4,128)S(1)}, f32[6,2,4,128]{3,2,1,0:T(4,128)S(1)}, u32[]{:S(2)}, u32[]{:S(2)}) collective-permute-start(f32[6,2,4,128]{3,2,1,0:T(4,128)S(1)} %pad_maximum_fusion.1.near), channel_id=1, source_target_pairs={{0,6},{2,4},{4,2},{6,0},{1,7},{3,5},{5,3},{7,1},{8,14},{10,12},{12... | collective-permute-start | bytes 73736 | tf_op jit(solution)/shard_map/ppermute | solution.py:38
  14.0 0.0 collective-permute-start.3
  14.0 3.0 %shard_map.87 = (bf16[512,128]{1,0:T(8,128)(2,1)S(1)}, f32[8,128]{1,0:T(8,128)S(1)}, f32[8,128]{1,0:T(8,128)S(1)}, bf16[12,128,128]{2,1,0:T(8,128)(2,1)S(1)}, f3...) custom-call(f32[6,2,4,128]{3,2,1,0:T(4,128)S(1)} %pad_maximum_fusion.1.near, ...), custom_call_target="tpu_custom_call" | custom-call | flops 402653184 | bytes 1048576 | tf_op jit(solution)/shard_map/pallas_call | solution.py:500
  17.0 0.0 collective-permute-done.4
  17.0 0.8 %collective-permute-done.3 = f32[6,2,4,128]{3,2,1,0:T(4,128)S(1)} collective-permute-done((f32[6,2,4,128]{3,2,1,0:T(4,128)S(1)}, f32[6,2,4,128]{3,2,1,0:T(4,128)S(1)}, u32[]{:S(2)}, u32[]{:S(2)}) %collective-permute-start.3) | collective-permute-done | bytes 24608 | tf_op jit(solution)/shard_map/ppermute | solution.py:39
  17.8 0.1 pad_maximum_fusion.region
  17.9 6.0 %shard_map.88 = (f32[1,2,2,1,192]{4,3,2,1,0:T(1,128)S(1)}, f32[2,2,1,192]{3,2,1,0:T(1,128)S(1)}, f32[4,3,64,128]{3,2,1,0:T(8,128)S(1)}, bf16[4,256,256]{2,1,0:T(...) custom-call(f32[6,6,4,128]{3,2,1,0:T(4,128)S(1)} %pad_maximum_fusion, ...), custom_call_target="tpu_custom_call" | custom-call | tf_op jit(solution)/shard_map/pallas_call | solution.py:520
  23.9 0.0 collective-permute-start.5
  23.9 1.9 %shard_map.89 = (f32[2,2,1,64]{3,2,1,0:T(1,128)}, f32[2,2,1,192]{3,2,1,0:T(1,128)S(1)}) custom-call(f32[6,6,4,128]{3,2,1,0:T(4,128)S(1)} %pad_maximum_fusion.region, f32[8,128]{1,0:T(8,128)S(1)} %get-tuple-element.18.readout_ref.readout, f32[8,128]{1,0:T(8,128)S(1)} %get-tuple-element.19.emb_energy, bf16[12,128,128]{2,1,0:T(8,128)(2,1)S(1)} %get-tuple-element.20.onehot_near, ...), custom_call_target="tpu_custom_call" | custom-call | tf_op jit(solution)/shard_map/pallas_call | solution.py:520
  25.8 0.0 collective-permute-done.5
  25.8 0.6 %add.12 = f32[2,2,1,192]{3,2,1,0:T(1,128)} add(f32[2,2,1,192]{3,2,1,0:T(1,128)S(1)} %get-tuple-element.32, f32[2,2,1,192]{3,2,1,0:T(1,128)S(1)} %collective-permute-done.5) | non-fusion elementwise | flops 768 | bytes 9216 | tf_op jit(solution)/shard_map/add | solution.py:593
  (2 shorter events, 0.0 us)
Async XLA Ops:
  1.4 1.3 %collective-permute-start = (f32[2,2,4,64]{3,2,1,0:T(4,128)S(1)}, f32[2,2,4,64]{3,2,1,0:T(4,128)S(1)}, u32[]{:S(2)}, u32[]{:S(2)}) collective-permute-start(f32[2,2,4,64]{3,2,1,0:T(4,128)S(1)} %shard_map.86), channel_id=1, source_target_pairs={{0,1},{1,0},{2,3},{3,2},{4,5},{5,4},{6,7},{7,6},{8,9},{9,8},{10,11... | collective-permute-start | bytes 12296 | tf_op jit(solution)/shard_map/ppermute | solution.py:578
  2.9 5.4 %collective-permute-start.2 = (f32[2,2,4,128]{3,2,1,0:T(4,128)S(1)}, f32[2,2,4,128]{3,2,1,0:T(4,128)S(1)}, u32[]{:S(2)}, u32[]{:S(2)}) collective-permute-start(f32[2,2,4,128]{3,2,1,0:T(4,128)S(1)} %pad_maximum_fusion.2), channel_id=1, source_target_pairs={{0,24},{8,16},{16,8},{24,0},{1,25},{9,17},{17,9},{25,1},{2,26},{10... | collective-permute-start | bytes 24584 | tf_op jit(solution)/shard_map/ppermute | solution.py:38
  6.6 3.7 %collective-permute-start.1 = (f32[2,2,4,128]{3,2,1,0:T(4,128)S(1)}, f32[2,2,4,128]{3,2,1,0:T(4,128)S(1)}, u32[]{:S(2)}, u32[]{:S(2)}) collective-permute-start(f32[2,2,4,128]{3,2,1,0:T(4,128)S(1)} %pad_maximum_fusion.2), channel_id=1, source_target_pairs={{0,8},{8,0},{16,24},{24,16},{1,9},{9,1},{17,25},{25,17},{2,10},{10... | collective-permute-start | bytes 24584 | tf_op jit(solution)/shard_map/ppermute | solution.py:39
  10.4 6.7 %collective-permute-start.4 = (f32[6,2,4,128]{3,2,1,0:T(4,128)S(1)}, f32[6,2,4,128]{3,2,1,0:T(4,128)S(1)}, u32[]{:S(2)}, u32[]{:S(2)}) collective-permute-start(f32[6,2,4,128]{3,2,1,0:T(4,128)S(1)} %pad_maximum_fusion.1.near), channel_id=1, source_target_pairs={{0,6},{2,4},{4,2},{6,0},{1,7},{3,5},{5,3},{7,1},{8,14},{10,12},{12... | collective-permute-start | bytes 73736 | tf_op jit(solution)/shard_map/ppermute | solution.py:38
  14.0 3.8 %collective-permute-start.3 = (f32[6,2,4,128]{3,2,1,0:T(4,128)S(1)}, f32[6,2,4,128]{3,2,1,0:T(4,128)S(1)}, u32[]{:S(2)}, u32[]{:S(2)}) collective-permute-start(f32[6,2,4,128]{3,2,1,0:T(4,128)S(1)} %pad_maximum_fusion.1.near), channel_id=1, source_target_pairs={{0,2},{2,0},{4,6},{6,4},{1,3},{3,1},{5,7},{7,5},{8,10},{10,8},{12,... | collective-permute-start | bytes 73736 | tf_op jit(solution)/shard_map/ppermute | solution.py:39
  23.9 1.9 %collective-permute-start.5 = (f32[2,2,1,192]{3,2,1,0:T(1,128)S(1)}, f32[2,2,1,192]{3,2,1,0:T(1,128)S(1)}, u32[]{:S(2)}, u32[]{:S(2)}) collective-permute-start(f32[2,2,1,192]{3,2,1,0:T(1,128)S(1)} %bitcast.11), channel_id=1, source_target_pairs={{1,0},{0,1},{3,2},{2,3},{5,4},{4,5},{7,6},{6,7},{9,8},{8,9},{11,10... | collective-permute-start | bytes 9224 | tf_op jit(solution)/shard_map/ppermute | solution.py:593

commit v8 on v7

--- a/solution.py
+++ b/solution.py
@@ -14,7 +14,7 @@
 LANES = 128
 STEP = 16
 WIDE = 4
-LAG = 2
+LAG = 0
 GROUP = 2
 LATER = 0
 BEHIND = 0
@@ -429,6 +429,14 @@
     slots = z.slots
     store = Store(z, onehot_near, onehot_far, anchors_near, None, kept_near, kept_own, None)
     cells = [(ox, oy) for ox in range(z.block[0]) for oy in range(z.block[1])]
+    hots = jnp.concatenate([store.onehot(ox + HALO, oy + HALO, 0)[:, 0:slots] for ox, oy in cells], axis=1)
+    acts = jnp.concatenate([act_own[o] for o in range(len(cells))], axis=0)
+    energy = dot(thirds(emb_energy[...]), hots, NN) + dot(thirds(readout[...]), acts, NT)
+    energy = jnp.sum(energy, axis=0, keepdims=True)
+    for o, (ox, oy) in enumerate(cells):
+        marked = region[ox + HALO, oy + HALO, 3:4, 0:slots]
+        energies[ox, oy, :, :] = jnp.where(marked >= 0.0, energy[:, o * slots:(o + 1) * slots], 0.0)
+
     work = []
     for o, (ox, oy) in enumerate(cells):
         some = [n for n, (dx, dy, _) in enumerate(z.offsets) if z.cell(ox + 1 + dx, oy + 1 + dy) is None]
@@ -448,14 +456,6 @@
             at = (o * 3 + q) * slots
             lanes = slice(q * slots, (q + 1) * slots)
             own[ox, oy, :, lanes] = part[ox, oy, :, lanes] - FORCE_SCALE * rows[:, at:at + slots]
-
-    hots = jnp.concatenate([store.onehot(ox + HALO, oy + HALO, 0)[:, 0:slots] for ox, oy in cells], axis=1)
-    acts = jnp.concatenate([act_own[o] for o in range(len(cells))], axis=0)
-    energy = dot(thirds(emb_energy[...]), hots, NN) + dot(thirds(readout[...]), acts, NT)
-    energy = jnp.sum(energy, axis=0, keepdims=True)
-    for o, (ox, oy) in enumerate(cells):
-        marked = region[ox + HALO, oy + HALO, 3:4, 0:slots]
-        energies[ox, oy, :, :] = jnp.where(marked >= 0.0, energy[:, o * slots:(o + 1) * slots], 0.0)
 
 
 VMEM = pl.BlockSpec(memory_space=pltpu.VMEM)

time: 26.6 us -> 26.1 us (0.981)
  Pallas kernels: 11.7 us -> 11.2 us
    pallas_call x2, Pallas kernels: 7.9 us -> 7.35 us  [call(): pl.pallas_call(functools.partial(kernel, z), out_shape=[jax.ShapeDtypeStr...]
  transfers between devices with their start and end apart: 6 -> 6, of which waited for: 4 -> 4; matrix products, arithmetic and copies ran while one was open for 0% -> 0% of each run, Pallas kernels for 19% -> 17%
where the time goes in v8:
time: 26.1 us; the launch traced here: 25.9 us
  Pallas kernels  11.2 us (43%)
  starting transfers between devices  8.46 us (32%)
  waiting for transfers between devices  4.72 us (18%)
  other arithmetic  0.86 us (3%)
  between operations  0.67 us (3%)
    ppermute x2, starting transfers between devices, exchange(): from_far = lax.ppermute(up, axis, far)  7.39 us
    pallas_call x2, Pallas kernels, call(): pl.pallas_call(functools.partial(kernel, z), out_shape=[jax.ShapeDtypeStr...  7.35 us
    pallas_call x1, Pallas kernels, near_layer(): pl.pallas_call(functools.partial(near_kernel, z), out_shape=[jax.ShapeDty...  3.03 us
    ppermute x2, waiting for transfers between devices, exchange(): from_near = lax.ppermute(down, axis, near)  2.79 us
    ppermute x2, waiting for transfers between devices, exchange(): from_far = lax.ppermute(up, axis, far)  1.1 us
    ppermute x1, waiting for transfers between devices, on_device(): low = lax.ppermute(block, 'gz', upward)  0.83 us
    pallas_call x1, Pallas kernels, pack(): pl.pallas_call(pack_kernel, out_shape=jax.ShapeDtypeStruct((bx, by, 4, sl...  0.8 us
    add x1, other arithmetic, on_device(): forces = own + lax.ppermute(other[0], 'gz', downward)  0.62 us
  transfers between devices with their start and end apart: 6, of which 4 were waited for; matrix products, arithmetic and copies ran while one was open for 0% of the time, Pallas kernels for 17%

profile of v8, /device:TPU:0, one launch (start us, length us, event | category | flops | bytes accessed | tf_op | source)
XLA Modules:
  0.0 25.9 jit_solution(16495134090458486698)
XLA Ops:
  0.6 0.8 %shard_map.86 = f32[2,2,4,64]{3,2,1,0:T(4,128)S(1)} custom-call(s32[2,2]{1,0:T(2,128)} %bitcast.22, f32[2,2,1,192]{3,2,1,0:T(1,128)} %positions_hbm.1, s32[2,2,1,64]{3,2,1,0:T(1,128)} %species_hbm.1), custom_call_target="tpu_custom_call" | custom-call | tf_op jit(solution)/shard_map/pallas_call | solution.py:471
  1.4 0.5 %collective-permute-start = (f32[2,2,4,64]{3,2,1,0:T(4,128)S(1)}, f32[2,2,4,64]{3,2,1,0:T(4,128)S(1)}, u32[]{:S(2)}, u32[]{:S(2)}) collective-permute-start(f32[2,2,4,64]{3,2,1,0:T(4,128)S(1)} %shard_map.86), channel_id=1, source_target_pairs={{0,1},{1,0},{2,3},{3,2},{4,5},{5,4},{6,7},{7,6},{8,9},{9,8},{10,11... | collective-permute-start | bytes 12296 | tf_op jit(solution)/shard_map/ppermute | solution.py:578
  2.0 0.8 %collective-permute-done = f32[2,2,4,64]{3,2,1,0:T(4,128)S(1)} collective-permute-done((f32[2,2,4,64]{3,2,1,0:T(4,128)S(1)}, f32[2,2,4,64]{3,2,1,0:T(4,128)S(1)}, u32[]{:S(2)}, u32[]{:S(2)}) %collective-permute-start) | collective-permute-done | bytes 4128 | tf_op jit(solution)/shard_map/ppermute | solution.py:578
  2.8 0.1 pad_maximum_fusion.2
  2.9 3.8 %collective-permute-start.2 = (f32[2,2,4,128]{3,2,1,0:T(4,128)S(1)}, f32[2,2,4,128]{3,2,1,0:T(4,128)S(1)}, u32[]{:S(2)}, u32[]{:S(2)}) collective-permute-start(f32[2,2,4,128]{3,2,1,0:T(4,128)S(1)} %pad_maximum_fusion.2), channel_id=1, source_target_pairs={{0,24},{8,16},{16,8},{24,0},{1,25},{9,17},{17,9},{25,1},{2,26},{10... | collective-permute-start | bytes 24584 | tf_op jit(solution)/shard_map/ppermute | solution.py:38
  6.6 0.5 %collective-permute-start.1 = (f32[2,2,4,128]{3,2,1,0:T(4,128)S(1)}, f32[2,2,4,128]{3,2,1,0:T(4,128)S(1)}, u32[]{:S(2)}, u32[]{:S(2)}) collective-permute-start(f32[2,2,4,128]{3,2,1,0:T(4,128)S(1)} %pad_maximum_fusion.2), channel_id=1, source_target_pairs={{0,8},{8,0},{16,24},{24,16},{1,9},{9,1},{17,25},{25,17},{2,10},{10... | collective-permute-start | bytes 24584 | tf_op jit(solution)/shard_map/ppermute | solution.py:39
  7.2 1.1 %collective-permute-done.2 = f32[2,2,4,128]{3,2,1,0:T(4,128)S(1)} collective-permute-done((f32[2,2,4,128]{3,2,1,0:T(4,128)S(1)}, f32[2,2,4,128]{3,2,1,0:T(4,128)S(1)}, u32[]{:S(2)}, u32[]{:S(2)}) %collective-permute-start.2) | collective-permute-done | bytes 8224 | tf_op jit(solution)/shard_map/ppermute | solution.py:38
  8.3 2.0 %collective-permute-done.1 = f32[2,2,4,128]{3,2,1,0:T(4,128)S(1)} collective-permute-done((f32[2,2,4,128]{3,2,1,0:T(4,128)S(1)}, f32[2,2,4,128]{3,2,1,0:T(4,128)S(1)}, u32[]{:S(2)}, u32[]{:S(2)}) %collective-permute-start.1) | collective-permute-done | bytes 8224 | tf_op jit(solution)/shard_map/ppermute | solution.py:39
  10.3 0.1 pad_maximum_fusion.1.near
  10.4 3.6 %collective-permute-start.4 = (f32[6,2,4,128]{3,2,1,0:T(4,128)S(1)}, f32[6,2,4,128]{3,2,1,0:T(4,128)S(1)}, u32[]{:S(2)}, u32[]{:S(2)}) collective-permute-start(f32[6,2,4,128]{3,2,1,0:T(4,128)S(1)} %pad_maximum_fusion.1.near), channel_id=1, source_target_pairs={{0,6},{2,4},{4,2},{6,0},{1,7},{3,5},{5,3},{7,1},{8,14},{10,12},{12... | collective-permute-start | bytes 73736 | tf_op jit(solution)/shard_map/ppermute | solution.py:38
  14.0 0.0 collective-permute-start.3
  14.0 3.0 %shard_map.87 = (bf16[512,128]{1,0:T(8,128)(2,1)S(1)}, f32[8,128]{1,0:T(8,128)S(1)}, f32[8,128]{1,0:T(8,128)S(1)}, bf16[12,128,128]{2,1,0:T(8,128)(2,1)S(1)}, f3...) custom-call(f32[6,2,4,128]{3,2,1,0:T(4,128)S(1)} %pad_maximum_fusion.1.near, ...), custom_call_target="tpu_custom_call" | custom-call | flops 402653184 | bytes 1048576 | tf_op jit(solution)/shard_map/pallas_call | solution.py:500
  17.0 0.0 collective-permute-done.4
  17.0 0.8 %collective-permute-done.3 = f32[6,2,4,128]{3,2,1,0:T(4,128)S(1)} collective-permute-done((f32[6,2,4,128]{3,2,1,0:T(4,128)S(1)}, f32[6,2,4,128]{3,2,1,0:T(4,128)S(1)}, u32[]{:S(2)}, u32[]{:S(2)}) %collective-permute-start.3) | collective-permute-done | bytes 24608 | tf_op jit(solution)/shard_map/ppermute | solution.py:39
  17.8 0.1 pad_maximum_fusion.region
  17.9 6.0 %shard_map.88 = (f32[1,2,2,1,192]{4,3,2,1,0:T(1,128)S(1)}, f32[2,2,1,192]{3,2,1,0:T(1,128)S(1)}, f32[4,3,64,128]{3,2,1,0:T(8,128)S(1)}, bf16[4,256,256]{2,1,0:T(...) custom-call(f32[6,6,4,128]{3,2,1,0:T(4,128)S(1)} %pad_maximum_fusion, ...), custom_call_target="tpu_custom_call" | custom-call | tf_op jit(solution)/shard_map/pallas_call | solution.py:520
  23.9 0.0 collective-permute-start.5
  23.9 1.4 %shard_map.89 = (f32[2,2,1,64]{3,2,1,0:T(1,128)}, f32[2,2,1,192]{3,2,1,0:T(1,128)S(1)}) custom-call(f32[6,6,4,128]{3,2,1,0:T(4,128)S(1)} %pad_maximum_fusion.region, f32[8,128]{1,0:T(8,128)S(1)} %get-tuple-element.18.readout_ref.readout, f32[8,128]{1,0:T(8,128)S(1)} %get-tuple-element.19.emb_energy, bf16[12,128,128]{2,1,0:T(8,128)(2,1)S(1)} %get-tuple-element.20.onehot_near, ...), custom_call_target="tpu_custom_call" | custom-call | tf_op jit(solution)/shard_map/pallas_call | solution.py:520
  25.3 0.0 collective-permute-done.5
  25.3 0.6 %add.12 = f32[2,2,1,192]{3,2,1,0:T(1,128)} add(f32[2,2,1,192]{3,2,1,0:T(1,128)S(1)} %get-tuple-element.32, f32[2,2,1,192]{3,2,1,0:T(1,128)S(1)} %collective-permute-done.5) | non-fusion elementwise | flops 768 | bytes 9216 | tf_op jit(solution)/shard_map/add | solution.py:593
  (2 shorter events, 0.0 us)
Async XLA Ops:
  1.4 1.3 %collective-permute-start = (f32[2,2,4,64]{3,2,1,0:T(4,128)S(1)}, f32[2,2,4,64]{3,2,1,0:T(4,128)S(1)}, u32[]{:S(2)}, u32[]{:S(2)}) collective-permute-start(f32[2,2,4,64]{3,2,1,0:T(4,128)S(1)} %shard_map.86), channel_id=1, source_target_pairs={{0,1},{1,0},{2,3},{3,2},{4,5},{5,4},{6,7},{7,6},{8,9},{9,8},{10,11... | collective-permute-start | bytes 12296 | tf_op jit(solution)/shard_map/ppermute | solution.py:578
  2.9 5.4 %collective-permute-start.2 = (f32[2,2,4,128]{3,2,1,0:T(4,128)S(1)}, f32[2,2,4,128]{3,2,1,0:T(4,128)S(1)}, u32[]{:S(2)}, u32[]{:S(2)}) collective-permute-start(f32[2,2,4,128]{3,2,1,0:T(4,128)S(1)} %pad_maximum_fusion.2), channel_id=1, source_target_pairs={{0,24},{8,16},{16,8},{24,0},{1,25},{9,17},{17,9},{25,1},{2,26},{10... | collective-permute-start | bytes 24584 | tf_op jit(solution)/shard_map/ppermute | solution.py:38
  6.6 3.7 %collective-permute-start.1 = (f32[2,2,4,128]{3,2,1,0:T(4,128)S(1)}, f32[2,2,4,128]{3,2,1,0:T(4,128)S(1)}, u32[]{:S(2)}, u32[]{:S(2)}) collective-permute-start(f32[2,2,4,128]{3,2,1,0:T(4,128)S(1)} %pad_maximum_fusion.2), channel_id=1, source_target_pairs={{0,8},{8,0},{16,24},{24,16},{1,9},{9,1},{17,25},{25,17},{2,10},{10... | collective-permute-start | bytes 24584 | tf_op jit(solution)/shard_map/ppermute | solution.py:39
  10.4 6.7 %collective-permute-start.4 = (f32[6,2,4,128]{3,2,1,0:T(4,128)S(1)}, f32[6,2,4,128]{3,2,1,0:T(4,128)S(1)}, u32[]{:S(2)}, u32[]{:S(2)}) collective-permute-start(f32[6,2,4,128]{3,2,1,0:T(4,128)S(1)} %pad_maximum_fusion.1.near), channel_id=1, source_target_pairs={{0,6},{2,4},{4,2},{6,0},{1,7},{3,5},{5,3},{7,1},{8,14},{10,12},{12... | collective-permute-start | bytes 73736 | tf_op jit(solution)/shard_map/ppermute | solution.py:38
  14.0 3.8 %collective-permute-start.3 = (f32[6,2,4,128]{3,2,1,0:T(4,128)S(1)}, f32[6,2,4,128]{3,2,1,0:T(4,128)S(1)}, u32[]{:S(2)}, u32[]{:S(2)}) collective-permute-start(f32[6,2,4,128]{3,2,1,0:T(4,128)S(1)} %pad_maximum_fusion.1.near), channel_id=1, source_target_pairs={{0,2},{2,0},{4,6},{6,4},{1,3},{3,1},{5,7},{7,5},{8,10},{10,8},{12,... | collective-permute-start | bytes 73736 | tf_op jit(solution)/shard_map/ppermute | solution.py:39
  23.9 1.4 %collective-permute-start.5 = (f32[2,2,1,192]{3,2,1,0:T(1,128)S(1)}, f32[2,2,1,192]{3,2,1,0:T(1,128)S(1)}, u32[]{:S(2)}, u32[]{:S(2)}) collective-permute-start(f32[2,2,1,192]{3,2,1,0:T(1,128)S(1)} %bitcast.11), channel_id=1, source_target_pairs={{1,0},{0,1},{3,2},{2,3},{5,4},{4,5},{7,6},{6,7},{9,8},{8,9},{11,10... | collective-permute-start | bytes 9224 | tf_op jit(solution)/shard_map/ppermute | solution.py:593

commit v9 on v8

--- a/solution.py
+++ b/solution.py
@@ -335,13 +335,13 @@
     store = Store(z, onehot_near, onehot_far, anchors_near, anchors_far, kept_near, kept_own, kept_far)
     outer = store.outer
 
+    place_anchors(
+        z, stage, [(region, ax + 1, y) for ax in range(z.nax) for y in (1, z.ny - HALO)], anchors_far
+    )
     for x in range(z.nx):
         for i, y in enumerate(outer):
             for g in range(z.groups):
                 place_onehot(z, region, x, y, g, onehot_far, (x * len(outer) + i) * z.groups + g)
-    place_anchors(
-        z, stage, [(region, ax + 1, y) for ax in range(z.nax) for y in (1, z.ny - HALO)], anchors_far
-    )
 
     def message_at(ax):
         totals = {ay: sums_near[ax * by + ay - 1] for ay in range(z.nay) if z.inner(ay)}

time: 26.1 us -> 26.1 us (level)
  no operation moved by 1% of the time
where the time goes in v9:
time: 26.1 us; the launch traced here: 25.9 us
  Pallas kernels  11.2 us (43%)
  starting transfers between devices  8.46 us (32%)
  waiting for transfers between devices  4.72 us (18%)
  other arithmetic  0.86 us (3%)
  between operations  0.67 us (3%)
    ppermute x2, starting transfers between devices, exchange(): from_far = lax.ppermute(up, axis, far)  7.39 us
    pallas_call x2, Pallas kernels, call(): pl.pallas_call(functools.partial(kernel, z), out_shape=[jax.ShapeDtypeStr...  7.36 us
    pallas_call x1, Pallas kernels, near_layer(): pl.pallas_call(functools.partial(near_kernel, z), out_shape=[jax.ShapeDty...  3.03 us
    ppermute x2, waiting for transfers between devices, exchange(): from_near = lax.ppermute(down, axis, near)  2.79 us
    ppermute x2, waiting for transfers between devices, exchange(): from_far = lax.ppermute(up, axis, far)  1.1 us
    ppermute x1, waiting for transfers between devices, on_device(): low = lax.ppermute(block, 'gz', upward)  0.83 us
    pallas_call x1, Pallas kernels, pack(): pl.pallas_call(pack_kernel, out_shape=jax.ShapeDtypeStruct((bx, by, 4, sl...  0.8 us
    add x1, other arithmetic, on_device(): forces = own + lax.ppermute(other[0], 'gz', downward)  0.62 us
  transfers between devices with their start and end apart: 6, of which 4 were waited for; matrix products, arithmetic and copies ran while one was open for 0% of the time, Pallas kernels for 17%

profile of v9, /device:TPU:0, one launch (start us, length us, event | category | flops | bytes accessed | tf_op | source)
XLA Modules:
  0.0 25.9 jit_solution(13679893034950617622)
XLA Ops:
  0.6 0.8 %shard_map.86 = f32[2,2,4,64]{3,2,1,0:T(4,128)S(1)} custom-call(s32[2,2]{1,0:T(2,128)} %bitcast.22, f32[2,2,1,192]{3,2,1,0:T(1,128)} %positions_hbm.1, s32[2,2,1,64]{3,2,1,0:T(1,128)} %species_hbm.1), custom_call_target="tpu_custom_call" | custom-call | tf_op jit(solution)/shard_map/pallas_call | solution.py:471
  1.4 0.5 %collective-permute-start = (f32[2,2,4,64]{3,2,1,0:T(4,128)S(1)}, f32[2,2,4,64]{3,2,1,0:T(4,128)S(1)}, u32[]{:S(2)}, u32[]{:S(2)}) collective-permute-start(f32[2,2,4,64]{3,2,1,0:T(4,128)S(1)} %shard_map.86), channel_id=1, source_target_pairs={{0,1},{1,0},{2,3},{3,2},{4,5},{5,4},{6,7},{7,6},{8,9},{9,8},{10,11... | collective-permute-start | bytes 12296 | tf_op jit(solution)/shard_map/ppermute | solution.py:578
  2.0 0.8 %collective-permute-done = f32[2,2,4,64]{3,2,1,0:T(4,128)S(1)} collective-permute-done((f32[2,2,4,64]{3,2,1,0:T(4,128)S(1)}, f32[2,2,4,64]{3,2,1,0:T(4,128)S(1)}, u32[]{:S(2)}, u32[]{:S(2)}) %collective-permute-start) | collective-permute-done | bytes 4128 | tf_op jit(solution)/shard_map/ppermute | solution.py:578
  2.8 0.1 pad_maximum_fusion.2
  2.9 3.8 %collective-permute-start.2 = (f32[2,2,4,128]{3,2,1,0:T(4,128)S(1)}, f32[2,2,4,128]{3,2,1,0:T(4,128)S(1)}, u32[]{:S(2)}, u32[]{:S(2)}) collective-permute-start(f32[2,2,4,128]{3,2,1,0:T(4,128)S(1)} %pad_maximum_fusion.2), channel_id=1, source_target_pairs={{0,24},{8,16},{16,8},{24,0},{1,25},{9,17},{17,9},{25,1},{2,26},{10... | collective-permute-start | bytes 24584 | tf_op jit(solution)/shard_map/ppermute | solution.py:38
  6.6 0.5 %collective-permute-start.1 = (f32[2,2,4,128]{3,2,1,0:T(4,128)S(1)}, f32[2,2,4,128]{3,2,1,0:T(4,128)S(1)}, u32[]{:S(2)}, u32[]{:S(2)}) collective-permute-start(f32[2,2,4,128]{3,2,1,0:T(4,128)S(1)} %pad_maximum_fusion.2), channel_id=1, source_target_pairs={{0,8},{8,0},{16,24},{24,16},{1,9},{9,1},{17,25},{25,17},{2,10},{10... | collective-permute-start | bytes 24584 | tf_op jit(solution)/shard_map/ppermute | solution.py:39
  7.2 1.1 %collective-permute-done.2 = f32[2,2,4,128]{3,2,1,0:T(4,128)S(1)} collective-permute-done((f32[2,2,4,128]{3,2,1,0:T(4,128)S(1)}, f32[2,2,4,128]{3,2,1,0:T(4,128)S(1)}, u32[]{:S(2)}, u32[]{:S(2)}) %collective-permute-start.2) | collective-permute-done | bytes 8224 | tf_op jit(solution)/shard_map/ppermute | solution.py:38
  8.3 2.0 %collective-permute-done.1 = f32[2,2,4,128]{3,2,1,0:T(4,128)S(1)} collective-permute-done((f32[2,2,4,128]{3,2,1,0:T(4,128)S(1)}, f32[2,2,4,128]{3,2,1,0:T(4,128)S(1)}, u32[]{:S(2)}, u32[]{:S(2)}) %collective-permute-start.1) | collective-permute-done | bytes 8224 | tf_op jit(solution)/shard_map/ppermute | solution.py:39
  10.3 0.1 pad_maximum_fusion.1.near
  10.4 3.6 %collective-permute-start.4 = (f32[6,2,4,128]{3,2,1,0:T(4,128)S(1)}, f32[6,2,4,128]{3,2,1,0:T(4,128)S(1)}, u32[]{:S(2)}, u32[]{:S(2)}) collective-permute-start(f32[6,2,4,128]{3,2,1,0:T(4,128)S(1)} %pad_maximum_fusion.1.near), channel_id=1, source_target_pairs={{0,6},{2,4},{4,2},{6,0},{1,7},{3,5},{5,3},{7,1},{8,14},{10,12},{12... | collective-permute-start | bytes 73736 | tf_op jit(solution)/shard_map/ppermute | solution.py:38
  14.0 0.0 collective-permute-start.3
  14.0 3.0 %shard_map.87 = (bf16[512,128]{1,0:T(8,128)(2,1)S(1)}, f32[8,128]{1,0:T(8,128)S(1)}, f32[8,128]{1,0:T(8,128)S(1)}, bf16[12,128,128]{2,1,0:T(8,128)(2,1)S(1)}, f3...) custom-call(f32[6,2,4,128]{3,2,1,0:T(4,128)S(1)} %pad_maximum_fusion.1.near, ...), custom_call_target="tpu_custom_call" | custom-call | flops 402653184 | bytes 1048576 | tf_op jit(solution)/shard_map/pallas_call | solution.py:500
  17.0 0.0 collective-permute-done.4
  17.0 0.8 %collective-permute-done.3 = f32[6,2,4,128]{3,2,1,0:T(4,128)S(1)} collective-permute-done((f32[6,2,4,128]{3,2,1,0:T(4,128)S(1)}, f32[6,2,4,128]{3,2,1,0:T(4,128)S(1)}, u32[]{:S(2)}, u32[]{:S(2)}) %collective-permute-start.3) | collective-permute-done | bytes 24608 | tf_op jit(solution)/shard_map/ppermute | solution.py:39
  17.8 0.1 pad_maximum_fusion.region
  17.9 6.0 %shard_map.88 = (f32[1,2,2,1,192]{4,3,2,1,0:T(1,128)S(1)}, f32[2,2,1,192]{3,2,1,0:T(1,128)S(1)}, f32[4,3,64,128]{3,2,1,0:T(8,128)S(1)}, bf16[4,256,256]{2,1,0:T(...) custom-call(f32[6,6,4,128]{3,2,1,0:T(4,128)S(1)} %pad_maximum_fusion, ...), custom_call_target="tpu_custom_call" | custom-call | tf_op jit(solution)/shard_map/pallas_call | solution.py:520
  23.9 0.0 collective-permute-start.5
  23.9 1.4 %shard_map.89 = (f32[2,2,1,64]{3,2,1,0:T(1,128)}, f32[2,2,1,192]{3,2,1,0:T(1,128)S(1)}) custom-call(f32[6,6,4,128]{3,2,1,0:T(4,128)S(1)} %pad_maximum_fusion.region, f32[8,128]{1,0:T(8,128)S(1)} %get-tuple-element.18.readout_ref.readout, f32[8,128]{1,0:T(8,128)S(1)} %get-tuple-element.19.emb_energy, bf16[12,128,128]{2,1,0:T(8,128)(2,1)S(1)} %get-tuple-element.20.onehot_near, ...), custom_call_target="tpu_custom_call" | custom-call | tf_op jit(solution)/shard_map/pallas_call | solution.py:520
  25.3 0.0 collective-permute-done.5
  25.3 0.6 %add.12 = f32[2,2,1,192]{3,2,1,0:T(1,128)} add(f32[2,2,1,192]{3,2,1,0:T(1,128)S(1)} %get-tuple-element.32, f32[2,2,1,192]{3,2,1,0:T(1,128)S(1)} %collective-permute-done.5) | non-fusion elementwise | flops 768 | bytes 9216 | tf_op jit(solution)/shard_map/add | solution.py:593
  (2 shorter events, 0.0 us)
Async XLA Ops:
  1.4 1.3 %collective-permute-start = (f32[2,2,4,64]{3,2,1,0:T(4,128)S(1)}, f32[2,2,4,64]{3,2,1,0:T(4,128)S(1)}, u32[]{:S(2)}, u32[]{:S(2)}) collective-permute-start(f32[2,2,4,64]{3,2,1,0:T(4,128)S(1)} %shard_map.86), channel_id=1, source_target_pairs={{0,1},{1,0},{2,3},{3,2},{4,5},{5,4},{6,7},{7,6},{8,9},{9,8},{10,11... | collective-permute-start | bytes 12296 | tf_op jit(solution)/shard_map/ppermute | solution.py:578
  2.9 5.4 %collective-permute-start.2 = (f32[2,2,4,128]{3,2,1,0:T(4,128)S(1)}, f32[2,2,4,128]{3,2,1,0:T(4,128)S(1)}, u32[]{:S(2)}, u32[]{:S(2)}) collective-permute-start(f32[2,2,4,128]{3,2,1,0:T(4,128)S(1)} %pad_maximum_fusion.2), channel_id=1, source_target_pairs={{0,24},{8,16},{16,8},{24,0},{1,25},{9,17},{17,9},{25,1},{2,26},{10... | collective-permute-start | bytes 24584 | tf_op jit(solution)/shard_map/ppermute | solution.py:38
  6.6 3.7 %collective-permute-start.1 = (f32[2,2,4,128]{3,2,1,0:T(4,128)S(1)}, f32[2,2,4,128]{3,2,1,0:T(4,128)S(1)}, u32[]{:S(2)}, u32[]{:S(2)}) collective-permute-start(f32[2,2,4,128]{3,2,1,0:T(4,128)S(1)} %pad_maximum_fusion.2), channel_id=1, source_target_pairs={{0,8},{8,0},{16,24},{24,16},{1,9},{9,1},{17,25},{25,17},{2,10},{10... | collective-permute-start | bytes 24584 | tf_op jit(solution)/shard_map/ppermute | solution.py:39
  10.4 6.7 %collective-permute-start.4 = (f32[6,2,4,128]{3,2,1,0:T(4,128)S(1)}, f32[6,2,4,128]{3,2,1,0:T(4,128)S(1)}, u32[]{:S(2)}, u32[]{:S(2)}) collective-permute-start(f32[6,2,4,128]{3,2,1,0:T(4,128)S(1)} %pad_maximum_fusion.1.near), channel_id=1, source_target_pairs={{0,6},{2,4},{4,2},{6,0},{1,7},{3,5},{5,3},{7,1},{8,14},{10,12},{12... | collective-permute-start | bytes 73736 | tf_op jit(solution)/shard_map/ppermute | solution.py:38
  14.0 3.8 %collective-permute-start.3 = (f32[6,2,4,128]{3,2,1,0:T(4,128)S(1)}, f32[6,2,4,128]{3,2,1,0:T(4,128)S(1)}, u32[]{:S(2)}, u32[]{:S(2)}) collective-permute-start(f32[6,2,4,128]{3,2,1,0:T(4,128)S(1)} %pad_maximum_fusion.1.near), channel_id=1, source_target_pairs={{0,2},{2,0},{4,6},{6,4},{1,3},{3,1},{5,7},{7,5},{8,10},{10,8},{12,... | collective-permute-start | bytes 73736 | tf_op jit(solution)/shard_map/ppermute | solution.py:39
  23.9 1.4 %collective-permute-start.5 = (f32[2,2,1,192]{3,2,1,0:T(1,128)S(1)}, f32[2,2,1,192]{3,2,1,0:T(1,128)S(1)}, u32[]{:S(2)}, u32[]{:S(2)}) collective-permute-start(f32[2,2,1,192]{3,2,1,0:T(1,128)S(1)} %bitcast.11), channel_id=1, source_target_pairs={{1,0},{0,1},{3,2},{2,3},{5,4},{4,5},{7,6},{6,7},{9,8},{8,9},{11,10... | collective-permute-start | bytes 9224 | tf_op jit(solution)/shard_map/ppermute | solution.py:593
